TPU v7x, 32 devices: a whole 2x2x4 slice. The times are simulated.
32 devices in a mesh: expert: 8 (over y, x, core), tensor: 4 (over z).
Axes of the slice: x: 2, y: 2, z: 4, core: 2. Of those that a mesh axis runs over, the one named last changes fastest.
Arguments:
- patches: bfloat16 [2, 32, 196, 768], P(None, ('expert', 'tensor')), may hold values from -6 to 6
- cotangent: bfloat16 [2, 32, 196, 768], P(None, ('expert', 'tensor')), may hold values from -6 to 6
- expert_ids: int32 [2, 32, 196, 2], P(None, ('expert', 'tensor')), may hold values from 0 to 7, as said below
- slots: int32 [2, 32, 196, 2], P(None, ('expert', 'tensor')), may hold values from 0 to 52, as said below
- attn_weights: float32 [768, 3072], P(('expert', 'tensor'))
- attn_first: float32 [768, 3072], P(('expert', 'tensor')), may hold values from -768 to 768
- attn_second: float32 [768, 3072], P(('expert', 'tensor')), may hold values from 6272 to 50176
- router_weights: float32 [768, 8], P(('expert', 'tensor')), may hold values from -0.15625 to 0.15625
- router_first: float32 [768, 8], P(('expert', 'tensor')), may hold values from -2048 to 2048
- router_second: float32 [768, 8], P(('expert', 'tensor')), may hold values from 50176 to 451584
- norm_params: float32 [4, 768], P(None, ('expert', 'tensor'))
- norm_first: float32 [4, 768], P(None, ('expert', 'tensor')), may hold values from -2560 to 2560
- norm_second: float32 [4, 768], P(None, ('expert', 'tensor')), may hold values from 100352 to 802816
- w_in: float32 [8, 768, 3072], P('expert', None, 'tensor'), may hold values from -0.21875 to 0.21875
- w_in_first: float32 [8, 768, 3072], P('expert', None, 'tensor'), may hold values from -256 to 256
- w_in_second: float32 [8, 768, 3072], P('expert', None, 'tensor'), may hold values from 2131.5 to 8538.25
- w_in_stat: float32 [8, 8, 384, 384], P('expert', 'tensor'), as said below
- w_in_basis: float32 [8, 8, 384, 384], P('expert', 'tensor'), as said below
- w_out: float32 [8, 3072, 768], P('expert', 'tensor'), may hold values from -2.5 to 2.5
- w_out_first: float32 [8, 3072, 768], P('expert', 'tensor'), may hold values from -28 to 28
- w_out_second: float32 [8, 3072, 768], P('expert', 'tensor'), may hold values from 24.5 to 98
- w_out_stat: float32 [8, 8, 384, 384], P('expert', 'tensor'), as said below
- w_out_basis: float32 [8, 8, 384, 384], P('expert', 'tensor'), as said below
- b_in: float32 [8, 3072], P('expert', 'tensor'), may hold values from -0.625 to 0.625
- b_in_first: float32 [8, 3072], P('expert', 'tensor'), may hold values from -256 to 256
- b_in_second: float32 [8, 3072], P('expert', 'tensor'), may hold values from 2131.5 to 8538.25
- b_out: float32 [8, 768], P('expert', 'tensor'), may hold values from -8 to 8
- b_out_first: float32 [8, 768], P('expert', 'tensor'), may hold values from -48 to 48
- b_out_second: float32 [8, 768], P('expert', 'tensor'), may hold values from 58.8 to 235.2
Outputs:
- block_output: bfloat16 [2, 32, 196, 768], P(None, ('expert', 'tensor'))
- input_grad: float32 [2, 32, 196, 768], P(None, ('expert', 'tensor'))
- attn_first_new: float32 [768, 3072], P(('expert', 'tensor'))
- attn_second_new: float32 [768, 3072], P(('expert', 'tensor'))
- attn_new: float32 [768, 3072], P(('expert', 'tensor'))
- attn_copy: bfloat16 [768, 3072], P(('expert', 'tensor'))
- router_first_new: float32 [768, 8], P(('expert', 'tensor'))
- router_second_new: float32 [768, 8], P(('expert', 'tensor'))
- router_new: float32 [768, 8], P(('expert', 'tensor'))
- router_copy: bfloat16 [768, 8], P(('expert', 'tensor'))
- norm_first_new: float32 [4, 768], P(None, ('expert', 'tensor'))
- norm_second_new: float32 [4, 768], P(None, ('expert', 'tensor'))
- norm_new: float32 [4, 768], P(None, ('expert', 'tensor'))
- w_in_first_new: float32 [8, 768, 3072], P('expert', None, 'tensor')
- w_in_second_new: float32 [8, 768, 3072], P('expert', None, 'tensor')
- w_in_new: float32 [8, 768, 3072], P('expert', None, 'tensor')
- w_in_copy: bfloat16 [8, 768, 3072], P('expert', None, 'tensor')
- w_in_stat_new: float32 [8, 8, 384, 384], P('expert', 'tensor')
- w_in_basis_new: float32 [8, 8, 384, 384], P('expert', 'tensor')
- w_out_first_new: float32 [8, 3072, 768], P('expert', 'tensor')
- w_out_second_new: float32 [8, 3072, 768], P('expert', 'tensor')
- w_out_new: float32 [8, 3072, 768], P('expert', 'tensor')
- w_out_copy: bfloat16 [8, 3072, 768], P('expert', 'tensor')
- w_out_stat_new: float32 [8, 8, 384, 384], P('expert', 'tensor')
- w_out_basis_new: float32 [8, 8, 384, 384], P('expert', 'tensor')
- b_in_first_new: float32 [8, 3072], P('expert', 'tensor')
- b_in_second_new: float32 [8, 3072], P('expert', 'tensor')
- b_in_new: float32 [8, 3072], P('expert', 'tensor')
- b_out_first_new: float32 [8, 768], P('expert', 'tensor')
- b_out_second_new: float32 [8, 768], P('expert', 'tensor')
- b_out_new: float32 [8, 768], P('expert', 'tensor')
Inputs may be any that keep to these rules, and one draw needn't show every extreme that they name: `expert_ids`: the 2 experts of a token are distinct. Within one device block (the 196 tokens of one device in one micro-batch) the pairs that name one expert take slots 0, 1, 2 and so on in a priority order in which all first choices come before all second choices; a pair whose turn comes after the expert's 52 slots are taken has slot 52 and is dropped. In every micro-batch some expert has all 52 slots taken in every device block. `w_in_basis`: each 384 x 384 block is orthogonal. `w_out_basis`: each 384 x 384 block is orthogonal. `w_in_stat`: each block is symmetric and positive definite. `w_out_stat`: each block is symmetric and positive definite.
All inputs are finite; a program needn't handle non-finite values.
Results may differ from a plain program's by a relative error of at most 0.038.
Values may be sent and summed in bfloat16 or wider, within the bound.
No kernel may reach another device: no remote copies, remote signals or barrier semaphores. Data moves between devices by JAX's collectives and lax.ppermute only.
A program may use at most 256 MiB of HBM per device.

v0:
```python
from functools import partial

import jax
import jax.numpy as jnp
from jax import lax
from jax.experimental import pallas as pl
from jax.experimental.pallas import tpu as pltpu
from jax.sharding import PartitionSpec as P

D = 768
HEADS = 12
HEAD_DIM = 64
SEQ = 196
TOPK = 2
MB = 2
STEP = 10
BLK = 384


MATMUL_ACCURACY = lax.Precision.HIGHEST
NORM_EPS = 1e-06
BETA_FIRST = 0.5
BETA_SECOND = 0.5
STAT_DECAY = 0.5
ADAM_EPS = 1e-08
DECAY_RATE = 0.1
RATE_DENSE = 0.05
RATE_NORMS = 0.4
RATE_INPUT = 0.04
RATE_OUTPUT = 0.4
RATE_BIASES = 0.05
RATE_OFFSETS = 1.0


def column_sum(left_side, right_side):
    return lax.dot_general(
        left_side, right_side, (((0,), (0,)), ((), ())), preferred_element_type=jnp.float32
    )


def row_product(left_side, right_side):
    return lax.dot_general(
        left_side, right_side, (((1,), (1,)), ((), ())), preferred_element_type=jnp.float32
    )


def moment_step(gradient, first_moment, second_moment):
    first_new = BETA_FIRST * first_moment + (1.0 - BETA_FIRST) * gradient
    second_new = BETA_SECOND * second_moment + (1.0 - BETA_SECOND) * gradient * gradient
    normed_step = (
        first_new
        / (1.0 - BETA_FIRST**STEP)
        / (jnp.sqrt(second_new / (1.0 - BETA_SECOND**STEP)) + ADAM_EPS)
    )
    return (first_new, second_new, normed_step)


def adam_update(weight, gradient, first_moment, second_moment, step_rate, weight_decay):
    first_new, second_new, normed_step = moment_step(gradient, first_moment, second_moment)
    return (first_new, second_new, weight - step_rate * (normed_step + weight_decay * weight))


EXPERT = "expert"
TENSOR = "tensor"
BOTH = (EXPERT, TENSOR)
VMEM_LIMIT = 56 * 2**20
SUB = 64


def mm(left, right):
    return jnp.dot(left, right, preferred_element_type=jnp.float32, precision=MATMUL_ACCURACY)


def mt(left, right):
    return lax.dot_general(
        left,
        right,
        (((1,), (1,)), ((), ())),
        preferred_element_type=jnp.float32,
        precision=MATMUL_ACCURACY,
    )


def tm(left, right):
    return lax.dot_general(
        left,
        right,
        (((0,), (0,)), ((), ())),
        preferred_element_type=jnp.float32,
        precision=MATMUL_ACCURACY,
    )


def factor_inverse(mats):
    n=SUB; B=jnp.broadcast_to; w=(8,2*n)
    lane=lax.broadcasted_iota(jnp.int32,w,1); sub=lax.broadcasted_iota(jnp.int32,w,0)
    X=[]
    for m in mats:
        tiles=[]
        for i in range(n//8):
            eye=jnp.where(lane==sub+8*i+n,1.0,0.0)
            tiles.append(jnp.concatenate([m[8*i:8*i+8,:],eye[:,n:]],axis=1))
        X.append(tiles)
    outs=[[] for _ in mats]
    for r in range(n//8):
        for m,tiles in enumerate(X):
            T=tiles[r]
            cols=[[B(tiles[t][:,8*r+k:8*r+k+1],w) for k in range(8)] for t in range(r,n//8)]
            a=[[B(cols[0][j][i:i+1,:],w) for j in range(i+1)] for i in range(8)]
            rows=[B(T[i:i+1,:],w) for i in range(8)]
            inv=[None]*8; l=[[None]*8 for _ in range(8)]
            for k in range(8):
                inv[k]=1.0/a[k][k]
                for i in range(k+1,8): l[i][k]=a[i][k]*inv[k]
                for i in range(k+1,8):
                    for j in range(k+1,i+1):
                        a[i][j]=a[i][j]-l[i][k]*a[j][k]
                for i in range(k+1,8): rows[i]=rows[i]-l[i][k]*rows[k]
            o=jnp.zeros(w,jnp.float32)
            for k in range(8): o=jnp.where(sub==k,rows[k]*lax.rsqrt(a[k][k]),o)
            outs[m].append(o[:,n:])
            if r+1<n//8:
                wv=[rows[k]*inv[k] for k in range(8)]
                for k in range(6,-1,-1):
                    for j in range(k+1,8): wv[k]=wv[k]-l[j][k]*wv[j]
                for t in range(r+1,n//8):
                    c=cols[t-r]
                    acc=c[0]*wv[0]
                    for k in range(1,8): acc=acc+c[k]*wv[k]
                    tiles[t]=tiles[t]-acc
    return [jnp.concatenate(o,axis=0) for o in outs]
def renew_kernel(z_ref,q_ref,m_ref):
    nb=z_ref.shape[0]; n=z_ref.shape[1]; kb=n//128; h=SUB
    for b in range(nb):
        z=z_ref[b]
        m_ref[b]=tm(z,z)
    for k in range(kb):
        o=128*k; sl=slice(o,o+128)
        d11=[m_ref[b,o:o+h,o:o+h] for b in range(nb)]
        i1=factor_inverse(d11)
        l21=[mt(m_ref[b,o+h:o+128,o:o+h],i1[b]) for b in range(nb)]
        d22=[m_ref[b,o+h:o+128,o+h:o+128]-mt(l21[b],l21[b]) for b in range(nb)]
        i2=factor_inverse(d22)
        inv=[]
        for b in range(nb):
            low=-mm(mm(i2[b],l21[b]),i1[b])
            inv.append(jnp.concatenate([jnp.concatenate([i1[b],jnp.zeros((h,h),jnp.float32)],1),jnp.concatenate([low,i2[b]],1)],0))
        for b in range(nb):
            q=z_ref[b,:,sl]
            for j in range(k):
                q=q-mt(q_ref[b,:,128*j:128*j+128],m_ref[b,sl,128*j:128*j+128])
            q_ref[b,:,sl]=mt(q,inv[b])
            if k+1<kb:
                p=mt(m_ref[b,o+128:,sl],inv[b])
                m_ref[b,o+128:,sl]=p
                m_ref[b,o+128:,o+128:]=m_ref[b,o+128:,o+128:]-mt(p,p)
def renew(z):
    return pl.pallas_call(renew_kernel,out_shape=jax.ShapeDtypeStruct(z.shape,z.dtype),
      in_specs=[pl.BlockSpec(memory_space=pltpu.VMEM)],out_specs=pl.BlockSpec(memory_space=pltpu.VMEM),
      scratch_shapes=[pltpu.VMEM(z.shape,jnp.float32)],
      compiler_params=pltpu.CompilerParams(vmem_limit_bytes=32*2**20))(z)


def low(values):
    return values.astype(jnp.bfloat16)


def wide(values):
    return values.astype(jnp.float32)


def dot(left, right):
    return jnp.dot(left, right, preferred_element_type=jnp.float32)


def vmem_call(kernel, **options):
    return pl.pallas_call(
        kernel, compiler_params=pltpu.CompilerParams(vmem_limit_bytes=VMEM_LIMIT), **options
    )


def full_block(shape):
    return pl.BlockSpec(shape, lambda *_: (0,) * len(shape))


def norm_parts(values):
    centred = values - jnp.mean(values, axis=-1, keepdims=True)
    scale = lax.rsqrt(jnp.mean(centred * centred, axis=-1, keepdims=True) + NORM_EPS)
    return centred * scale, scale


def norm_backward(grads, normed, scale, gain):
    inner = grads * gain
    return scale * (
        inner
        - jnp.mean(inner, axis=-1, keepdims=True)
        - normed * jnp.mean(inner * normed, axis=-1, keepdims=True)
    )


def route_mask(target, slot_total):
    slot_index = lax.broadcasted_iota(jnp.int32, (target.shape[0], slot_total), 1)
    hit = (slot_index == target[:, :1]) | (slot_index == target[:, 1:2])
    return jnp.where(hit, 1.0, 0.0)


def masked_softmax(logits, count):
    lanes = lax.broadcasted_iota(jnp.int32, logits.shape, 1)
    inside = lanes < count
    peak = jnp.max(jnp.where(inside, logits, -jnp.inf), axis=-1, keepdims=True)
    raised = jnp.where(inside, jnp.exp(jnp.where(inside, logits - peak, 0.0)), 0.0)
    return raised / jnp.sum(raised, axis=-1, keepdims=True)


def softmax_rows(scores):
    raised = jnp.exp(scores - jnp.max(scores, axis=-1, keepdims=True))
    return raised / jnp.sum(raised, axis=-1, keepdims=True)


def dispatch_kernel(target_ref, rows_ref, out_ref):
    experts, copies, steps, padded, _ = out_ref.shape
    for step in range(steps):
        routing = low(route_mask(target_ref[step], experts * padded))
        rows = column_sum(routing, rows_ref[step, 0])
        rows = low(rows.reshape(experts, padded, D))
        for copy in range(copies):
            out_ref[:, copy, step] = rows


def attention_kernel(
    experts, x_ref, target_ref, a_ref, out_ref, qkv_ref, mixed_ref, middle_ref, probs_ref
):
    copies, padded = (out_ref.shape[2], out_ref.shape[3])
    inputs = wide(x_ref[0, 0])
    extra = a_ref[:, 4 * D :]
    vectors = wide(extra).T
    gains = [vectors[experts + i : experts + i + 1] for i in range(4)]
    normed, _ = norm_parts(inputs)
    normed_low = low(normed * gains[0] + gains[1])
    qkv_ref[0] = low(dot(normed_low, a_ref[:, : 3 * D]))
    lanes = lax.broadcasted_iota(jnp.int32, (SEQ, 2 * HEAD_DIM), 1)
    for pair in range(HEADS // 2):
        start = 2 * HEAD_DIM * pair
        query = qkv_ref[0, :, start : start + 2 * HEAD_DIM]
        keys = qkv_ref[0, :, D + start : D + start + 2 * HEAD_DIM]
        values = qkv_ref[0, :, 2 * D + start : 2 * D + start + 2 * HEAD_DIM]
        both = []
        for side in range(2):
            here = (lanes < HEAD_DIM) if side == 0 else (lanes >= HEAD_DIM)
            scores = row_product(jnp.where(here, query, 0), keys) * HEAD_DIM ** (-0.5)
            both.append(dot(low(softmax_rows(scores)), values))
        mixed_ref[0, :, start : start + 2 * HEAD_DIM] = low(
            jnp.where(lanes < HEAD_DIM, both[0], both[1])
        )
    middle = inputs + dot(mixed_ref[0], a_ref[:, 3 * D : 4 * D])
    middle_ref[0] = middle
    normed, _ = norm_parts(middle)
    moe_low = low(normed * gains[2] + gains[3])
    probs_ref[0] = masked_softmax(dot(moe_low, extra), experts)
    routing = low(route_mask(target_ref[0], experts * padded))
    rows = low(column_sum(routing, moe_low).reshape(experts, padded, D))
    for copy in range(copies):
        out_ref[0, :, copy] = rows


def attention_backward_kernel(
    experts,
    x_ref,
    up_ref,
    target_ref,
    back_ref,
    qkv_ref,
    mixed_ref,
    middle_ref,
    probs_ref,
    a_ref,
    *refs,
):
    out_ref, grad_ref, normed_ref, joined_ref, branch_ref, moe_ref, logit_ref, vector_ref = refs[-8:]
    copies, padded = (back_ref.shape[1], back_ref.shape[3])
    slot_total = experts * padded
    extra = a_ref[:, 4 * D :]
    vectors = wide(extra).T
    gains = [vectors[experts + i : experts + i + 1] for i in range(4)]
    inputs = wide(x_ref[0, 0])
    upstream_low = up_ref[0, 0]
    upstream = wide(upstream_low)
    middle = middle_ref[0]
    probs = probs_ref[0]

    def collected(kind):
        total = wide(back_ref[:, 0, kind])
        for copy in range(1, copies):
            total = total + wide(back_ref[:, copy, kind])
        return low(total.reshape(slot_total, D))

    coming = collected(0)
    grad_coming = collected(1)
    routing = route_mask(target_ref[0], slot_total)
    member = jnp.where(
        lax.broadcasted_iota(jnp.int32, (probs.shape[1], slot_total), 1) // padded
        == lax.broadcasted_iota(jnp.int32, (probs.shape[1], slot_total), 0),
        1.0,
        0.0,
    )
    member_low = low(member)
    probs_high = low(probs)
    slot_gate = routing * (dot(probs_high, member_low) + dot(low(probs - wide(probs_high)), member_low))
    gate_high = low(slot_gate)
    final = middle + dot(gate_high, coming) + dot(low(slot_gate - wide(gate_high)), coming)
    out_ref[0, 0] = low(final)
    slot_grads = routing * row_product(upstream_low, coming)
    slot_high = low(slot_grads)
    prob_grads = row_product(slot_high, member_low) + row_product(
        low(slot_grads - wide(slot_high)), member_low
    )
    logit_low = low(
        probs * (prob_grads - jnp.sum(prob_grads * probs, axis=-1, keepdims=True))
    )
    logit_ref[...] = logit_low
    moe_grad = dot(low(routing), grad_coming) + row_product(logit_low, extra)
    normed, scale = norm_parts(middle)
    moe_ref[...] = low(normed * gains[2] + gains[3])
    vector_ref[2:3] = jnp.sum(moe_grad * normed, axis=0, keepdims=True)
    vector_ref[3:4] = jnp.sum(moe_grad, axis=0, keepdims=True)
    grad_middle = upstream + norm_backward(moe_grad, normed, scale, gains[2])
    branch_low = low(grad_middle)
    branch_ref[...] = branch_low
    grad_mixed = low(row_product(branch_low, a_ref[:, 3 * D : 4 * D]))
    lanes = lax.broadcasted_iota(jnp.int32, (SEQ, 2 * HEAD_DIM), 1)
    for pair in range(HEADS // 2):
        start = 2 * HEAD_DIM * pair
        stop = start + 2 * HEAD_DIM
        query = qkv_ref[0, :, start:stop]
        keys = qkv_ref[0, :, D + start : D + stop]
        values = qkv_ref[0, :, 2 * D + start : 2 * D + stop]
        grad_here = grad_mixed[:, start:stop]
        results = []
        for side in range(2):
            here = (lanes < HEAD_DIM) if side == 0 else (lanes >= HEAD_DIM)
            scores = row_product(jnp.where(here, query, 0), keys) * HEAD_DIM ** (-0.5)
            weights = softmax_rows(scores)
            grad_probs = row_product(jnp.where(here, grad_here, 0), values)
            grad_scores = low(
                weights
                * (grad_probs - jnp.sum(grad_probs * weights, axis=-1, keepdims=True))
            )
            results.append(
                (
                    dot(grad_scores, keys) * HEAD_DIM ** (-0.5),
                    column_sum(grad_scores, query) * HEAD_DIM ** (-0.5),
                    column_sum(low(weights), grad_here),
                )
            )
        for part in range(3):
            joined_ref[:, part * D + start : part * D + stop] = low(
                jnp.where(lanes < HEAD_DIM, results[0][part], results[1][part])
            )
    grad_normed = row_product(joined_ref[...], a_ref[:, : 3 * D])
    normed, scale = norm_parts(inputs)
    normed_ref[...] = low(normed * gains[0] + gains[1])
    vector_ref[4:8] = jnp.zeros((4, D), jnp.float32)
    vector_ref[0:1] = jnp.sum(grad_normed * normed, axis=0, keepdims=True)
    vector_ref[1:2] = jnp.sum(grad_normed, axis=0, keepdims=True)
    grad_ref[0, 0] = grad_middle + norm_backward(grad_normed, normed, scale, gains[0])


def weight_sums_kernel(experts, core_ref, mixed_ref, *refs):
    own_ref, other_ref = refs[-2:]
    steps = [refs[6 * i : 6 * i + 6] for i in range(MB)]
    held, block, _ = own_ref.shape
    first_core = core_ref[0] == 0

    def write(total, start):
        stop = start + total.shape[1]
        pairs = total.reshape(held, 2, block, total.shape[1])
        even, odd = (pairs[:, 0], pairs[:, 1])
        own_ref[:, :, start:stop] = jnp.where(first_core, even, odd)
        other_ref[:, :, start:stop] = low(jnp.where(first_core, odd, even))

    for part in range(3):
        total = sum(column_sum(s[0][...], s[1][:, part * D : part * D + D]) for s in steps)
        write(total, part * D)
    write(sum(column_sum(mixed_ref[i], s[2][...]) for i, s in enumerate(steps)), 3 * D)
    vectors = sum(s[5][...] for s in steps)
    vectors = jnp.concatenate(
        [
            jnp.zeros((experts, D), jnp.float32),
            vectors,
            jnp.zeros((128 - experts - vectors.shape[0], D), jnp.float32),
        ],
        axis=0,
    )
    write(sum(column_sum(s[3][...], s[4][...]) for s in steps) + vectors.T, 4 * D)


def gelu_parts(values):
    raised = jnp.exp(-0.5 * values * values)
    root = 1.0 / (1.0 + (0.3275911 * 0.5**0.5) * jnp.abs(values))
    tail = 1.061405429 * root - 1.453152027
    tail = tail * root + 1.421413741
    tail = tail * root - 0.284496736
    tail = tail * root + 0.254829592
    tail = 0.5 * tail * root * raised
    return jnp.where(values >= 0.0, 1.0 - tail, tail), raised * 0.3989422804014327


def hidden_kernel(
    experts,
    expert_ref,
    rows_ref,
    up_ref,
    router_ref,
    own_ref,
    peer_ref,
    bias_ref,
    hidden_own_ref,
    hidden_peer_ref,
    slope_own_ref,
    slope_peer_ref,
    grad_ref,
    sum_ref,
):
    count, padded = rows_ref.shape[:2]
    units = own_ref.shape[1]
    rows = low(wide(rows_ref[...]).reshape(count * padded, D))
    probs = masked_softmax(dot(rows, router_ref[...]), experts)
    lanes = lax.broadcasted_iota(jnp.int32, probs.shape, 1)
    gate = jnp.sum(jnp.where(lanes == expert_ref[0], probs, 0.0), axis=-1, keepdims=True)
    grad = low(gate * wide(up_ref[...]).reshape(count * padded, D))
    grad_ref[...] = grad
    partial = jnp.sum(wide(grad), axis=0, keepdims=True)

    @pl.when(pl.program_id(0) == 0)
    def _():
        sum_ref[...] = jnp.zeros_like(sum_ref)

    sum_ref[0:1] += partial
    for side, (weight, hidden_ref, slope_ref) in enumerate(
        ((own_ref, hidden_own_ref, slope_own_ref), (peer_ref, hidden_peer_ref, slope_peer_ref))
    ):
        values = dot(rows, weight[...]) + bias_ref[:, side * units : (side + 1) * units]
        area, density = gelu_parts(values)
        hidden_ref[...] = low(values * area)
        slope_ref[...] = low(area + values * density)


def result_kernel(
    hidden_own_ref,
    hidden_peer_ref,
    slope_own_ref,
    slope_peer_ref,
    grad_ref,
    out_own_ref,
    out_peer_ref,
    in_own_ref,
    in_peer_ref,
    bias_ref,
    back_ref,
    pre_own_ref,
    pre_peer_ref,
    sum_ref,
):
    count, _, padded, _ = back_ref.shape
    units = in_own_ref.shape[1]

    @pl.when(pl.program_id(0) == 0)
    def _():
        sum_ref[...] = jnp.zeros_like(sum_ref)

    out_term = (
        dot(hidden_own_ref[...], out_own_ref[...])
        + dot(hidden_peer_ref[...], out_peer_ref[...])
        + bias_ref[...]
    )
    back_ref[:, 0] = low(out_term.reshape(count, padded, D))
    grad_term = None
    for side, (slope, out_weight, in_weight, pre_ref) in enumerate(
        (
            (slope_own_ref, out_own_ref, in_own_ref, pre_own_ref),
            (slope_peer_ref, out_peer_ref, in_peer_ref, pre_peer_ref),
        )
    ):
        pre = low(row_product(grad_ref[...], out_weight[...]) * wide(slope[...]))
        pre_ref[...] = pre
        sum_ref[0:1, side * units : (side + 1) * units] += jnp.sum(
            wide(pre), axis=0, keepdims=True
        )
        term = row_product(pre, in_weight[...])
        grad_term = term if grad_term is None else grad_term + term
    back_ref[:, 1] = low(grad_term.reshape(count, padded, D))


def split(values):
    high = low(values)
    return high, low(values - wide(high))


def split_dot(left, right, dims):
    def one(a, b):
        return lax.dot_general(a, b, (dims, ((), ())), preferred_element_type=jnp.float32)

    return one(left[0], right[0]) + (one(left[0], right[1]) + one(left[1], right[0]))


def turn_kernel(
    along_rows,
    rate,
    own_ref,
    other_ref,
    weight_ref,
    first_ref,
    second_ref,
    stat_ref,
    basis_ref,
    first_out,
    second_out,
    weight_out,
    copy_out,
    stat_out,
    stretched_out,
):
    gradient = own_ref[...] + wide(other_ref[...])
    basis = basis_ref[0, 0]
    gradient_parts, basis_parts = (split(gradient), split(basis))
    if along_rows:
        turned = split_dot(basis_parts, gradient_parts, ((0,), (0,)))
        outer = mt(gradient, gradient)
    else:
        turned = split_dot(gradient_parts, basis_parts, ((1,), (0,)))
        outer = tm(gradient, gradient)
    first_new, second_new, step = moment_step(turned, first_ref[0], second_ref[0])
    first_out[0] = first_new
    second_out[0] = second_new
    step_parts = split(step)
    if along_rows:
        returned = split_dot(basis_parts, step_parts, ((1,), (0,)))
    else:
        returned = split_dot(step_parts, basis_parts, ((1,), (1,)))
    weight = weight_ref[0]
    weight_new = weight - rate * (returned + DECAY_RATE * weight)
    weight_out[0] = weight_new
    copy_out[0] = low(weight_new)
    stat_new = STAT_DECAY * stat_ref[0, 0] + (1.0 - STAT_DECAY) * outer
    stat_out[0, 0] = stat_new
    stretched_out[0] = mm(stat_new, basis)


def swap(values, axis, distance):
    size = lax.axis_size(axis)
    return lax.ppermute(values, axis, [(i, i ^ distance) for i in range(size)])


def ordered(bit, mine, other):
    return jnp.where(bit == 0, jnp.stack([mine, other]), jnp.stack([other, mine]))


def gather_rows(shard):
    experts, tensors = (lax.axis_size(EXPERT), lax.axis_size(TENSOR))
    expert, tensor = (lax.axis_index(EXPERT), lax.axis_index(TENSOR))
    block = shard[None]
    distance = 1
    while distance < tensors:
        other = swap(block, TENSOR, distance)
        block = ordered((tensor // distance) % 2, block, other).reshape(-1, *shard.shape)
        distance *= 2
    first_stage = block
    block = block[None]
    distance = 2
    while distance < experts // 4:
        other = swap(block, EXPERT, distance)
        block = ordered((expert // distance) % 2, block, other).reshape(-1, *block.shape[1:])
        distance *= 2
    near, far = (distance, 2 * distance)
    middle = tensors // 2
    from_near, from_far = (swap(block, EXPERT, near), swap(block, EXPERT, far))
    corner = jnp.concatenate(
        [swap(from_far[:, :middle], EXPERT, near), swap(from_near[:, middle:], EXPERT, far)],
        axis=1,
    )
    second_stage = corner
    pieces = (block, from_near, from_far, corner)
    crossed = [swap(piece, EXPERT, 1) for piece in pieces]
    near_bit, far_bit = ((expert // near) % 2, (expert // far) % 2)

    def arranged(four):
        return ordered(
            far_bit,
            ordered(near_bit, four[0], four[1]),
            ordered(near_bit, four[2], four[3]),
        ).reshape(-1, *block.shape[1:])

    whole = ordered(expert % 2, arranged(pieces), arranged(crossed))
    whole = jnp.moveaxis(whole, 0, 1)
    return whole.reshape(-1, shard.shape[1]), first_stage, second_stage


def scatter_sums(held, sending):
    experts, tensors = (lax.axis_size(EXPERT), lax.axis_size(TENSOR))
    expert, tensor = (lax.axis_index(EXPERT), lax.axis_index(TENSOR))
    columns = held.shape[2]

    def pick(values, index, axis=0):
        return lax.dynamic_index_in_dim(values, index, axis, False)

    held = held + wide(swap(sending, EXPERT, 1))
    near, far = (experts // 4, experts // 2)
    near_bit, far_bit = ((expert // near) % 2, (expert // far) % 2)
    held = held.reshape(4, experts // 8, tensors, -1, columns)
    place = 2 * far_bit + near_bit
    own, to_near, to_far, to_corner = (
        pick(held, place),
        pick(held, place ^ 1),
        pick(held, place ^ 2),
        pick(held, place ^ 3),
    )
    middle = tensors // 2
    passed_near = swap(low(to_corner[:, :middle]), EXPERT, near)
    passed_far = swap(low(to_corner[:, middle:]), EXPERT, far)
    to_far = jnp.concatenate([to_far[:, :middle] + wide(passed_near), to_far[:, middle:]], axis=1)
    to_near = jnp.concatenate([to_near[:, :middle], to_near[:, middle:] + wide(passed_far)], axis=1)
    held = (
        own
        + wide(swap(low(to_near), EXPERT, near))
        + wide(swap(low(to_far), EXPERT, far))
    )
    distance = experts // 8
    while distance >= 2:
        bit = (expert // distance) % 2
        halves = held.reshape(2, -1, *held.shape[1:])
        held = pick(halves, bit) + wide(swap(low(pick(halves, 1 - bit)), EXPERT, distance))
        distance //= 2
    held = held.reshape(tensors, -1, columns)
    distance = tensors // 2
    while distance >= 1:
        bit = (tensor // distance) % 2
        halves = held.reshape(2, -1, *held.shape[1:])
        held = pick(halves, bit) + wide(swap(low(pick(halves, 1 - bit)), TENSOR, distance))
        distance //= 2
    return held.reshape(-1, columns)


def soap(along_rows, rate, own, other, weight, first, second, statistic, rotation):
    blocks = statistic.shape[1]
    f32 = jnp.float32
    if along_rows:
        flat = pl.BlockSpec((BLK, D), lambda i: (i, 0))
        deep = pl.BlockSpec((1, BLK, D), lambda i: (0, i, 0))
    else:
        flat = pl.BlockSpec((D, BLK), lambda i: (0, i))
        deep = pl.BlockSpec((1, D, BLK), lambda i: (0, 0, i))
    square = pl.BlockSpec((1, 1, BLK, BLK), lambda i: (0, i, 0, 0))
    results = vmem_call(
        partial(turn_kernel, along_rows, rate),
        grid=(blocks,),
        in_specs=[flat, flat, deep, deep, deep, square, square],
        out_specs=[deep] * 4 + [square, pl.BlockSpec((1, BLK, BLK), lambda i: (i, 0, 0))],
        out_shape=[jax.ShapeDtypeStruct(weight.shape, f32)] * 3
        + [
            jax.ShapeDtypeStruct(weight.shape, jnp.bfloat16),
            jax.ShapeDtypeStruct(statistic.shape, f32),
            jax.ShapeDtypeStruct(statistic.shape[1:], f32),
        ],
    )(own, other, weight, first, second, statistic, rotation)
    return (*results[:5], renew(results[5])[None])


def per_device(
    patches,
    cotangent,
    expert_ids,
    slots,
    attn_weights,
    attn_first,
    attn_second,
    router_weights,
    router_first,
    router_second,
    norm_params,
    norm_first,
    norm_second,
    w_in,
    w_in_first,
    w_in_second,
    w_in_stat,
    w_in_basis,
    w_out,
    w_out_first,
    w_out_second,
    w_out_stat,
    w_out_basis,
    b_in,
    b_in_first,
    b_in_second,
    b_out,
    b_out_first,
    b_out_second,
):
    tokens_here = SEQ
    expert_total = router_weights.shape[1]
    capacity = (105 * TOPK * tokens_here + 100 * expert_total - 1) // (100 * expert_total)
    padded = 8 * ((capacity + 7) // 8)
    experts, tensors = (lax.axis_size(EXPERT), lax.axis_size(TENSOR))
    expert, tensor = (lax.axis_index(EXPERT), lax.axis_index(TENSOR))
    half = tensors // 2
    members = expert_total * half
    units = w_in.shape[2]
    shard_columns = b_out.shape[1]
    columns = 4 * D + 128
    bf16, f32 = (jnp.bfloat16, jnp.float32)
    shape = jax.ShapeDtypeStruct
    partner = [(i, (i + half) % tensors) for i in range(tensors)]
    groups = [
        [e * tensors + z for e in range(experts) for z in range(h * half, (h + 1) * half)]
        for h in range(2)
    ]

    def exchange(values):
        return lax.all_to_all(values, BOTH, 0, 0, axis_index_groups=groups, tiled=True)

    def across(values):
        return lax.ppermute(values, TENSOR, partner)

    packed = jnp.concatenate(
        [
            low(attn_weights),
            low(router_weights),
            low(norm_params).T,
            jnp.zeros((attn_weights.shape[0], 128 - expert_total - 4), bf16),
        ],
        axis=1,
    )
    gathered, first_stage, second_stage = gather_rows(packed)
    in_own, out_own = (low(w_in[0]), low(w_out[0]))
    sent_in, sent_out, _ = lax.optimization_barrier((in_own, out_own, first_stage))
    in_peer, out_peer = (across(sent_in), across(sent_out))
    b_in_low, b_out_low = (low(b_in), low(b_out))
    peer_bias = across(jnp.concatenate([b_in_low, b_out_low], axis=1))
    bias_in = wide(jnp.concatenate([b_in_low, peer_bias[:, :units]], axis=1))
    bias_out = jnp.zeros((1, D), f32)
    own_place = tensor * shard_columns
    peer_place = ((tensor + half) % tensors) * shard_columns
    bias_out = lax.dynamic_update_slice(bias_out, wide(b_out_low), (0, own_place))
    bias_out = lax.dynamic_update_slice(bias_out, wide(peer_bias[:, units:]), (0, peer_place))
    chosen = expert_ids.reshape(MB, tokens_here, TOPK)
    placed = slots.reshape(MB, tokens_here, TOPK)
    target = jnp.where(placed < capacity, chosen * padded + placed, -1)
    target_all = full_block(target.shape)
    up_sent = vmem_call(
        dispatch_kernel,
        grid=(1,),
        in_specs=[target_all, full_block(cotangent.shape)],
        out_specs=full_block((expert_total, half, MB, padded, D)),
        out_shape=shape((expert_total, half, MB, padded, D), bf16),
    )(target, cotangent)
    up_sent, _ = lax.optimization_barrier((up_sent, second_stage))
    up_all = exchange(up_sent.reshape(members, MB, padded, D))
    image = pl.BlockSpec((1, 1, SEQ, D), lambda i: (i, 0, 0, 0))

    def per_step(*tail):
        return pl.BlockSpec((1, *tail), lambda i: (i,) + (0,) * len(tail))

    sent, qkv, mixed, middle, probs = vmem_call(
        partial(attention_kernel, expert_total),
        grid=(MB,),
        in_specs=[image, per_step(SEQ, TOPK), full_block((D, columns))],
        out_specs=[
            per_step(expert_total, half, padded, D),
            per_step(SEQ, 3 * D),
            per_step(SEQ, D),
            per_step(SEQ, D),
            per_step(SEQ, 128),
        ],
        out_shape=[
            shape((MB, expert_total, half, padded, D), bf16),
            shape((MB, SEQ, 3 * D), bf16),
            shape((MB, SEQ, D), bf16),
            shape((MB, SEQ, D), f32),
            shape((MB, SEQ, 128), f32),
        ],
    )(patches, target, gathered)
    arrived = [exchange(sent[step].reshape(members, padded, D)) for step in range(MB)]
    count = max(
        n
        for n in range(1, members + 1)
        if members % n == 0 and n * padded <= 256 and (n * padded) % 16 == 0
    )
    tile = count * padded
    total_rows = members * padded
    tiles = members // count

    def rows_of(width):
        return pl.BlockSpec((tile, width), lambda i: (i, 0))

    expert_scalar = jnp.reshape(expert, (1,)).astype(jnp.int32)
    in_smem = pl.BlockSpec(memory_space=pltpu.SMEM)
    hidden = []
    for step in range(MB):
        hidden.append(
            vmem_call(
                partial(hidden_kernel, expert_total),
                grid=(tiles,),
                in_specs=[
                    in_smem,
                    pl.BlockSpec((count, padded, D), lambda i: (i, 0, 0)),
                    pl.BlockSpec((count, None, padded, D), lambda i, step=step: (i, step, 0, 0)),
                    pl.BlockSpec((D, 128), lambda i: (0, 4 * D // 128)),
                    full_block((D, units)),
                    full_block((D, units)),
                    full_block((1, 2 * units)),
                ],
                out_specs=[rows_of(units)] * 4 + [rows_of(D), full_block((8, D))],
                out_shape=[shape((total_rows, units), bf16)] * 4
                + [shape((total_rows, D), bf16), shape((8, D), f32)],
            )(expert_scalar, arrived[step], up_all, gathered, in_own, in_peer, bias_in)
        )
    sum_out = sum(column_sum(h[1], h[4]) for h in hidden)
    out_other = across(low(sum_out))
    sum_out_own = sum(column_sum(h[0], h[4]) for h in hidden)
    results = []
    for step in range(MB):
        results.append(
            vmem_call(
                result_kernel,
                grid=(tiles,),
                in_specs=[rows_of(units)] * 4
                + [
                    rows_of(D),
                    full_block((units, D)),
                    full_block((units, D)),
                    full_block((D, units)),
                    full_block((D, units)),
                    full_block((1, D)),
                ],
                out_specs=[
                    pl.BlockSpec((count, 2, padded, D), lambda i: (i, 0, 0, 0)),
                    rows_of(units),
                    rows_of(units),
                    full_block((8, 2 * units)),
                ],
                out_shape=[
                    shape((members, 2, padded, D), bf16),
                    shape((total_rows, units), bf16),
                    shape((total_rows, units), bf16),
                    shape((8, 2 * units), f32),
                ],
            )(*hidden[step][:5], out_own, out_peer, in_own, in_peer, bias_out)
        )
    returned = [exchange(r[0]) for r in results]
    flat_rows = [rows.reshape(total_rows, D) for rows in arrived]
    sum_in = sum(column_sum(rows, r[2]) for rows, r in zip(flat_rows, results))
    in_other = across(low(sum_in))
    sum_in_own = sum(column_sum(rows, r[1]) for rows, r in zip(flat_rows, results))
    sum_bin = sum(r[3][:1] for r in results)
    sum_bout = sum(h[5][:1] for h in hidden)
    bias_sums = jnp.concatenate(
        [
            sum_bin[:, units:],
            lax.dynamic_slice_in_dim(sum_bout, peer_place, shard_columns, 1),
        ],
        axis=1,
    )
    bias_other = across(bias_sums)
    grad_bin = sum_bin[:, :units] + bias_other[:, :units]
    grad_bout = (
        lax.dynamic_slice_in_dim(sum_bout, own_place, shard_columns, 1) + bias_other[:, units:]
    )
    backward = []
    for step in range(MB):
        first = step == 0
        here = pl.BlockSpec((1, 1, SEQ, D), lambda i, step=step: (step, 0, 0, 0))

        def of_step(*tail, step=step):
            return pl.BlockSpec((1, *tail), lambda i: (step,) + (0,) * len(tail))

        back = returned[step].reshape(expert_total, half, 2, padded, D)
        outs = [
            (shape(patches.shape, bf16), here),
            (shape(patches.shape, f32), here),
            (shape((SEQ, D), bf16), full_block((SEQ, D))),
            (shape((SEQ, 3 * D), bf16), full_block((SEQ, 3 * D))),
            (shape((SEQ, D), bf16), full_block((SEQ, D))),
            (shape((SEQ, D), bf16), full_block((SEQ, D))),
            (shape((SEQ, 128), bf16), full_block((SEQ, 128))),
            (shape((8, D), f32), full_block((8, D))),
        ]
        earlier = [] if first else list(backward[-1][:2])
        backward.append(
            vmem_call(
                partial(attention_backward_kernel, expert_total),
                grid=(1,),
                in_specs=[
                    here,
                    here,
                    of_step(SEQ, TOPK),
                    full_block(back.shape),
                    of_step(SEQ, 3 * D),
                    of_step(SEQ, D),
                    of_step(SEQ, D),
                    of_step(SEQ, 128),
                    full_block((D, columns)),
                ]
                + [pl.BlockSpec(memory_space=pl.ANY)] * len(earlier),
                out_specs=[o[1] for o in outs],
                out_shape=[o[0] for o in outs],
                input_output_aliases={} if first else {9: 0, 10: 1},
            )(patches, cotangent, target, back, qkv, mixed, middle, probs, gathered, *earlier)
        )
    core_scalar = jnp.reshape(expert % 2, (1,)).astype(jnp.int32)
    block_rows = tensors * attn_weights.shape[0]
    flat_steps = [value for b in backward for value in b[2:]]
    core_shape = (experts // 2, block_rows, columns)
    whole_vmem = pl.BlockSpec(memory_space=pltpu.VMEM)
    held, sending = vmem_call(
        partial(weight_sums_kernel, expert_total),
        in_specs=[in_smem] + [whole_vmem] * (1 + len(flat_steps)),
        out_specs=[whole_vmem] * 2,
        out_shape=[shape(core_shape, f32), shape(core_shape, bf16)],
    )(core_scalar, mixed, *flat_steps)
    mine = scatter_sums(held, sending)
    grad_attn = mine[:, : 4 * D]
    grad_router = mine[:, 4 * D : 4 * D + expert_total]
    grad_norm = mine[:, 4 * D + expert_total : 4 * D + expert_total + 4].T
    attn_first_new, attn_second_new, attn_new = adam_update(
        attn_weights, grad_attn, attn_first, attn_second, RATE_DENSE, DECAY_RATE
    )
    router_first_new, router_second_new, router_new = adam_update(
        router_weights, grad_router, router_first, router_second, RATE_DENSE, DECAY_RATE
    )
    norm_first_new, norm_second_new, norm_new = adam_update(
        norm_params, grad_norm, norm_first, norm_second, RATE_NORMS, 0.0
    )
    w_out_results = soap(
        True,
        RATE_OUTPUT,
        sum_out_own,
        out_other,
        w_out,
        w_out_first,
        w_out_second,
        w_out_stat,
        w_out_basis,
    )
    w_in_results = soap(
        False,
        RATE_INPUT,
        sum_in_own,
        in_other,
        w_in,
        w_in_first,
        w_in_second,
        w_in_stat,
        w_in_basis,
    )
    bin_first_new, bin_second_new, bin_new = adam_update(
        b_in, grad_bin, b_in_first, b_in_second, RATE_BIASES, 0.0
    )
    bout_first_new, bout_second_new, bout_new = adam_update(
        b_out, grad_bout, b_out_first, b_out_second, RATE_OFFSETS, 0.0
    )
    return (
        *backward[-1][:2],
        attn_first_new,
        attn_second_new,
        attn_new,
        low(attn_new),
        router_first_new,
        router_second_new,
        router_new,
        low(router_new),
        norm_first_new,
        norm_second_new,
        norm_new,
        *w_in_results,
        *w_out_results,
        bin_first_new,
        bin_second_new,
        bin_new,
        bout_first_new,
        bout_second_new,
        bout_new,
    )


def solution(mesh):
    tokens = P(None, BOTH, None, None)
    rows = P(BOTH, None)
    columns = P(None, BOTH)
    first_layer = P(EXPERT, None, TENSOR)
    second_layer = P(EXPERT, TENSOR, None)
    blocks = P(EXPERT, TENSOR, None, None)
    biases = P(EXPERT, TENSOR)
    in_specs = (
        (tokens,) * 4
        + (rows,) * 6
        + (columns,) * 3
        + (first_layer,) * 3
        + (blocks,) * 2
        + (second_layer,) * 3
        + (blocks,) * 2
        + (biases,) * 6
    )
    out_specs = (
        (tokens,) * 2
        + (rows,) * 8
        + (columns,) * 3
        + (first_layer,) * 4
        + (blocks,) * 2
        + (second_layer,) * 4
        + (blocks,) * 2
        + (biases,) * 6
    )
    return jax.shard_map(
        per_device, mesh=mesh, in_specs=in_specs, out_specs=out_specs, check_vma=False
    )
```

profile of v0, /device:TPU:0, one launch (start us, length us, event | category | flops | bytes accessed | tf_op | source)
XLA Modules:
  0.0 599.1 jit_solution(4093956800732454820)
XLA Ops:
  13.4 13.1 %collective-permute-done.1 = bf16[2,24,3200]{2,1,0:T(8,128)(2,1)S(1)} collective-permute-done((bf16[2,24,3200]{2,1,0:T(8,128)(2,1)S(1)}, bf16[2,24,3200]{2,1,0:T(8,128)(2,1)S(1)}, u32[]{:S(2)}, u32[]{:S(2)}) %collective-permute-start.1) | collective-permute-done | bytes 307232 | tf_op jit(solution)/shard_map/ppermute | solution.py:551
  30.6 10.9 %collective-permute-done.3 = bf16[1,4,24,3200]{3,2,1,0:T(8,128)(2,1)S(1)} collective-permute-done((bf16[1,4,24,3200]{3,2,1,0:T(8,128)(2,1)S(1)}, bf16[1,4,24,3200]{3,2,1,0:T(8,128)(2,1)S(1)}, u32[]{:S(2)}, u32[]{:S(2)}) %collective-permute-start.3) | collective-permute-done | bytes 614432 | tf_op jit(solution)/shard_map/ppermute | solution.py:551
  55.5 11.5 %shard_map.516 = (bf16[2,8,2,56,768]{4,3,2,1,0:T(8,128)(2,1)}, bf16[2,196,2304]{2,1,0:T(8,128)(2,1)}, bf16[2,196,768]{2,1,0:T(8,128)(2,1)}, f32[2,196,768]{2,1,0:T(8,128)}, f32[2,196,128]{2,1,0:T(8,128)}) custom-call(bf16[2,1,196,768]{3,2,1,0:T(8,128)(2,1)} %copy.128.x_ref, s32[2,196,2]{2,1,0:T(8,128)} %select_bitcast_fusion.target_ref, ...), custom_call_target="tpu_custom_call" | custom-call | tf_op jit(solution)/shard_map/pallas_call | solution.py:763
  70.5 5.4 all-to-all-start.3
  80.2 14.5 %all-to-all-done.3.rows_ref = bf16[16,56,768]{2,1,0:T(8,128)(2,1)S(1)} async-done(((bf16[16,56,768]{2,1,0:T(8,128)(2,1)}), bf16[16,56,768]{2,1,0:T(8,128)(2,1)S(1)}, u32[]{:S(2)}, u32[]{:S(2)}) %all-to-all-start.3) | async-done | bytes 1376288 | tf_op jit(solution)/shard_map/all_to_all | solution.py:719
  94.8 38.3 %all_to_all.25.up_ref = bf16[16,2,56,768]{3,2,1,0:T(8,128)(2,1)} all-to-all(bf16[16,2,56,768]{3,2,1,0:T(8,128)(2,1)} %bitcast.88), channel_id=1, replica_groups={{0,1,4,5,8,9,12,13,16,17,20,21,24,25,28,29},{2,3,6,7,10,11,14,15,18,19,..., dimensions={0} | all-to-all | bytes 5505024 | tf_op jit(solution)/shard_map/all_to_all | solution.py:719
  149.0 97.8 %collective-permute-done.11 = bf16[1,960]{1,0:T(2,128)(2,1)} collective-permute-done((bf16[1,960]{1,0:T(2,128)(2,1)}, bf16[1,960]{1,0:T(2,128)(2,1)}, u32[]{:S(2)}, u32[]{:S(2)}) %collective-permute-start.11) | collective-permute-done | bytes 1952 | tf_op jit(solution)/shard_map/ppermute | solution.py:722
  251.1 12.0 %shard_map.520 = (bf16[896,768]{1,0:T(8,128)(2,1)}, bf16[896,768]{1,0:T(8,128)(2,1)}, bf16[896,768]{1,0:T(8,128)(2,1)}, bf16[896,768]{1,0:T(8,128)(2,1)}, bf16[896,768]{1,0:T(8,128)(2,1)}, /*index=5*/f32[8,768]{1,0:T(8,128)}) custom-call(s32[1]{0:T(128)} %bitcast.1.expert_ref, bf16[16,56,768]{2,1,0:T(8,128)(2,1)} %copy-done.11, ...), custom_call_target="tpu_custom_call" | custom-call | tf_op jit(solution)/shard_map/pallas_call | solution.py:800
  263.1 12.8 %shard_map.521 = (bf16[16,2,56,768]{3,2,1,0:T(8,128)(2,1)}, bf16[896,768]{1,0:T(8,128)(2,1)}, bf16[896,768]{1,0:T(8,128)(2,1)}, f32[8,1536]{1,0:T(8,128)}) custom-call(bf16[896,768]{1,0:T(8,128)(2,1)} %get-tuple-element.103.hidden_own_ref, bf16[896,768]{1,0:T(8,128)(2,1)} %get-tuple-element.104.hidden_peer_ref, ...), custom_call_target="tpu_custom_call" | custom-call | tf_op jit(solution)/shard_map/pallas_call | solution.py:823
  280.1 12.0 %shard_map.518 = (bf16[896,768]{1,0:T(8,128)(2,1)}, bf16[896,768]{1,0:T(8,128)(2,1)}, bf16[896,768]{1,0:T(8,128)(2,1)}, bf16[896,768]{1,0:T(8,128)(2,1)}, bf16[896,768]{1,0:T(8,128)(2,1)}, /*index=5*/f32[8,768]{1,0:T(8,128)}) custom-call(s32[1]{0:T(128)} %bitcast.1.expert_ref, bf16[16,56,768]{2,1,0:T(8,128)(2,1)} %all-to-all-done.rows_ref, ...), custom_call_target="tpu_custom_call" | custom-call | tf_op jit(solution)/shard_map/pallas_call | solution.py:800
  292.1 12.8 %shard_map.519 = (bf16[16,2,56,768]{3,2,1,0:T(8,128)(2,1)}, bf16[896,768]{1,0:T(8,128)(2,1)}, bf16[896,768]{1,0:T(8,128)(2,1)}, f32[8,1536]{1,0:T(8,128)}) custom-call(bf16[896,768]{1,0:T(8,128)(2,1)} %get-tuple-element.92.hidden_own_ref, bf16[896,768]{1,0:T(8,128)(2,1)} %get-tuple-element.93.hidden_peer_ref, ...), custom_call_target="tpu_custom_call" | custom-call | tf_op jit(solution)/shard_map/pallas_call | solution.py:823
  304.9 10.7 %all-to-all-done.4 = bf16[16,2,56,768]{3,2,1,0:T(8,128)(2,1)S(1)} async-done(((bf16[16,2,56,768]{3,2,1,0:T(8,128)(2,1)}), bf16[16,2,56,768]{3,2,1,0:T(8,128)(2,1)S(1)}, u32[]{:S(2)}, u32[]{:S(2)}) %all-to-all-start.4) | async-done | bytes 2752544 | tf_op jit(solution)/shard_map/all_to_all | solution.py:719
  317.1 5.4 all-to-all-start.2
  339.3 15.8 %shard_map.522 = (bf16[2,1,196,768]{3,2,1,0:T(8,128)(2,1)}, f32[2,1,196,768]{3,2,1,0:T(8,128)}, bf16[196,768]{1,0:T(8,128)(2,1)}, bf16[196,2304]{1,0:T(8,128)(2,...) custom-call(bf16[2,1,196,768]{3,2,1,0:T(8,128)(2,1)} %copy.128.x_ref, ...), custom_call_target="tpu_custom_call" | custom-call | tf_op jit(solution)/shard_map/pallas_call | solution.py:889
  355.1 23.3 %all-to-all-done.2 = bf16[16,2,56,768]{3,2,1,0:T(8,128)(2,1)} async-done(((bf16[16,2,56,768]{3,2,1,0:T(8,128)(2,1)}), bf16[16,2,56,768]{3,2,1,0:T(8,128)(2,1)}, u32[]{:S(2)}, u32[]{:S(2)}) %all-to-all-start.2) | async-done | bytes 2752544 | tf_op jit(solution)/shard_map/all_to_all | solution.py:719
  378.4 15.4 %shard_map.523 = (bf16[2,1,196,768]{3,2,1,0:T(8,128)(2,1)}, f32[2,1,196,768]{3,2,1,0:T(8,128)}, bf16[196,768]{1,0:T(8,128)(2,1)}, bf16[196,2304]{1,0:T(8,128)(2,...) custom-call(bf16[2,1,196,768]{3,2,1,0:T(8,128)(2,1)} %copy.128.x_ref, ...), custom_call_target="tpu_custom_call", output_to_operand_aliasing={{0}: (9, {}), {1}: (10, {})} | custom-call | tf_op jit(solution)/shard_map/pallas_call | solution.py:889
  393.8 8.2 %shard_map.524 = (f32[4,96,3200]{2,1,0:T(8,128)}, bf16[4,96,3200]{2,1,0:T(8,128)(2,1)}) custom-call(s32[1]{0:T(128)} %bitcast.28.core_ref, bf16[2,196,768]{2,1,0:T(8,128)(2,1)} %get-tuple-element.100.mixed_ref, bf16[196,768]{1,0:T(8,128)(2,1)} %get-tuple-element.113.refs_0_, bf16[196,2304]{1,0:T(8,128)(2,1)} %get-tuple-element.114.refs_1_, ...), custom_call_target="tpu_custom_call" | custom-call | tf_op jit(solution)/shard_map/pallas_call | solution.py:914
  420.8 7.4 %collective-permute-done.16 = bf16[1,2,24,3200]{3,2,1,0:T(8,128)(2,1)S(1)} collective-permute-done((bf16[1,2,24,3200]{3,2,1,0:T(8,128)(2,1)S(1)}, bf16[1,2,24,3200]{3,2,1,0:T(8,128)(2,1)S(1)}, u32[]{:S(2)}, u32[]{:S(2)}) %collective-permute-start.16) | collective-permute-done | bytes 307232 | tf_op jit(solution)/shard_map/ppermute | solution.py:551
  433.4 27.0 %collective-permute-done.22 = f32[1,960]{1,0:T(1,128)S(1)} collective-permute-done((f32[1,960]{1,0:T(1,128)S(1)}, f32[1,960]{1,0:T(1,128)S(1)}, u32[]{:S(2)}, u32[]{:S(2)}) %collective-permute-start.22) | collective-permute-done | bytes 3872 | tf_op jit(solution)/shard_map/ppermute | solution.py:722
  464.8 11.6 %collective-permute-done.18 = bf16[2,24,3200]{2,1,0:T(8,128)(2,1)} collective-permute-done((bf16[2,24,3200]{2,1,0:T(8,128)(2,1)}, bf16[2,24,3200]{2,1,0:T(8,128)(2,1)}, u32[]{:S(2)}, u32[]{:S(2)}) %collective-permute-start.18) | collective-permute-done | bytes 307232 | tf_op jit(solution)/shard_map/ppermute | solution.py:551
  483.6 16.3 %shard_map.525 = (f32[1,768,768]{2,1,0:T(8,128)}, f32[1,768,768]{2,1,0:T(8,128)}, f32[1,768,768]{2,1,0:T(8,128)}, bf16[1,768,768]{2,1,0:T(8,128)(2,1)}, f32[1,2,...) custom-call(f32[768,768]{1,0:T(8,128)} %convolution_add_fusion.1.own_ref, bf16[768,768]{1,0:T(8,128)(2,1)} %collective-permute-done.20.other_ref, ...), custom_call_target="tpu_custom_call" | custom-call | tf_op jit(solution)/shard_map/pallas_call | solution.py:653
  501.1 29.9 %shard_map.526 = f32[2,384,384]{2,1,0:T(8,128)} custom-call(f32[2,384,384]{2,1,0:T(8,128)S(1)} %copy-done), custom_call_target="tpu_custom_call" | custom-call | tf_op jit(solution)/shard_map/pallas_call | solution.py:158
  531.0 15.8 %shard_map.527 = (f32[1,768,768]{2,1,0:T(8,128)}, f32[1,768,768]{2,1,0:T(8,128)}, f32[1,768,768]{2,1,0:T(8,128)}, bf16[1,768,768]{2,1,0:T(8,128)(2,1)}, f32[1,2,...) custom-call(f32[768,768]{1,0:T(8,128)} %convolution_add_fusion.own_ref, bf16[768,768]{1,0:T(8,128)(2,1)} %collective-permute-done.21.other_ref, ...), custom_call_target="tpu_custom_call" | custom-call | tf_op jit(solution)/shard_map/pallas_call | solution.py:653
  548.1 29.9 %shard_map.528 = f32[2,384,384]{2,1,0:T(8,128)} custom-call(f32[2,384,384]{2,1,0:T(8,128)S(1)} %copy-done.1), custom_call_target="tpu_custom_call" | custom-call | tf_op jit(solution)/shard_map/pallas_call | solution.py:158
  (226 shorter events, 139.9 us)
Async XLA Ops:
  3.3 7.0 %collective-permute-start = (bf16[1,24,3200]{2,1,0:T(8,128)(2,1)S(1)}, bf16[1,24,3200]{2,1,0:T(8,128)(2,1)S(1)}, u32[]{:S(2)}, u32[]{:S(2)}) collective-permute-start(bf16[1,24,3200]{2,1,0:T(8,128)(2,1)S(1)} %bitcast.101), channel_id=1, source_target_pairs={{0,1},{1,0},{2,3},{3,2},{4,5},{5,4},{6,7},{7,6},{8,9},{9,8},{10,11... | collective-permute-start | bytes 460808 | tf_op jit(solution)/shard_map/ppermute | solution.py:551
  10.5 16.0 %collective-permute-start.1 = (bf16[2,24,3200]{2,1,0:T(8,128)(2,1)S(1)}, bf16[2,24,3200]{2,1,0:T(8,128)(2,1)S(1)}, u32[]{:S(2)}, u32[]{:S(2)}) collective-permute-start(bf16[2,24,3200]{2,1,0:T(8,128)(2,1)S(1)} %maximum_select_fusion.9), channel_id=1, source_target_pairs={{0,2},{1,3},{2,0},{3,1},{4,6},{5,7},{6,4},{7,5},{8,10},{9,11},{10,... | collective-permute-start | bytes 921608 | tf_op jit(solution)/shard_map/ppermute | solution.py:551
  26.6 14.9 %collective-permute-start.3 = (bf16[1,4,24,3200]{3,2,1,0:T(8,128)(2,1)S(1)}, bf16[1,4,24,3200]{3,2,1,0:T(8,128)(2,1)S(1)}, u32[]{:S(2)}, u32[]{:S(2)}) collective-permute-start(bf16[1,4,24,3200]{3,2,1,0:T(8,128)(2,1)S(1)} %bitcast.97), channel_id=1, source_target_pairs={{0,16},{4,20},{8,24},{12,28},{16,0},{20,4},{24,8},{28,12},{1,17},{... | collective-permute-start | bytes 1843208 | tf_op jit(solution)/shard_map/ppermute | solution.py:551
  28.0 14.8 %collective-permute-start.2 = (bf16[1,4,24,3200]{3,2,1,0:T(8,128)(2,1)S(1)}, bf16[1,4,24,3200]{3,2,1,0:T(8,128)(2,1)S(1)}, u32[]{:S(2)}, u32[]{:S(2)}) collective-permute-start(bf16[1,4,24,3200]{3,2,1,0:T(8,128)(2,1)S(1)} %bitcast.98), channel_id=1, source_target_pairs={{0,8},{4,12},{8,0},{12,4},{16,24},{20,28},{24,16},{28,20},{1,9},{5... | collective-permute-start | bytes 1843208 | tf_op jit(solution)/shard_map/ppermute | solution.py:551
  30.6 19.9 %collective-permute-start.6 = (bf16[1,4,24,3200]{3,2,1,0:T(8,128)(2,1)S(1)}, bf16[1,4,24,3200]{3,2,1,0:T(8,128)(2,1)S(1)}, u32[]{:S(2)}, u32[]{:S(2)}) collective-permute-start(bf16[1,4,24,3200]{3,2,1,0:T(8,128)(2,1)S(1)} %bitcast.99), channel_id=1, source_target_pairs={{0,4},{4,0},{8,12},{12,8},{16,20},{20,16},{24,28},{28,24},{1,5},{5... | collective-permute-start | bytes 1843208 | tf_op jit(solution)/shard_map/ppermute | solution.py:551
  41.5 7.5 %collective-permute-start.4 = (bf16[1,2,24,3200]{3,2,1,0:T(8,128)(2,1)S(1)}, bf16[1,2,24,3200]{3,2,1,0:T(8,128)(2,1)S(1)}, u32[]{:S(2)}, u32[]{:S(2)}) collective-permute-start(bf16[1,2,24,3200]{3,2,1,0:T(8,128)(2,1)S(1)} %slice.96), channel_id=1, source_target_pairs={{0,8},{4,12},{8,0},{12,4},{16,24},{20,28},{24,16},{28,20},{1,9},{5... | collective-permute-start | bytes 921608 | tf_op jit(solution)/shard_map/ppermute | solution.py:551
  42.8 7.0 %collective-permute-start.5 = (bf16[1,2,24,3200]{3,2,1,0:T(8,128)(2,1)S(1)}, bf16[1,2,24,3200]{3,2,1,0:T(8,128)(2,1)S(1)}, u32[]{:S(2)}, u32[]{:S(2)}) collective-permute-start(bf16[1,2,24,3200]{3,2,1,0:T(8,128)(2,1)S(1)} %slice.97), channel_id=1, source_target_pairs={{0,16},{4,20},{8,24},{12,28},{16,0},{20,4},{24,8},{28,12},{1,17},{... | collective-permute-start | bytes 921608 | tf_op jit(solution)/shard_map/ppermute | solution.py:551
  70.5 24.3 %all-to-all-start.3 = ((bf16[16,56,768]{2,1,0:T(8,128)(2,1)}), bf16[16,56,768]{2,1,0:T(8,128)(2,1)S(1)}, u32[]{:S(2)}, u32[]{:S(2)}) async-start(bf16[16,56,768]{2,1,0:T(8,128)(2,1)} %bitcast.25), calls=%async_computation.3 | async-start | bytes 2752512 | tf_op jit(solution)/shard_map/all_to_all | solution.py:719
  133.1 142.8 %all-to-all-start = ((bf16[16,56,768]{2,1,0:T(8,128)(2,1)}), bf16[16,56,768]{2,1,0:T(8,128)(2,1)}, u32[]{:S(2)}, u32[]{:S(2)}) async-start(bf16[16,56,768]{2,1,0:T(8,128)(2,1)} %bitcast.20), calls=%async_computation | async-start | bytes 2752512 | tf_op jit(solution)/shard_map/all_to_all | solution.py:719
  140.6 109.4 %collective-permute-start.10 = (bf16[768,768]{1,0:T(8,128)(2,1)S(1)}, bf16[768,768]{1,0:T(8,128)(2,1)S(1)}, u32[]{:S(2)}, u32[]{:S(2)}) collective-permute-start(bf16[768,768]{1,0:T(8,128)(2,1)S(1)} %get-tuple-element.91.own_ref.in_own_ref), channel_id=1, source_target_pairs={{0,2},{1,3},{2,0},{3,1},{4,6},{5,7},{6,4},{7,5},{8,10},{9,11},{10,... | collective-permute-start | bytes 3538952 | tf_op jit(solution)/shard_map/ppermute | solution.py:722
  144.1 119.0 %collective-permute-start.12 = (bf16[768,768]{1,0:T(8,128)(2,1)S(1)}, bf16[768,768]{1,0:T(8,128)(2,1)}, u32[]{:S(2)}, u32[]{:S(2)}) collective-permute-start(bf16[768,768]{1,0:T(8,128)(2,1)S(1)} %get-tuple-element.97.out_own_ref), channel_id=1, source_target_pairs={{0,2},{1,3},{2,0},{3,1},{4,6},{5,7},{6,4},{7,5},{8,10},{9,11},{10,... | collective-permute-start | bytes 3538952 | tf_op jit(solution)/shard_map/ppermute | solution.py:722
  145.4 101.4 %collective-permute-start.11 = (bf16[1,960]{1,0:T(2,128)(2,1)}, bf16[1,960]{1,0:T(2,128)(2,1)}, u32[]{:S(2)}, u32[]{:S(2)}) collective-permute-start(bf16[1,960]{1,0:T(2,128)(2,1)} %pad_maximum_fusion.2), channel_id=1, source_target_pairs={{0,2},{1,3},{2,0},{3,1},{4,6},{5,7},{6,4},{7,5},{8,10},{9,11},{10,... | collective-permute-start | bytes 5768 | tf_op jit(solution)/shard_map/ppermute | solution.py:722
  275.9 39.6 %all-to-all-start.4 = ((bf16[16,2,56,768]{3,2,1,0:T(8,128)(2,1)}), bf16[16,2,56,768]{3,2,1,0:T(8,128)(2,1)S(1)}, u32[]{:S(2)}, u32[]{:S(2)}) async-start(bf16[16,2,56,768]{3,2,1,0:T(8,128)(2,1)} %get-tuple-element.108), calls=%async_computation.4 | async-start | bytes 5505024 | tf_op jit(solution)/shard_map/all_to_all | solution.py:719
  317.1 61.3 %all-to-all-start.2 = ((bf16[16,2,56,768]{3,2,1,0:T(8,128)(2,1)}), bf16[16,2,56,768]{3,2,1,0:T(8,128)(2,1)}, u32[]{:S(2)}, u32[]{:S(2)}) async-start(bf16[16,2,56,768]{3,2,1,0:T(8,128)(2,1)} %get-tuple-element.98), calls=%async_computation.2 | async-start | bytes 5505024 | tf_op jit(solution)/shard_map/all_to_all | solution.py:719
  333.0 150.6 %collective-permute-start.20 = (bf16[768,768]{1,0:T(8,128)(2,1)}, bf16[768,768]{1,0:T(8,128)(2,1)}, u32[]{:S(2)}, u32[]{:S(2)}) collective-permute-start(bf16[768,768]{1,0:T(8,128)(2,1)} %add_convert_fusion.1), channel_id=1, source_target_pairs={{0,2},{1,3},{2,0},{3,1},{4,6},{5,7},{6,4},{7,5},{8,10},{9,11},{10,... | collective-permute-start | bytes 3538952 | tf_op jit(solution)/shard_map/ppermute | solution.py:722
  402.1 16.6 %collective-permute-start.13 = (bf16[4,96,3200]{2,1,0:T(8,128)(2,1)}, bf16[4,96,3200]{2,1,0:T(8,128)(2,1)S(1)}, u32[]{:S(2)}, u32[]{:S(2)}) collective-permute-start(bf16[4,96,3200]{2,1,0:T(8,128)(2,1)} %get-tuple-element.126), channel_id=1, source_target_pairs={{0,4},{4,0},{8,12},{12,8},{16,20},{20,16},{24,28},{28,24},{1,5},{5... | collective-permute-start | bytes 7372808 | tf_op jit(solution)/shard_map/ppermute | solution.py:551
  406.6 124.5 %collective-permute-start.21 = (bf16[768,768]{1,0:T(8,128)(2,1)}, bf16[768,768]{1,0:T(8,128)(2,1)}, u32[]{:S(2)}, u32[]{:S(2)}) collective-permute-start(bf16[768,768]{1,0:T(8,128)(2,1)} %add_convert_fusion), channel_id=1, source_target_pairs={{0,2},{1,3},{2,0},{3,1},{4,6},{5,7},{6,4},{7,5},{8,10},{9,11},{10,... | collective-permute-start | bytes 3538952 | tf_op jit(solution)/shard_map/ppermute | solution.py:722
  408.3 52.1 %collective-permute-start.22 = (f32[1,960]{1,0:T(1,128)S(1)}, f32[1,960]{1,0:T(1,128)S(1)}, u32[]{:S(2)}, u32[]{:S(2)}) collective-permute-start(f32[1,960]{1,0:T(1,128)S(1)} %pad_maximum_fusion.3), channel_id=1, source_target_pairs={{0,2},{1,3},{2,0},{3,1},{4,6},{5,7},{6,4},{7,5},{8,10},{9,11},{10,... | collective-permute-start | bytes 11528 | tf_op jit(solution)/shard_map/ppermute | solution.py:722
  419.2 9.0 %collective-permute-start.16 = (bf16[1,2,24,3200]{3,2,1,0:T(8,128)(2,1)S(1)}, bf16[1,2,24,3200]{3,2,1,0:T(8,128)(2,1)S(1)}, u32[]{:S(2)}, u32[]{:S(2)}) collective-permute-start(bf16[1,2,24,3200]{3,2,1,0:T(8,128)(2,1)S(1)} %get-tuple-element.262), channel_id=1, source_target_pairs={{0,8},{4,12},{8,0},{12,4},{16,24},{20,28},{24,16},{28,20},{1,9},{5... | collective-permute-start | bytes 921608 | tf_op jit(solution)/shard_map/ppermute | solution.py:551
  419.5 10.2 %collective-permute-start.14 = (bf16[1,2,24,3200]{3,2,1,0:T(8,128)(2,1)S(1)}, bf16[1,2,24,3200]{3,2,1,0:T(8,128)(2,1)S(1)}, u32[]{:S(2)}, u32[]{:S(2)}) collective-permute-start(bf16[1,2,24,3200]{3,2,1,0:T(8,128)(2,1)S(1)} %get-tuple-element.261), channel_id=1, source_target_pairs={{0,16},{4,20},{8,24},{12,28},{16,0},{20,4},{24,8},{28,12},{1,17},{... | collective-permute-start | bytes 921608 | tf_op jit(solution)/shard_map/ppermute | solution.py:551
  428.4 32.6 %collective-permute-start.17 = (bf16[1,4,24,3200]{3,2,1,0:T(8,128)(2,1)S(1)}, bf16[1,4,24,3200]{3,2,1,0:T(8,128)(2,1)S(1)}, u32[]{:S(2)}, u32[]{:S(2)}) collective-permute-start(bf16[1,4,24,3200]{3,2,1,0:T(8,128)(2,1)S(1)} %pad_maximum_fusion.1), channel_id=1, source_target_pairs={{0,16},{4,20},{8,24},{12,28},{16,0},{20,4},{24,8},{28,12},{1,17},{... | collective-permute-start | bytes 1843208 | tf_op jit(solution)/shard_map/ppermute | solution.py:551
  429.8 31.2 %collective-permute-start.15 = (bf16[1,4,24,3200]{3,2,1,0:T(8,128)(2,1)S(1)}, bf16[1,4,24,3200]{3,2,1,0:T(8,128)(2,1)S(1)}, u32[]{:S(2)}, u32[]{:S(2)}) collective-permute-start(bf16[1,4,24,3200]{3,2,1,0:T(8,128)(2,1)S(1)} %pad_maximum_fusion), channel_id=1, source_target_pairs={{0,8},{4,12},{8,0},{12,4},{16,24},{20,28},{24,16},{28,20},{1,9},{5... | collective-permute-start | bytes 1843208 | tf_op jit(solution)/shard_map/ppermute | solution.py:551
  462.0 14.4 %collective-permute-start.18 = (bf16[2,24,3200]{2,1,0:T(8,128)(2,1)}, bf16[2,24,3200]{2,1,0:T(8,128)(2,1)}, u32[]{:S(2)}, u32[]{:S(2)}) collective-permute-start(bf16[2,24,3200]{2,1,0:T(8,128)(2,1)} %fusion.5), channel_id=1, source_target_pairs={{0,2},{1,3},{2,0},{3,1},{4,6},{5,7},{6,4},{7,5},{8,10},{9,11},{10,... | collective-permute-start | bytes 921608 | tf_op jit(solution)/shard_map/ppermute | solution.py:551
  482.6 98.9 %collective-permute-start.19 = (bf16[1,24,3200]{2,1,0:T(8,128)(2,1)S(1)}, bf16[1,24,3200]{2,1,0:T(8,128)(2,1)}, u32[]{:S(2)}, u32[]{:S(2)}) collective-permute-start(bf16[1,24,3200]{2,1,0:T(8,128)(2,1)S(1)} %copy.133), channel_id=1, source_target_pairs={{0,1},{1,0},{2,3},{3,2},{4,5},{5,4},{6,7},{7,6},{8,9},{9,8},{10,11... | collective-permute-start | bytes 460808 | tf_op jit(solution)/shard_map/ppermute | solution.py:551
  (50 other events, 580.2 us)
where the time goes:
time: 607 us; the launch traced here: 599 us
  waiting for transfers between devices  224 us (37%)
  Pallas kernels  196 us (32%)
  starting transfers between devices  48.4 us (8%)
  local copies, waits for them, and re-layouts  40.5 us (7%)
  blocking collectives  38.3 us (6%)
  other arithmetic  27.8 us (5%)
  matrix products  22.8 us (4%)
    ppermute x6, waiting for transfers between devices, across(): return lax.ppermute(values, TENSOR, partner)  125 us
    pallas_call x2, Pallas kernels, renew(): pl.pallas_call(renew_kernel, out_shape=jax.ShapeDtypeStruct(z.shape, z.dt...  59.8 us
    ppermute x17, waiting for transfers between devices, swap(): return lax.ppermute(values, axis, [(i, i ^ distance) for i in range(size)])  50.6 us
    all_to_all x4, waiting for transfers between devices, exchange(): lax.all_to_all(values, BOTH, 0, 0, axis_index_groups=groups, tiled=True)  48.5 us
    all_to_all x1, blocking collectives, exchange(): lax.all_to_all(values, BOTH, 0, 0, axis_index_groups=groups, tiled=True)  38.3 us
    pallas_call x2, Pallas kernels, soap(): vmem_call(partial(turn_kernel, along_rows, rate), grid=(blocks,), in_spec...  32 us
    pallas_call x2, Pallas kernels, per_device(): vmem_call(partial(attention_backward_kernel, expert_total), grid=(1,), in...  31.2 us
    pallas_call x2, Pallas kernels, per_device(): vmem_call(result_kernel, grid=(tiles,), in_specs=[rows_of(units)] * 4 + [...  25.6 us
  transfers between devices with their start and end apart: 27, of which 13 were waited for; matrix products, arithmetic and copies ran while one was open for 9% of the time, Pallas kernels for 31%

commit v1 on v0

--- a/solution.py
+++ b/solution.py
@@ -64,6 +64,8 @@
 TENSOR = "tensor"
 BOTH = (EXPERT, TENSOR)
 VMEM_LIMIT = 56 * 2**20
+FLOPS_PER_US = 1.1e9
+ROW_TILE = 512
 SUB = 64
 
 
@@ -129,10 +131,15 @@
                     for k in range(1,8): acc=acc+c[k]*wv[k]
                     tiles[t]=tiles[t]-acc
     return [jnp.concatenate(o,axis=0) for o in outs]
-def renew_kernel(z_ref,q_ref,m_ref):
-    nb=z_ref.shape[0]; n=z_ref.shape[1]; kb=n//128; h=SUB
+def renew_kernel(skipped, *refs):
+    refs=refs[skipped:]
+    m_ref=refs[-1]
+    zs=refs[:-2]
+    nb=len(zs)
+    qs=[refs[-2].at[0,i] for i in range(nb)]
+    n=BLK; kb=n//128; h=SUB
     for b in range(nb):
-        z=z_ref[b]
+        z=zs[b][...]
         m_ref[b]=tm(z,z)
     for k in range(kb):
         o=128*k; sl=slice(o,o+128)
@@ -146,19 +153,26 @@
             low=-mm(mm(i2[b],l21[b]),i1[b])
             inv.append(jnp.concatenate([jnp.concatenate([i1[b],jnp.zeros((h,h),jnp.float32)],1),jnp.concatenate([low,i2[b]],1)],0))
         for b in range(nb):
-            q=z_ref[b,:,sl]
+            q=zs[b][:,sl]
             for j in range(k):
-                q=q-mt(q_ref[b,:,128*j:128*j+128],m_ref[b,sl,128*j:128*j+128])
-            q_ref[b,:,sl]=mt(q,inv[b])
+                q=q-mt(qs[b][:,128*j:128*j+128],m_ref[b,sl,128*j:128*j+128])
+            qs[b][:,sl]=mt(q,inv[b])
             if k+1<kb:
                 p=mt(m_ref[b,o+128:,sl],inv[b])
                 m_ref[b,o+128:,sl]=p
                 m_ref[b,o+128:,o+128:]=m_ref[b,o+128:,o+128:]-mt(p,p)
-def renew(z):
-    return pl.pallas_call(renew_kernel,out_shape=jax.ShapeDtypeStruct(z.shape,z.dtype),
-      in_specs=[pl.BlockSpec(memory_space=pltpu.VMEM)],out_specs=pl.BlockSpec(memory_space=pltpu.VMEM),
-      scratch_shapes=[pltpu.VMEM(z.shape,jnp.float32)],
-      compiler_params=pltpu.CompilerParams(vmem_limit_bytes=32*2**20))(z)
+def renew(tokens, stretched):
+    count=len(stretched)
+    return vmem_call(
+        partial(renew_kernel, len(tokens)),
+        30,
+        grid=(1,),
+        out_shape=jax.ShapeDtypeStruct((1, count, BLK, BLK), jnp.float32),
+        in_specs=[pl.BlockSpec(memory_space=pl.ANY)] * len(tokens)
+        + [full_block((BLK, BLK))] * count,
+        out_specs=full_block((1, count, BLK, BLK)),
+        scratch_shapes=[pltpu.VMEM((count, BLK, BLK), jnp.float32)],
+    )(*tokens, *stretched)
 
 
 def low(values):
@@ -173,9 +187,15 @@
     return jnp.dot(left, right, preferred_element_type=jnp.float32)
 
 
-def vmem_call(kernel, **options):
+def vmem_call(kernel, microseconds, **options):
+    cost = pl.CostEstimate(
+        flops=int(microseconds * FLOPS_PER_US), bytes_accessed=0, transcendentals=0
+    )
     return pl.pallas_call(
-        kernel, compiler_params=pltpu.CompilerParams(vmem_limit_bytes=VMEM_LIMIT), **options
+        kernel,
+        compiler_params=pltpu.CompilerParams(vmem_limit_bytes=VMEM_LIMIT),
+        cost_estimate=cost,
+        **options,
     )
 
 
@@ -227,10 +247,10 @@
             out_ref[:, copy, step] = rows
 
 
-def attention_kernel(
-    experts, x_ref, target_ref, a_ref, out_ref, qkv_ref, mixed_ref, middle_ref, probs_ref
-):
-    copies, padded = (out_ref.shape[2], out_ref.shape[3])
+def attention_kernel(experts, x_ref, target_ref, a_ref, *refs):
+    out_refs = refs[:MB]
+    qkv_ref, mixed_ref, middle_ref, probs_ref, score_ref, weight_ref = refs[MB:]
+    copies, padded = out_refs[0].shape[1:3]
     inputs = wide(x_ref[0, 0])
     extra = a_ref[:, 4 * D :]
     vectors = wide(extra).T
@@ -239,16 +259,17 @@
     normed_low = low(normed * gains[0] + gains[1])
     qkv_ref[0] = low(dot(normed_low, a_ref[:, : 3 * D]))
     lanes = lax.broadcasted_iota(jnp.int32, (SEQ, 2 * HEAD_DIM), 1)
+    for head in range(HEADS):
+        start = 2 * HEAD_DIM * (head // 2)
+        query = qkv_ref[0, :, start : start + 2 * HEAD_DIM]
+        keys = qkv_ref[0, :, D + start : D + start + 2 * HEAD_DIM]
+        here = (lanes < HEAD_DIM) if head % 2 == 0 else (lanes >= HEAD_DIM)
+        score_ref[head] = row_product(jnp.where(here, query, 0), keys) * HEAD_DIM ** (-0.5)
+    weight_ref[...] = low(softmax_rows(score_ref[...]))
     for pair in range(HEADS // 2):
         start = 2 * HEAD_DIM * pair
-        query = qkv_ref[0, :, start : start + 2 * HEAD_DIM]
-        keys = qkv_ref[0, :, D + start : D + start + 2 * HEAD_DIM]
         values = qkv_ref[0, :, 2 * D + start : 2 * D + start + 2 * HEAD_DIM]
-        both = []
-        for side in range(2):
-            here = (lanes < HEAD_DIM) if side == 0 else (lanes >= HEAD_DIM)
-            scores = row_product(jnp.where(here, query, 0), keys) * HEAD_DIM ** (-0.5)
-            both.append(dot(low(softmax_rows(scores)), values))
+        both = [dot(weight_ref[2 * pair + side], values) for side in range(2)]
         mixed_ref[0, :, start : start + 2 * HEAD_DIM] = low(
             jnp.where(lanes < HEAD_DIM, both[0], both[1])
         )
@@ -259,24 +280,21 @@
     probs_ref[0] = masked_softmax(dot(moe_low, extra), experts)
     routing = low(route_mask(target_ref[0], experts * padded))
     rows = low(column_sum(routing, moe_low).reshape(experts, padded, D))
-    for copy in range(copies):
-        out_ref[0, :, copy] = rows
-
-
-def attention_backward_kernel(
-    experts,
-    x_ref,
-    up_ref,
-    target_ref,
-    back_ref,
-    qkv_ref,
-    mixed_ref,
-    middle_ref,
-    probs_ref,
-    a_ref,
-    *refs,
-):
-    out_ref, grad_ref, normed_ref, joined_ref, branch_ref, moe_ref, logit_ref, vector_ref = refs[-8:]
+    for step, out_ref in enumerate(out_refs):
+
+        @pl.when(pl.program_id(0) == step)
+        def _(out_ref=out_ref):
+            for copy in range(copies):
+                out_ref[:, copy] = rows
+
+
+def attention_backward_kernel(experts, skipped, *refs):
+    refs = refs[skipped:]
+    x_ref, up_ref, target_ref, back_ref, qkv_ref, mixed_ref, middle_ref, probs_ref, a_ref = refs[:9]
+    score_ref, slope_ref, weight_ref, grad_score_ref = refs[-4:]
+    out_ref, grad_ref, normed_ref, joined_ref, branch_ref, moe_ref, logit_ref, vector_ref = refs[
+        -12:-4
+    ]
     copies, padded = (back_ref.shape[1], back_ref.shape[3])
     slot_total = experts * padded
     extra = a_ref[:, 4 * D :]
@@ -328,28 +346,35 @@
     branch_ref[...] = branch_low
     grad_mixed = low(row_product(branch_low, a_ref[:, 3 * D : 4 * D]))
     lanes = lax.broadcasted_iota(jnp.int32, (SEQ, 2 * HEAD_DIM), 1)
+    for head in range(HEADS):
+        start = 2 * HEAD_DIM * (head // 2)
+        stop = start + 2 * HEAD_DIM
+        query = qkv_ref[0, :, start:stop]
+        keys = qkv_ref[0, :, D + start : D + stop]
+        values = qkv_ref[0, :, 2 * D + start : 2 * D + stop]
+        here = (lanes < HEAD_DIM) if head % 2 == 0 else (lanes >= HEAD_DIM)
+        score_ref[head] = row_product(jnp.where(here, query, 0), keys) * HEAD_DIM ** (-0.5)
+        slope_ref[head] = row_product(jnp.where(here, grad_mixed[:, start:stop], 0), values)
+    weights = softmax_rows(score_ref[...])
+    weight_ref[...] = low(weights)
+    slopes = slope_ref[...]
+    grad_score_ref[...] = low(
+        weights * (slopes - jnp.sum(slopes * weights, axis=-1, keepdims=True))
+    )
     for pair in range(HEADS // 2):
         start = 2 * HEAD_DIM * pair
         stop = start + 2 * HEAD_DIM
         query = qkv_ref[0, :, start:stop]
         keys = qkv_ref[0, :, D + start : D + stop]
-        values = qkv_ref[0, :, 2 * D + start : 2 * D + stop]
         grad_here = grad_mixed[:, start:stop]
         results = []
         for side in range(2):
-            here = (lanes < HEAD_DIM) if side == 0 else (lanes >= HEAD_DIM)
-            scores = row_product(jnp.where(here, query, 0), keys) * HEAD_DIM ** (-0.5)
-            weights = softmax_rows(scores)
-            grad_probs = row_product(jnp.where(here, grad_here, 0), values)
-            grad_scores = low(
-                weights
-                * (grad_probs - jnp.sum(grad_probs * weights, axis=-1, keepdims=True))
-            )
+            grad_scores = grad_score_ref[2 * pair + side]
             results.append(
                 (
                     dot(grad_scores, keys) * HEAD_DIM ** (-0.5),
                     column_sum(grad_scores, query) * HEAD_DIM ** (-0.5),
-                    column_sum(low(weights), grad_here),
+                    column_sum(weight_ref[2 * pair + side], grad_here),
                 )
             )
         for part in range(3):
@@ -365,8 +390,9 @@
     grad_ref[0, 0] = grad_middle + norm_backward(grad_normed, normed, scale, gains[0])
 
 
-def weight_sums_kernel(experts, core_ref, mixed_ref, *refs):
-    own_ref, other_ref = refs[-2:]
+def weight_sums_kernel(experts, after_ref, core_ref, mixed_ref, *refs):
+    own_ref, other_ref, token_ref = refs[-3:]
+    token_ref[...] = jnp.zeros_like(token_ref)
     steps = [refs[6 * i : 6 * i + 6] for i in range(MB)]
     held, block, _ = own_ref.shape
     first_core = core_ref[0] == 0
@@ -411,82 +437,63 @@
     rows_ref,
     up_ref,
     router_ref,
-    own_ref,
-    peer_ref,
+    weight_ref,
     bias_ref,
-    hidden_own_ref,
-    hidden_peer_ref,
-    slope_own_ref,
-    slope_peer_ref,
+    hidden_ref,
+    slope_ref,
     grad_ref,
     sum_ref,
 ):
     count, padded = rows_ref.shape[:2]
-    units = own_ref.shape[1]
+    units = weight_ref.shape[2]
     rows = low(wide(rows_ref[...]).reshape(count * padded, D))
     probs = masked_softmax(dot(rows, router_ref[...]), experts)
     lanes = lax.broadcasted_iota(jnp.int32, probs.shape, 1)
     gate = jnp.sum(jnp.where(lanes == expert_ref[0], probs, 0.0), axis=-1, keepdims=True)
     grad = low(gate * wide(up_ref[...]).reshape(count * padded, D))
     grad_ref[...] = grad
-    partial = jnp.sum(wide(grad), axis=0, keepdims=True)
 
     @pl.when(pl.program_id(0) == 0)
     def _():
         sum_ref[...] = jnp.zeros_like(sum_ref)
 
-    sum_ref[0:1] += partial
-    for side, (weight, hidden_ref, slope_ref) in enumerate(
-        ((own_ref, hidden_own_ref, slope_own_ref), (peer_ref, hidden_peer_ref, slope_peer_ref))
-    ):
-        values = dot(rows, weight[...]) + bias_ref[:, side * units : (side + 1) * units]
+    sum_ref[0:1] += jnp.sum(wide(grad), axis=0, keepdims=True)
+    for side in range(2):
+        values = dot(rows, weight_ref[side]) + bias_ref[:, side * units : (side + 1) * units]
         area, density = gelu_parts(values)
-        hidden_ref[...] = low(values * area)
-        slope_ref[...] = low(area + values * density)
-
-
-def result_kernel(
-    hidden_own_ref,
-    hidden_peer_ref,
-    slope_own_ref,
-    slope_peer_ref,
-    grad_ref,
-    out_own_ref,
-    out_peer_ref,
-    in_own_ref,
-    in_peer_ref,
-    bias_ref,
-    back_ref,
-    pre_own_ref,
-    pre_peer_ref,
-    sum_ref,
-):
+        hidden_ref[side] = low(values * area)
+        slope_ref[side] = low(area + values * density)
+
+
+def result_kernel(skipped, *refs):
+    (
+        hidden_ref,
+        slope_ref,
+        grad_ref,
+        out_ref,
+        in_ref,
+        bias_ref,
+        back_ref,
+        pre_ref,
+        sum_ref,
+    ) = refs[skipped:]
     count, _, padded, _ = back_ref.shape
-    units = in_own_ref.shape[1]
+    units = in_ref.shape[2]
 
     @pl.when(pl.program_id(0) == 0)
     def _():
         sum_ref[...] = jnp.zeros_like(sum_ref)
 
-    out_term = (
-        dot(hidden_own_ref[...], out_own_ref[...])
-        + dot(hidden_peer_ref[...], out_peer_ref[...])
-        + bias_ref[...]
-    )
+    out_term = dot(hidden_ref[0], out_ref[0]) + dot(hidden_ref[1], out_ref[1]) + bias_ref[...]
     back_ref[:, 0] = low(out_term.reshape(count, padded, D))
     grad_term = None
-    for side, (slope, out_weight, in_weight, pre_ref) in enumerate(
-        (
-            (slope_own_ref, out_own_ref, in_own_ref, pre_own_ref),
-            (slope_peer_ref, out_peer_ref, in_peer_ref, pre_peer_ref),
-        )
-    ):
-        pre = low(row_product(grad_ref[...], out_weight[...]) * wide(slope[...]))
-        pre_ref[...] = pre
+    for side in range(2):
+        pre = low(row_product(grad_ref[...], out_ref[side]) * wide(slope_ref[side]))
+        pre_ref[side] = pre
         sum_ref[0:1, side * units : (side + 1) * units] += jnp.sum(
             wide(pre), axis=0, keepdims=True
         )
-        term = row_product(pre, in_weight[...])
+        term = row_product(pre, in_ref[side])
         grad_term = term if grad_term is None else grad_term + term
     back_ref[:, 1] = low(grad_term.reshape(count, padded, D))
 
@@ -503,32 +510,19 @@
     return one(left[0], right[0]) + (one(left[0], right[1]) + one(left[1], right[0]))
 
 
-def turn_kernel(
-    along_rows,
-    rate,
-    own_ref,
-    other_ref,
-    weight_ref,
-    first_ref,
-    second_ref,
-    stat_ref,
-    basis_ref,
-    first_out,
-    second_out,
-    weight_out,
-    copy_out,
-    stat_out,
-    stretched_out,
-):
-    gradient = own_ref[...] + wide(other_ref[...])
+def turn_kernel(along_rows, rate, skipped, *refs):
+    refs = refs[skipped:]
+    gradient_ref, weight_ref, first_ref, second_ref, stat_ref, basis_ref = refs[:6]
+    first_out, second_out, weight_out, copy_out, stat_out, stretched_out = refs[-6:]
+    gradient = gradient_ref[...]
     basis = basis_ref[0, 0]
-    gradient_parts, basis_parts = (split(gradient), split(basis))
+    basis_parts = split(basis)
     if along_rows:
-        turned = split_dot(basis_parts, gradient_parts, ((0,), (0,)))
-        outer = mt(gradient, gradient)
+        turned = column_sum(basis_parts[0], gradient) + column_sum(basis_parts[1], gradient)
+        outer = row_product(gradient, gradient)
     else:
-        turned = split_dot(gradient_parts, basis_parts, ((1,), (0,)))
-        outer = tm(gradient, gradient)
+        turned = dot(gradient, basis_parts[0]) + dot(gradient, basis_parts[1])
+        outer = column_sum(gradient, gradient)
     first_new, second_new, step = moment_step(turned, first_ref[0], second_ref[0])
     first_out[0] = first_new
     second_out[0] = second_new
@@ -543,7 +537,34 @@
     copy_out[0] = low(weight_new)
     stat_new = STAT_DECAY * stat_ref[0, 0] + (1.0 - STAT_DECAY) * outer
     stat_out[0, 0] = stat_new
-    stretched_out[0] = mm(stat_new, basis)
+    stretched_out[...] = mm(stat_new, basis)
+
+
+def dense_update_kernel(kept_ref, received_ref, *refs):
+    inputs, outputs = (refs[:9], refs[9:])
+    gradient = kept_ref[...] + wide(received_ref[...])
+    extra = gradient[:, 4 * D :]
+    experts = inputs[3].shape[1]
+    gradients = (gradient[:, : 4 * D], extra[:, :experts], extra.T[experts : experts + 4])
+    rates = ((RATE_DENSE, DECAY_RATE), (RATE_DENSE, DECAY_RATE), (RATE_NORMS, 0.0))
+    place = 0
+    for kind in range(3):
+        weight, first, second = (r[...] for r in inputs[3 * kind : 3 * kind + 3])
+        first_new, second_new, weight_new = adam_update(
+            weight, gradients[kind], first, second, *rates[kind]
+        )
+        outputs[place][...] = first_new
+        outputs[place + 1][...] = second_new
+        outputs[place + 2][...] = weight_new
+        place += 3
+        if kind < 2:
+            outputs[place][...] = low(weight_new)
+            place += 1
+
+
+def row_sums_kernel(*refs):
+    total = sum(column_sum(refs[i][...], refs[MB + i][...]) for i in range(MB))
+    refs[-1][...] = low(total)
 
 
 def swap(values, axis, distance):
@@ -551,20 +572,30 @@
     return lax.ppermute(values, axis, [(i, i ^ distance) for i in range(size)])
 
 
+def across(values):
+    size = lax.axis_size(TENSOR)
+    return lax.ppermute(values, TENSOR, [(i, (i + size // 2) % size) for i in range(size)])
+
+
 def ordered(bit, mine, other):
     return jnp.where(bit == 0, jnp.stack([mine, other]), jnp.stack([other, mine]))
 
 
-def gather_rows(shard):
-    experts, tensors = (lax.axis_size(EXPERT), lax.axis_size(TENSOR))
-    expert, tensor = (lax.axis_index(EXPERT), lax.axis_index(TENSOR))
+def gather_tensor(shard):
+    tensors, tensor = (lax.axis_size(TENSOR), lax.axis_index(TENSOR))
     block = shard[None]
     distance = 1
     while distance < tensors:
         other = swap(block, TENSOR, distance)
         block = ordered((tensor // distance) % 2, block, other).reshape(-1, *shard.shape)
         distance *= 2
-    first_stage = block
+    return block
+
+
+def gather_experts(block, beside, released, waiting):
+    experts, tensors = (lax.axis_size(EXPERT), lax.axis_size(TENSOR))
+    expert = lax.axis_index(EXPERT)
+    columns = block.shape[-1]
     block = block[None]
     distance = 2
     while distance < experts // 4:
@@ -578,7 +609,9 @@
         [swap(from_far[:, :middle], EXPERT, near), swap(from_near[:, middle:], EXPERT, far)],
         axis=1,
     )
-    second_stage = corner
+    corner, beside, released, waiting = lax.optimization_barrier(
+        (corner, beside, released, waiting)
+    )
     pieces = (block, from_near, from_far, corner)
     crossed = [swap(piece, EXPERT, 1) for piece in pieces]
     near_bit, far_bit = ((expert // near) % 2, (expert // far) % 2)
@@ -592,7 +625,7 @@
 
     whole = ordered(expert % 2, arranged(pieces), arranged(crossed))
     whole = jnp.moveaxis(whole, 0, 1)
-    return whole.reshape(-1, shard.shape[1]), first_stage, second_stage
+    return whole.reshape(-1, columns), beside, across(released), waiting
 
 
 def scatter_sums(held, sending):
@@ -604,6 +637,7 @@
         return lax.dynamic_index_in_dim(values, index, axis, False)
 
     held = held + wide(swap(sending, EXPERT, 1))
+    stages = [held]
     near, far = (experts // 4, experts // 2)
     near_bit, far_bit = ((expert // near) % 2, (expert // far) % 2)
     held = held.reshape(4, experts // 8, tensors, -1, columns)
@@ -619,6 +653,7 @@
     passed_far = swap(low(to_corner[:, middle:]), EXPERT, far)
     to_far = jnp.concatenate([to_far[:, :middle] + wide(passed_near), to_far[:, middle:]], axis=1)
     to_near = jnp.concatenate([to_near[:, :middle], to_near[:, middle:] + wide(passed_far)], axis=1)
+    stages.append(to_near)
     held = (
         own
         + wide(swap(low(to_near), EXPERT, near))
@@ -630,39 +665,65 @@
         halves = held.reshape(2, -1, *held.shape[1:])
         held = pick(halves, bit) + wide(swap(low(pick(halves, 1 - bit)), EXPERT, distance))
         distance //= 2
+    stages.append(held)
     held = held.reshape(tensors, -1, columns)
     distance = tensors // 2
     while distance >= 1:
         bit = (tensor // distance) % 2
         halves = held.reshape(2, -1, *held.shape[1:])
-        held = pick(halves, bit) + wide(swap(low(pick(halves, 1 - bit)), TENSOR, distance))
+        kept = pick(halves, bit)
+        received = swap(low(pick(halves, 1 - bit)), TENSOR, distance)
+        if distance > 1:
+            held = kept + wide(received)
         distance //= 2
-    return held.reshape(-1, columns)
-
-
-def soap(along_rows, rate, own, other, weight, first, second, statistic, rotation):
-    blocks = statistic.shape[1]
+    stages.append(kept)
+    return kept.reshape(-1, columns), received.reshape(-1, columns), stages
+
+
+def soap_turn(along_rows, rate, at, token, gradient, state, statistics, earlier):
+    weight, first, second = state
+    statistic = statistics[0]
     f32 = jnp.float32
     if along_rows:
-        flat = pl.BlockSpec((BLK, D), lambda i: (i, 0))
-        deep = pl.BlockSpec((1, BLK, D), lambda i: (0, i, 0))
+        deep = pl.BlockSpec((1, BLK, D), lambda i: (0, at, 0))
     else:
-        flat = pl.BlockSpec((D, BLK), lambda i: (0, i))
-        deep = pl.BlockSpec((1, D, BLK), lambda i: (0, 0, i))
-    square = pl.BlockSpec((1, 1, BLK, BLK), lambda i: (0, i, 0, 0))
-    results = vmem_call(
-        partial(turn_kernel, along_rows, rate),
-        grid=(blocks,),
-        in_specs=[flat, flat, deep, deep, deep, square, square],
-        out_specs=[deep] * 4 + [square, pl.BlockSpec((1, BLK, BLK), lambda i: (i, 0, 0))],
+        deep = pl.BlockSpec((1, D, BLK), lambda i: (0, 0, at))
+    square = pl.BlockSpec((1, 1, BLK, BLK), lambda i: (0, at, 0, 0))
+    anywhere = pl.BlockSpec(memory_space=pl.ANY)
+    return vmem_call(
+        partial(turn_kernel, along_rows, rate, len(token)),
+        8,
+        grid=(1,),
+        in_specs=[anywhere] * len(token)
+        + [full_block(gradient.shape)]
+        + [deep] * 3
+        + [square] * 2
+        + [anywhere] * len(earlier),
+        out_specs=[deep] * 4 + [square, full_block((BLK, BLK))],
         out_shape=[jax.ShapeDtypeStruct(weight.shape, f32)] * 3
         + [
             jax.ShapeDtypeStruct(weight.shape, jnp.bfloat16),
             jax.ShapeDtypeStruct(statistic.shape, f32),
-            jax.ShapeDtypeStruct(statistic.shape[1:], f32),
+            jax.ShapeDtypeStruct((BLK, BLK), f32),
         ],
-    )(own, other, weight, first, second, statistic, rotation)
-    return (*results[:5], renew(results[5])[None])
+        input_output_aliases={6 + len(token) + i: i for i in range(len(earlier))},
+    )(*token, gradient, *state, *statistics, *earlier)
+
+
+def row_sums(left, right, at, left_paired):
+    rows, width = left[0].shape[-2:]
+    height, columns = (BLK, right[0].shape[-1]) if left_paired else (width, BLK)
+    paired = pl.BlockSpec((None, rows, BLK), lambda i: (i, 0, at))
+    plain = full_block((rows, columns if left_paired else width))
+    return vmem_call(
+        row_sums_kernel,
+        5,
+        grid=(2,),
+        in_specs=[paired if left_paired else plain] * MB
+        + [plain if left_paired else paired] * MB,
+        out_specs=pl.BlockSpec((None, height, columns), lambda i: (i, 0, 0)),
+        out_shape=jax.ShapeDtypeStruct((2, height, columns), jnp.bfloat16),
+    )(*left, *right)
 
 
 def per_device(
@@ -709,7 +770,7 @@
     columns = 4 * D + 128
     bf16, f32 = (jnp.bfloat16, jnp.float32)
     shape = jax.ShapeDtypeStruct
-    partner = [(i, (i + half) % tensors) for i in range(tensors)]
+    pairs = [[i, i + half] for i in range(half)]
     groups = [
         [e * tensors + z for e in range(experts) for z in range(h * half, (h + 1) * half)]
         for h in range(2)
@@ -717,9 +778,6 @@
 
     def exchange(values):
         return lax.all_to_all(values, BOTH, 0, 0, axis_index_groups=groups, tiled=True)
-
-    def across(values):
-        return lax.ppermute(values, TENSOR, partner)
 
     packed = jnp.concatenate(
         [
@@ -730,60 +788,78 @@
         ],
         axis=1,
     )
-    gathered, first_stage, second_stage = gather_rows(packed)
     in_own, out_own = (low(w_in[0]), low(w_out[0]))
-    sent_in, sent_out, _ = lax.optimization_barrier((in_own, out_own, first_stage))
-    in_peer, out_peer = (across(sent_in), across(sent_out))
     b_in_low, b_out_low = (low(b_in), low(b_out))
     peer_bias = across(jnp.concatenate([b_in_low, b_out_low], axis=1))
-    bias_in = wide(jnp.concatenate([b_in_low, peer_bias[:, :units]], axis=1))
+    chosen = expert_ids.reshape(MB, tokens_here, TOPK)
+    placed = slots.reshape(MB, tokens_here, TOPK)
+    target = jnp.where(placed < capacity, chosen * padded + placed, -1)
+    up_sent = vmem_call(
+        dispatch_kernel,
+        4,
+        grid=(1,),
+        in_specs=[full_block(target.shape), full_block(cotangent.shape)],
+        out_specs=full_block((expert_total, half, MB, padded, D)),
+        out_shape=shape((expert_total, half, MB, padded, D), bf16),
+    )(target, cotangent)
+    first_stage, peer_bias, sent_first = lax.optimization_barrier(
+        (gather_tensor(packed), peer_bias, in_own[: D // 2])
+    )
+    out_pair = lax.all_gather(out_own, TENSOR, axis_index_groups=pairs)
+    gathered, in_first, in_second, up_sent = gather_experts(
+        first_stage, across(sent_first), in_own[D // 2 :], up_sent
+    )
+    up_all = exchange(up_sent.reshape(members, MB, padded, D))
+    upper = tensor >= half
+    peer_in = peer_bias[:, :units]
+    bias_in = wide(
+        jnp.where(
+            upper,
+            jnp.concatenate([peer_in, b_in_low], axis=1),
+            jnp.concatenate([b_in_low, peer_in], axis=1),
+        )
+    )
     bias_out = jnp.zeros((1, D), f32)
     own_place = tensor * shard_columns
     peer_place = ((tensor + half) % tensors) * shard_columns
     bias_out = lax.dynamic_update_slice(bias_out, wide(b_out_low), (0, own_place))
     bias_out = lax.dynamic_update_slice(bias_out, wide(peer_bias[:, units:]), (0, peer_place))
-    chosen = expert_ids.reshape(MB, tokens_here, TOPK)
-    placed = slots.reshape(MB, tokens_here, TOPK)
-    target = jnp.where(placed < capacity, chosen * padded + placed, -1)
-    target_all = full_block(target.shape)
-    up_sent = vmem_call(
-        dispatch_kernel,
-        grid=(1,),
-        in_specs=[target_all, full_block(cotangent.shape)],
-        out_specs=full_block((expert_total, half, MB, padded, D)),
-        out_shape=shape((expert_total, half, MB, padded, D), bf16),
-    )(target, cotangent)
-    up_sent, _ = lax.optimization_barrier((up_sent, second_stage))
-    up_all = exchange(up_sent.reshape(members, MB, padded, D))
     image = pl.BlockSpec((1, 1, SEQ, D), lambda i: (i, 0, 0, 0))
 
     def per_step(*tail):
         return pl.BlockSpec((1, *tail), lambda i: (i,) + (0,) * len(tail))
 
-    sent, qkv, mixed, middle, probs = vmem_call(
+    *sent, qkv, mixed, middle, probs = vmem_call(
         partial(attention_kernel, expert_total),
+        11,
         grid=(MB,),
         in_specs=[image, per_step(SEQ, TOPK), full_block((D, columns))],
         out_specs=[
-            per_step(expert_total, half, padded, D),
+            *[full_block((expert_total, half, padded, D))] * MB,
             per_step(SEQ, 3 * D),
             per_step(SEQ, D),
             per_step(SEQ, D),
             per_step(SEQ, 128),
         ],
         out_shape=[
-            shape((MB, expert_total, half, padded, D), bf16),
+            *[shape((expert_total, half, padded, D), bf16)] * MB,
             shape((MB, SEQ, 3 * D), bf16),
             shape((MB, SEQ, D), bf16),
             shape((MB, SEQ, D), f32),
             shape((MB, SEQ, 128), f32),
         ],
+        scratch_shapes=[pltpu.VMEM((HEADS, SEQ, SEQ), f32), pltpu.VMEM((HEADS, SEQ, SEQ), bf16)],
     )(patches, target, gathered)
-    arrived = [exchange(sent[step].reshape(members, padded, D)) for step in range(MB)]
+    earlier, up_all, in_second = lax.optimization_barrier((sent[0], up_all, in_second))
+    in_peer = jnp.concatenate([in_first, in_second], axis=0)
+    in_pair = jnp.where(upper, jnp.stack([in_peer, in_own]), jnp.stack([in_own, in_peer]))
+    arrived = [exchange(earlier.reshape(members, padded, D))]
+    later, arrived[0] = lax.optimization_barrier((sent[1], arrived[0]))
+    arrived.append(exchange(later.reshape(members, padded, D)))
     count = max(
         n
         for n in range(1, members + 1)
-        if members % n == 0 and n * padded <= 256 and (n * padded) % 16 == 0
+        if members % n == 0 and n * padded <= ROW_TILE and (n * padded) % 16 == 0
     )
     tile = count * padded
     total_rows = members * padded
@@ -794,78 +870,81 @@
 
     expert_scalar = jnp.reshape(expert, (1,)).astype(jnp.int32)
     in_smem = pl.BlockSpec(memory_space=pltpu.SMEM)
+    anywhere = pl.BlockSpec(memory_space=pl.ANY)
+    both_rows = pl.BlockSpec((2, tile, units), lambda i: (0, i, 0))
+    both_shape = shape((2, total_rows, units), bf16)
     hidden = []
     for step in range(MB):
         hidden.append(
             vmem_call(
                 partial(hidden_kernel, expert_total),
+                12,
                 grid=(tiles,),
                 in_specs=[
                     in_smem,
                     pl.BlockSpec((count, padded, D), lambda i: (i, 0, 0)),
                     pl.BlockSpec((count, None, padded, D), lambda i, step=step: (i, step, 0, 0)),
                     pl.BlockSpec((D, 128), lambda i: (0, 4 * D // 128)),
-                    full_block((D, units)),
-                    full_block((D, units)),
+                    full_block((2, D, units)),
                     full_block((1, 2 * units)),
                 ],
-                out_specs=[rows_of(units)] * 4 + [rows_of(D), full_block((8, D))],
-                out_shape=[shape((total_rows, units), bf16)] * 4
+                out_specs=[both_rows] * 2 + [rows_of(D), full_block((8, D))],
+                out_shape=[both_shape] * 2
                 + [shape((total_rows, D), bf16), shape((8, D), f32)],
-            )(expert_scalar, arrived[step], up_all, gathered, in_own, in_peer, bias_in)
+            )(expert_scalar, arrived[step], up_all, gathered, in_pair, bias_in)
         )
-    sum_out = sum(column_sum(h[1], h[4]) for h in hidden)
-    out_other = across(low(sum_out))
-    sum_out_own = sum(column_sum(h[0], h[4]) for h in hidden)
+    blocks = units // BLK
+    row_grads = [h[2] for h in hidden]
+    sum_out = [row_sums([h[0] for h in hidden], row_grads, at, True) for at in range(blocks)]
     results = []
     for step in range(MB):
+        before = [] if step == 0 else sum_out
         results.append(
             vmem_call(
-                result_kernel,
+                partial(result_kernel, len(before)),
+                12,
                 grid=(tiles,),
-                in_specs=[rows_of(units)] * 4
+                in_specs=[anywhere] * len(before)
+                + [both_rows] * 2
                 + [
                     rows_of(D),
-                    full_block((units, D)),
-                    full_block((units, D)),
-                    full_block((D, units)),
-                    full_block((D, units)),
+                    full_block((2, units, D)),
+                    full_block((2, D, units)),
                     full_block((1, D)),
                 ],
                 out_specs=[
                     pl.BlockSpec((count, 2, padded, D), lambda i: (i, 0, 0, 0)),
-                    rows_of(units),
-                    rows_of(units),
+                    both_rows,
                     full_block((8, 2 * units)),
                 ],
                 out_shape=[
                     shape((members, 2, padded, D), bf16),
-                    shape((total_rows, units), bf16),
-                    shape((total_rows, units), bf16),
+                    both_shape,
                     shape((8, 2 * units), f32),
                 ],
-            )(*hidden[step][:5], out_own, out_peer, in_own, in_peer, bias_out)
+            )(*before, *hidden[step][:3], out_pair, in_pair, bias_out)
         )
+    flat_rows = [rows.reshape(total_rows, D) for rows in arrived]
+    sum_in = [row_sums(flat_rows, [r[1] for r in results], at, False) for at in range(blocks)]
+
+    def shared(sums):
+        return lax.psum_scatter(sums, TENSOR, axis_index_groups=pairs)
+
+    grads_out = [shared(sums) for sums in sum_out]
+    grads_in = [shared(sums) for sums in sum_in]
     returned = [exchange(r[0]) for r in results]
-    flat_rows = [rows.reshape(total_rows, D) for rows in arrived]
-    sum_in = sum(column_sum(rows, r[2]) for rows, r in zip(flat_rows, results))
-    in_other = across(low(sum_in))
-    sum_in_own = sum(column_sum(rows, r[1]) for rows, r in zip(flat_rows, results))
-    sum_bin = sum(r[3][:1] for r in results)
-    sum_bout = sum(h[5][:1] for h in hidden)
+    sum_bin = sum(r[2][:1] for r in results)
+    sum_bout = sum(h[3][:1] for h in hidden)
     bias_sums = jnp.concatenate(
         [
-            sum_bin[:, units:],
+            jnp.where(upper, sum_bin[:, :units], sum_bin[:, units:]),
             lax.dynamic_slice_in_dim(sum_bout, peer_place, shard_columns, 1),
         ],
         axis=1,
     )
     bias_other = across(bias_sums)
-    grad_bin = sum_bin[:, :units] + bias_other[:, :units]
-    grad_bout = (
-        lax.dynamic_slice_in_dim(sum_bout, own_place, shard_columns, 1) + bias_other[:, units:]
-    )
     backward = []
+    tokens = [sum_in]
     for step in range(MB):
         first = step == 0
         here = pl.BlockSpec((1, 1, SEQ, D), lambda i, step=step: (step, 0, 0, 0))
@@ -887,9 +966,11 @@
         earlier = [] if first else list(backward[-1][:2])
         backward.append(
             vmem_call(
-                partial(attention_backward_kernel, expert_total),
+                partial(attention_backward_kernel, expert_total, len(tokens[step])),
+        15,
                 grid=(1,),
-                in_specs=[
+                in_specs=[anywhere] * len(tokens[step])
+                + [
                     here,
                     here,
                     of_step(SEQ, TOPK),
@@ -903,54 +984,113 @@
                 + [pl.BlockSpec(memory_space=pl.ANY)] * len(earlier),
                 out_specs=[o[1] for o in outs],
                 out_shape=[o[0] for o in outs],
-                input_output_aliases={} if first else {9: 0, 10: 1},
-            )(patches, cotangent, target, back, qkv, mixed, middle, probs, gathered, *earlier)
+                scratch_shapes=[pltpu.VMEM((HEADS, SEQ, SEQ), f32)] * 2
+                + [pltpu.VMEM((HEADS, SEQ, SEQ), bf16)] * 2,
+                input_output_aliases={}
+                if first
+                else {9 + len(tokens[step]): 0, 10 + len(tokens[step]): 1},
+            )(
+                *tokens[step],
+                patches,
+                cotangent,
+                target,
+                back,
+                qkv,
+                mixed,
+                middle,
+                probs,
+                gathered,
+                *earlier,
+            )
         )
+        if first:
+            out_turned = [
+                soap_turn(
+                    True,
+                    RATE_OUTPUT,
+                    0,
+                    [backward[0][6]],
+                    grads_out[0],
+                    (w_out, w_out_first, w_out_second),
+                    (w_out_stat, w_out_basis),
+                    [],
+                )
+            ]
+            tokens.append([out_turned[0][5]])
     core_scalar = jnp.reshape(expert % 2, (1,)).astype(jnp.int32)
     block_rows = tensors * attn_weights.shape[0]
     flat_steps = [value for b in backward for value in b[2:]]
     core_shape = (experts // 2, block_rows, columns)
-    whole_vmem = pl.BlockSpec(memory_space=pltpu.VMEM)
-    held, sending = vmem_call(
+    held, sending, token = vmem_call(
         partial(weight_sums_kernel, expert_total),
-        in_specs=[in_smem] + [whole_vmem] * (1 + len(flat_steps)),
-        out_specs=[whole_vmem] * 2,
-        out_shape=[shape(core_shape, f32), shape(core_shape, bf16)],
-    )(core_scalar, mixed, *flat_steps)
-    mine = scatter_sums(held, sending)
-    grad_attn = mine[:, : 4 * D]
-    grad_router = mine[:, 4 * D : 4 * D + expert_total]
-    grad_norm = mine[:, 4 * D + expert_total : 4 * D + expert_total + 4].T
-    attn_first_new, attn_second_new, attn_new = adam_update(
-        attn_weights, grad_attn, attn_first, attn_second, RATE_DENSE, DECAY_RATE
-    )
-    router_first_new, router_second_new, router_new = adam_update(
-        router_weights, grad_router, router_first, router_second, RATE_DENSE, DECAY_RATE
-    )
-    norm_first_new, norm_second_new, norm_new = adam_update(
-        norm_params, grad_norm, norm_first, norm_second, RATE_NORMS, 0.0
-    )
-    w_out_results = soap(
-        True,
-        RATE_OUTPUT,
-        sum_out_own,
-        out_other,
-        w_out,
-        w_out_first,
-        w_out_second,
-        w_out_stat,
-        w_out_basis,
-    )
-    w_in_results = soap(
-        False,
-        RATE_INPUT,
-        sum_in_own,
-        in_other,
-        w_in,
-        w_in_first,
-        w_in_second,
-        w_in_stat,
-        w_in_basis,
+        8,
+        grid=(1,),
+        in_specs=[anywhere, in_smem] + [full_block(v.shape) for v in (mixed, *flat_steps)],
+        out_specs=[full_block(core_shape)] * 2 + [full_block((8, 128))],
+        out_shape=[shape(core_shape, f32), shape(core_shape, bf16), shape((8, 128), f32)],
+    )(b_in_low, core_scalar, mixed, *flat_steps)
+    kept, received, stages = scatter_sums(held, sending)
+    dense = [shape(attn_weights.shape, f32)] * 3 + [shape(attn_weights.shape, bf16)]
+    routers = [shape(router_weights.shape, f32)] * 3 + [shape(router_weights.shape, bf16)]
+    norms = [shape(norm_params.shape, f32)] * 3
+    states = (
+        kept,
+        received,
+        attn_weights,
+        attn_first,
+        attn_second,
+        router_weights,
+        router_first,
+        router_second,
+        norm_params,
+        norm_first,
+        norm_second,
+    )
+    updated_shapes = dense + routers + norms
+    updated = vmem_call(
+        dense_update_kernel,
+        3,
+        grid=(1,),
+        in_specs=[full_block(v.shape) for v in states],
+        out_specs=[full_block(v.shape) for v in updated_shapes],
+        out_shape=updated_shapes,
+    )(*states)
+    for at in range(1, blocks):
+        out_turned.append(
+            soap_turn(
+                True,
+                RATE_OUTPUT,
+                at,
+                [token],
+                grads_out[at],
+                (w_out, w_out_first, w_out_second),
+                (w_out_stat, w_out_basis),
+                out_turned[-1][:5],
+            )
+        )
+    w_out_basis_new = renew(stages[:1], [turned[5] for turned in out_turned])
+    in_turned = []
+    for at in range(blocks):
+        in_turned.append(
+            soap_turn(
+                False,
+                RATE_INPUT,
+                at,
+                [w_out_basis_new, stages[1]] if at == 0 else [in_turned[-1][5], stages[2]],
+                grads_in[at],
+                (w_in, w_in_first, w_in_second),
+                (w_in_stat, w_in_basis),
+                in_turned[-1][:5] if at > 0 else [],
+            )
+        )
+    w_in_basis_new = renew(stages[3:], [turned[5] for turned in in_turned])
+    bias_other, w_in_basis_new = lax.optimization_barrier((bias_other, w_in_basis_new))
+    w_in_results = (*in_turned[-1][:5], w_in_basis_new)
+    w_out_results = (*out_turned[-1][:5], w_out_basis_new)
+    own_bin = jnp.where(upper, sum_bin[:, units:], sum_bin[:, :units])
+    grad_bin = own_bin + bias_other[:, :units]
+    grad_bout = (
+        lax.dynamic_slice_in_dim(sum_bout, own_place, shard_columns, 1) + bias_other[:, units:]
     )
     bin_first_new, bin_second_new, bin_new = adam_update(
         b_in, grad_bin, b_in_first, b_in_second, RATE_BIASES, 0.0
@@ -960,17 +1100,7 @@
     )
     return (
         *backward[-1][:2],
-        attn_first_new,
-        attn_second_new,
-        attn_new,
-        low(attn_new),
-        router_first_new,
-        router_second_new,
-        router_new,
-        low(router_new),
-        norm_first_new,
-        norm_second_new,
-        norm_new,
+        *updated,
         *w_in_results,
         *w_out_results,
         bin_first_new,

time: 607 us -> 469 us (0.77)
  waiting for transfers between devices: 224 us -> 136 us
  blocking collectives: 38.3 us -> 0 us
  matrix products: 22.8 us -> 0 us
  Pallas kernels: 196 us -> 215 us
  local copies, waits for them, and re-layouts: 40.5 us -> 24.1 us
  between operations: 1.6 us -> 14.6 us
    ppermute x6 -> x4, waiting for transfers between devices: 125 us -> 29 us  [across(): lax.ppermute(values, TENSOR, [(i, (i + size // 2) % size) for i in range(...]
    all_to_all x1 -> x0, blocking collectives: 38.3 us -> none  [exchange(): lax.all_to_all(values, BOTH, 0, 0, axis_index_groups=groups, tiled=True)]
    all_gather x0 -> x1, waiting for transfers between devices: none -> 27.9 us  [per_device(): out_pair = lax.all_gather(out_own, TENSOR, axis_index_groups=pairs)]
    dot_general x8 -> x0, matrix products: 22.8 us -> none  [column_sum(): lax.dot_general(left_side, right_side, (((0,), (0,)), ((), ())), preferre...]
    pallas_call x13 -> x20, Pallas kernels: 196 us -> 215 us  [the longest x2 62.3 us: renew(): vmem_call(partial(renew_kernel, len(tokens)), 30, grid=(1,), out_shape=ja...]
    ppermute x17, waiting for transfers between devices: 50.6 us -> 40.4 us  [swap(): return lax.ppermute(values, axis, [(i, i ^ distance) for i in range(size)])]
    all_to_all x4 -> x5, waiting for transfers between devices: 48.5 us -> 38.7 us  [exchange(): lax.all_to_all(values, BOTH, 0, 0, axis_index_groups=groups, tiled=True)]
    ppermute x6 -> x4, starting transfers between devices: 12.9 us -> 3.62 us  [across(): lax.ppermute(values, TENSOR, [(i, (i + size // 2) % size) for i in range(...]
  transfers between devices with their start and end apart: 27 -> 31, of which waited for: 13 -> 13; matrix products, arithmetic and copies ran while one was open for 9% -> 8% of each run, Pallas kernels for 31% -> 46%
where the time goes in v1:
time: 469 us; the launch traced here: 460 us
  Pallas kernels  215 us (46%)
  waiting for transfers between devices  136 us (29%)
  starting transfers between devices  43.8 us (9%)
  other arithmetic  26.6 us (6%)
  local copies, waits for them, and re-layouts  24.1 us (5%)
  between operations  14.6 us (3%)
    pallas_call x2, Pallas kernels, renew(): vmem_call(partial(renew_kernel, len(tokens)), 30, grid=(1,), out_shape=ja...  62.3 us
    ppermute x17, waiting for transfers between devices, swap(): return lax.ppermute(values, axis, [(i, i ^ distance) for i in range(size)])  40.4 us
    all_to_all x5, waiting for transfers between devices, exchange(): lax.all_to_all(values, BOTH, 0, 0, axis_index_groups=groups, tiled=True)  38.7 us
    ppermute x4, waiting for transfers between devices, across(): lax.ppermute(values, TENSOR, [(i, (i + size // 2) % size) for i in range(...  29 us
    pallas_call x4, Pallas kernels, soap_turn(): vmem_call(partial(turn_kernel, along_rows, rate, len(token)), 8, grid=(1,...  28.8 us
    all_gather x1, waiting for transfers between devices, per_device(): out_pair = lax.all_gather(out_own, TENSOR, axis_index_groups=pairs)  27.9 us
    pallas_call x2, Pallas kernels, per_device(): vmem_call(partial(result_kernel, len(before)), 12, grid=(tiles,), in_spec...  25.6 us
    pallas_call x4, Pallas kernels, row_sums(): vmem_call(row_sums_kernel, 5, grid=(2,), in_specs=[paired if left_paired...  25 us
  transfers between devices with their start and end apart: 31, of which 13 were waited for; matrix products, arithmetic and copies ran while one was open for 8% of the time, Pallas kernels for 46%

profile of v1, /device:TPU:0, one launch (start us, length us, event | category | flops | bytes accessed | tf_op | source)
XLA Modules:
  0.0 460.4 jit_solution(2421424941551718066)
XLA Ops:
  21.3 15.4 %collective-permute-done.1 = bf16[2,24,3200]{2,1,0:T(8,128)(2,1)S(1)} collective-permute-done((bf16[2,24,3200]{2,1,0:T(8,128)(2,1)S(1)}, bf16[2,24,3200]{2,1,0:T(8,128)(2,1)S(1)}, u32[]{:S(2)}, u32[]{:S(2)}) %collective-permute-start.1) | collective-permute-done | bytes 307232 | tf_op jit(solution)/shard_map/ppermute | solution.py:572
  43.0 9.6 %collective-permute-done.3 = bf16[1,4,24,3200]{3,2,1,0:T(8,128)(2,1)S(1)} collective-permute-done((bf16[1,4,24,3200]{3,2,1,0:T(8,128)(2,1)S(1)}, bf16[1,4,24,3200]{3,2,1,0:T(8,128)(2,1)S(1)}, u32[]{:S(2)}, u32[]{:S(2)}) %collective-permute-start.3) | collective-permute-done | bytes 614432 | tf_op jit(solution)/shard_map/ppermute | solution.py:572
  83.5 11.7 %shard_map.517 = (bf16[8,2,56,768]{3,2,1,0:T(8,128)(2,1)}, bf16[8,2,56,768]{3,2,1,0:T(8,128)(2,1)}, bf16[2,196,2304]{2,1,0:T(8,128)(2,1)}, bf16[2,196,768]{2,1,0...) custom-call(bf16[2,1,196,768]{3,2,1,0:T(8,128)(2,1)} %copy.122.x_ref.refs_2_.refs_1_, ...), custom_call_target="tpu_custom_call" | custom-call | flops 12099999744 | tf_op jit(solution)/shard_map/pallas_call | solution.py:832
  95.1 23.5 %collective-permute-done.12 = bf16[384,768]{1,0:T(8,128)(2,1)} collective-permute-done((bf16[384,768]{1,0:T(8,128)(2,1)S(1)}, bf16[384,768]{1,0:T(8,128)(2,1)}, u32[]{:S(2)}, u32[]{:S(2)}) %collective-permute-start.12) | collective-permute-done | bytes 589856 | tf_op jit(solution)/shard_map/ppermute | solution.py:577
  126.8 17.7 %all-to-all-done.1.rows_ref = bf16[16,56,768]{2,1,0:T(8,128)(2,1)} async-done(((bf16[16,56,768]{2,1,0:T(8,128)(2,1)}), bf16[16,56,768]{2,1,0:T(8,128)(2,1)}, u32[]{:S(2)}, u32[]{:S(2)}) %all-to-all-start.1) | async-done | bytes 1376288 | tf_op jit(solution)/shard_map/all_to_all | solution.py:780
  151.2 11.8 %shard_map.518 = (bf16[2,896,768]{2,1,0:T(8,128)(2,1)}, bf16[2,896,768]{2,1,0:T(8,128)(2,1)}, bf16[896,768]{1,0:T(8,128)(2,1)}, f32[8,768]{1,0:T(8,128)}) custom-call(s32[1]{0:T(128)} %bitcast.27.expert_ref, bf16[16,56,768]{2,1,0:T(8,128)(2,1)} %all-to-all-done.1.rows_ref, bf16[16,2,56,768]{3,2,1,0:T(8,128)(2,1)} %all-to-all-done.up_ref, ...), custom_call_target="tpu_custom_call" | custom-call | flops 13200000000 | tf_op jit(solution)/shard_map/pallas_call | solution.py:879
  162.9 27.9 %all-gather.2.cloned.1.call-done.refs_3_.refs_5_ = bf16[2,768,768]{2,1,0:T(8,128)(2,1)} async-done(((bf16[1,768,768]{2,1,0:T(8,128)(2,1)}), bf16[2,768,768]{2,1,0:T(8,128)(2,1)}) %all-gather.2.cloned.1.call-update) | async-done | bytes 2359312 | tf_op jit(solution)/shard_map/all_gather | solution.py:808
  190.8 12.7 %shard_map.519 = (bf16[16,2,56,768]{3,2,1,0:T(8,128)(2,1)}, bf16[2,896,768]{2,1,0:T(8,128)(2,1)}, f32[8,1536]{1,0:T(8,128)}) custom-call(bf16[2,896,768]{2,1,0:T(8,128)(2,1)} %get-tuple-element.133.refs_0_, bf16[2,896,768]{2,1,0:T(8,128)(2,1)} %get-tuple-element.134.refs_1_, bf16[896,768]{1,0:T(8,128)(2,1)} %get-tuple-element.135.refs_2_, ...), custom_call_target="tpu_custom_call" | custom-call | flops 13200000000 | tf_op jit(solution)/shard_map/pallas_call | solution.py:903
  207.4 11.8 %shard_map.520 = (bf16[2,896,768]{2,1,0:T(8,128)(2,1)}, bf16[2,896,768]{2,1,0:T(8,128)(2,1)}, bf16[896,768]{1,0:T(8,128)(2,1)}, f32[8,768]{1,0:T(8,128)}) custom-call(s32[1]{0:T(128)} %bitcast.27.expert_ref, bf16[16,56,768]{2,1,0:T(8,128)(2,1)} %all-to-all-done.2.rows_ref, bf16[16,2,56,768]{3,2,1,0:T(8,128)(2,1)} %all-to-all-done.up_ref, ...), custom_call_target="tpu_custom_call" | custom-call | flops 13200000000 | tf_op jit(solution)/shard_map/pallas_call | solution.py:879
  231.2 12.9 %shard_map.523 = (bf16[16,2,56,768]{3,2,1,0:T(8,128)(2,1)}, bf16[2,896,768]{2,1,0:T(8,128)(2,1)}, f32[8,1536]{1,0:T(8,128)}) custom-call(bf16[2,384,768]{2,1,0:T(8,128)(2,1)} %shard_map.521.refs_0_, bf16[2,384,768]{2,1,0:T(8,128)(2,1)} %shard_map.522.refs_1_, bf16[2,896,768]{2,1,0:T(8,128)(2,1)} %get-tuple-element.137.refs_1_.refs_2_, ...), custom_call_target="tpu_custom_call" | custom-call | flops 13200000000 | tf_op jit(solution)/shard_map/pallas_call | solution.py:903
  244.1 7.7 %all-to-all-done.3 = bf16[16,2,56,768]{3,2,1,0:T(8,128)(2,1)S(1)} async-done(((bf16[16,2,56,768]{3,2,1,0:T(8,128)(2,1)}), bf16[16,2,56,768]{3,2,1,0:T(8,128)(2,1)S(1)}, u32[]{:S(2)}, u32[]{:S(2)}) %all-to-all-start.3) | async-done | bytes 2752544 | tf_op jit(solution)/shard_map/all_to_all | solution.py:780
  257.8 6.5 %shard_map.524.refs_0_ = bf16[2,768,384]{2,1,0:T(8,128)(2,1)} custom-call(bf16[896,768]{1,0:T(8,128)(2,1)} %bitcast.24.refs_0_, bf16[896,768]{1,0:T(8,128)(2,1)} %bitcast.26.refs_1_, bf16[2,896,768]{2,1,0:T(8,128)(2,1)} %get-tuple-element.136.refs_2_, bf16[2,896,768]{2,1,0:T(8,128)(2,1)} %get-tuple-element.140.refs_3_), custom_call_target="tpu_custom_call" | custom-call | flops 5500000256 | tf_op jit(solution)/shard_map/pallas_call | solution.py:718
  264.5 6.7 %shard_map.525.refs_1_ = bf16[2,768,384]{2,1,0:T(8,128)(2,1)} custom-call(bf16[896,768]{1,0:T(8,128)(2,1)} %bitcast.24.refs_0_, bf16[896,768]{1,0:T(8,128)(2,1)} %bitcast.26.refs_1_, bf16[2,896,768]{2,1,0:T(8,128)(2,1)} %get-tuple-element.136.refs_2_, bf16[2,896,768]{2,1,0:T(8,128)(2,1)} %get-tuple-element.140.refs_3_), custom_call_target="tpu_custom_call" | custom-call | flops 5500000256 | tf_op jit(solution)/shard_map/pallas_call | solution.py:718
  271.2 11.7 %shard_map.526 = (bf16[2,1,196,768]{3,2,1,0:T(8,128)(2,1)}, f32[2,1,196,768]{3,2,1,0:T(8,128)}, bf16[196,768]{1,0:T(8,128)(2,1)}, bf16[196,2304]{1,0:T(8,128)(2,...) custom-call(bf16[2,768,384]{2,1,0:T(8,128)(2,1)} %shard_map.524.refs_0_, ...), custom_call_target="tpu_custom_call" | custom-call | flops 16499999744 | tf_op jit(solution)/shard_map/pallas_call | solution.py:968
  282.9 6.9 %shard_map.527 = (f32[1,768,768]{2,1,0:T(8,128)}, f32[1,768,768]{2,1,0:T(8,128)}, f32[1,768,768]{2,1,0:T(8,128)}, bf16[1,768,768]{2,1,0:T(8,128)(2,1)}, f32[1,2,384,384]{3,2,1,0:T(8,128)}, /*index=5*/f32[384,384]{1,0:T(8,128)}) custom-call(bf16[196,128]{1,0:T(8,128)(2,1)} %get-tuple-element.146.refs_0_.refs_4_, bf16[384,768]{1,0:T(8,128)(2,1)} %bitcast.96, ...), custom_call_target="tpu_custom_call" | custom-call | flops 8800000000 | tf_op jit(solution)/shard_map/pallas_call | solution.py:693
  289.7 13.3 %all-to-all-done.4 = bf16[16,2,56,768]{3,2,1,0:T(8,128)(2,1)} async-done(((bf16[16,2,56,768]{3,2,1,0:T(8,128)(2,1)}), bf16[16,2,56,768]{3,2,1,0:T(8,128)(2,1)}, u32[]{:S(2)}, u32[]{:S(2)}) %all-to-all-start.4) | async-done | bytes 2752544 | tf_op jit(solution)/shard_map/all_to_all | solution.py:780
  303.0 12.4 %shard_map.528 = (bf16[2,1,196,768]{3,2,1,0:T(8,128)(2,1)}, f32[2,1,196,768]{3,2,1,0:T(8,128)}, bf16[196,768]{1,0:T(8,128)(2,1)}, bf16[196,2304]{1,0:T(8,128)(2,...) custom-call(f32[384,384]{1,0:T(8,128)} %get-tuple-element.147.refs_0, ...), custom_call_target="tpu_custom_call", output_to_operand_aliasing={{0}: (10, {}), {1}: (11, {})} | custom-call | flops 16499999744 | tf_op jit(solution)/shard_map/pallas_call | solution.py:968
  315.5 8.1 %shard_map.529 = (f32[4,96,3200]{2,1,0:T(8,128)}, bf16[4,96,3200]{2,1,0:T(8,128)(2,1)}, f32[8,128]{1,0:T(8,128)}) custom-call(bf16[1,768]{1,0:T(2,128)(2,1)} %copy-done.9, s32[1]{0:T(128)} %bitcast.33.core_ref, bf16[2,196,768]{2,1,0:T(8,128)(2,1)} %get-tuple-element.143.refs_7_.refs_6_.mixed_ref, bf16[196,768]{1,0:T(8,128)(2,1)} %get-tuple-element.153.refs_0_, ...), custom_call_target="tpu_custom_call" | custom-call | flops 8800000000 | tf_op jit(solution)/shard_map/pallas_call | solution.py:1024
  331.8 7.0 %shard_map.531 = (f32[1,768,768]{2,1,0:T(8,128)}, f32[1,768,768]{2,1,0:T(8,128)}, f32[1,768,768]{2,1,0:T(8,128)}, bf16[1,768,768]{2,1,0:T(8,128)(2,1)}, f32[1,2,384,384]{3,2,1,0:T(8,128)}, /*index=5*/f32[384,384]{1,0:T(8,128)}) custom-call(f32[8,128]{1,0:T(8,128)} %get-tuple-element.177.refs_0_,, ...), custom_call_target="tpu_custom_call", output_to_operand_aliasing={{0}: (7, {}), {1}: (8, {}), {2}: (9, {}), {3}: (10, {}), {4... | custom-call | flops 8800000000 | tf_op jit(solution)/shard_map/pallas_call | solution.py:693
  344.8 31.2 %shard_map.532.refs_0_ = f32[1,2,384,384]{3,2,1,0:T(8,128)} custom-call(f32[4,96,3200]{2,1,0:T(8,128)} %copy-done, f32[384,384]{1,0:T(8,128)} %get-tuple-element.147.refs_0_.refs_1_, f32[384,384]{1,0:T(8,128)} %get-tuple-element.183.refs_2_), custom_call_target="tpu_custom_call" | custom-call | flops 32999999488 | tf_op jit(solution)/shard_map/pallas_call | solution.py:166
  378.7 7.7 %shard_map.533 = (f32[1,768,768]{2,1,0:T(8,128)}, f32[1,768,768]{2,1,0:T(8,128)}, f32[1,768,768]{2,1,0:T(8,128)}, bf16[1,768,768]{2,1,0:T(8,128)(2,1)}, f32[1,2,384,384]{3,2,1,0:T(8,128)}, /*index=5*/f32[384,384]{1,0:T(8,128)}) custom-call(f32[1,2,384,384]{3,2,1,0:T(8,128)} %shard_map.532.refs_0_, f32[1,4,24,3200]{3,2,1,0:T(8,128)} %pad_maximum_fusion.refs_1_, ...), custom_call_target="tpu_custom_call" | custom-call | flops 8800000000 | tf_op jit(solution)/shard_map/pallas_call | solution.py:693
  386.3 6.5 %collective-permute-done.17 = bf16[1,4,24,3200]{3,2,1,0:T(8,128)(2,1)S(1)} collective-permute-done((bf16[1,4,24,3200]{3,2,1,0:T(8,128)(2,1)S(1)}, bf16[1,4,24,3200]{3,2,1,0:T(8,128)(2,1)S(1)}, u32[]{:S(2)}, u32[]{:S(2)}) %collective-permute-start.17) | collective-permute-done | bytes 614432 | tf_op jit(solution)/shard_map/ppermute | solution.py:572
  396.9 7.3 %shard_map.534 = (f32[1,768,768]{2,1,0:T(8,128)}, f32[1,768,768]{2,1,0:T(8,128)}, f32[1,768,768]{2,1,0:T(8,128)}, bf16[1,768,768]{2,1,0:T(8,128)(2,1)}, f32[1,2,384,384]{3,2,1,0:T(8,128)}, /*index=5*/f32[384,384]{1,0:T(8,128)}) custom-call(f32[384,384]{1,0:T(8,128)} %get-tuple-element.184.refs_0, ...), custom_call_target="tpu_custom_call", output_to_operand_aliasing={{0}: (8, {}), {1}: (9, {}), {2}: (10, {}), {3}: (11, {}), {... | custom-call | flops 8800000000 | tf_op jit(solution)/shard_map/pallas_call | solution.py:693
  412.6 31.1 %shard_map.535 = f32[1,2,384,384]{3,2,1,0:T(8,128)} custom-call(f32[1,24,3200]{2,1,0:T(8,128)} %constant_dynamic-slice_fusion.2.refs_0_, f32[384,384]{1,0:T(8,128)} %get-tuple-element.184.refs_0_.refs_1_, f32[384,384]{1,0:T(8,128)} %get-tuple-element.199.refs_2_), custom_call_target="tpu_custom_call" | custom-call | flops 32999999488 | tf_op jit(solution)/shard_map/pallas_call | solution.py:166
  (187 shorter events, 126.9 us)
Async XLA Ops:
  14.3 22.5 %collective-permute-start.2 = (bf16[1,960]{1,0:T(2,128)(2,1)S(1)}, bf16[1,960]{1,0:T(2,128)(2,1)S(1)}, u32[]{:S(2)}, u32[]{:S(2)}) collective-permute-start(bf16[1,960]{1,0:T(2,128)(2,1)S(1)} %pad_maximum_fusion.3), channel_id=1, source_target_pairs={{0,2},{1,3},{2,0},{3,1},{4,6},{5,7},{6,4},{7,5},{8,10},{9,11},{10,... | collective-permute-start | bytes 5768 | tf_op jit(solution)/shard_map/ppermute | solution.py:577
  20.8 15.9 %collective-permute-start.1 = (bf16[2,24,3200]{2,1,0:T(8,128)(2,1)S(1)}, bf16[2,24,3200]{2,1,0:T(8,128)(2,1)S(1)}, u32[]{:S(2)}, u32[]{:S(2)}) collective-permute-start(bf16[2,24,3200]{2,1,0:T(8,128)(2,1)S(1)} %maximum_select_fusion.10), channel_id=1, source_target_pairs={{0,2},{1,3},{2,0},{3,1},{4,6},{5,7},{6,4},{7,5},{8,10},{9,11},{10,... | collective-permute-start | bytes 921608 | tf_op jit(solution)/shard_map/ppermute | solution.py:572
  36.8 15.8 %collective-permute-start.3 = (bf16[1,4,24,3200]{3,2,1,0:T(8,128)(2,1)S(1)}, bf16[1,4,24,3200]{3,2,1,0:T(8,128)(2,1)S(1)}, u32[]{:S(2)}, u32[]{:S(2)}) collective-permute-start(bf16[1,4,24,3200]{3,2,1,0:T(8,128)(2,1)S(1)} %bitcast.77), channel_id=1, source_target_pairs={{0,8},{4,12},{8,0},{12,4},{16,24},{20,28},{24,16},{28,20},{1,9},{5... | collective-permute-start | bytes 1843208 | tf_op jit(solution)/shard_map/ppermute | solution.py:572
  38.4 15.9 %collective-permute-start.4 = (bf16[1,4,24,3200]{3,2,1,0:T(8,128)(2,1)S(1)}, bf16[1,4,24,3200]{3,2,1,0:T(8,128)(2,1)S(1)}, u32[]{:S(2)}, u32[]{:S(2)}) collective-permute-start(bf16[1,4,24,3200]{3,2,1,0:T(8,128)(2,1)S(1)} %bitcast.78), channel_id=1, source_target_pairs={{0,16},{4,20},{8,24},{12,28},{16,0},{20,4},{24,8},{28,12},{1,17},{... | collective-permute-start | bytes 1843208 | tf_op jit(solution)/shard_map/ppermute | solution.py:572
  43.0 24.9 %collective-permute-start.7 = (bf16[384,768]{1,0:T(8,128)(2,1)S(1)}, bf16[384,768]{1,0:T(8,128)(2,1)}, u32[]{:S(2)}, u32[]{:S(2)}) collective-permute-start(bf16[384,768]{1,0:T(8,128)(2,1)S(1)} %copy-done.8), channel_id=1, source_target_pairs={{0,2},{1,3},{2,0},{3,1},{4,6},{5,7},{6,4},{7,5},{8,10},{9,11},{10,... | collective-permute-start | bytes 1769480 | tf_op jit(solution)/shard_map/ppermute | solution.py:577
  67.9 50.7 %all-to-all-start = ((bf16[16,2,56,768]{3,2,1,0:T(8,128)(2,1)}), bf16[16,2,56,768]{3,2,1,0:T(8,128)(2,1)}, u32[]{:S(2)}, u32[]{:S(2)}) async-start(bf16[16,2,56,768]{3,2,1,0:T(8,128)(2,1)} %bitcast.75), calls=%async_computation | async-start | bytes 5505024 | tf_op jit(solution)/shard_map/all_to_all | solution.py:780
  77.1 41.6 %collective-permute-start.12 = (bf16[384,768]{1,0:T(8,128)(2,1)S(1)}, bf16[384,768]{1,0:T(8,128)(2,1)}, u32[]{:S(2)}, u32[]{:S(2)}) collective-permute-start(bf16[384,768]{1,0:T(8,128)(2,1)S(1)} %copy-done.7), channel_id=1, source_target_pairs={{0,2},{1,3},{2,0},{3,1},{4,6},{5,7},{6,4},{7,5},{8,10},{9,11},{10,... | collective-permute-start | bytes 1769480 | tf_op jit(solution)/shard_map/ppermute | solution.py:577
  118.6 25.9 %all-to-all-start.1 = ((bf16[16,56,768]{2,1,0:T(8,128)(2,1)}), bf16[16,56,768]{2,1,0:T(8,128)(2,1)}, u32[]{:S(2)}, u32[]{:S(2)}) async-start(bf16[16,56,768]{2,1,0:T(8,128)(2,1)} %bitcast.88), calls=%async_computation.1 | async-start | bytes 2752512 | tf_op jit(solution)/shard_map/all_to_all | solution.py:780
  123.2 67.6 %all-gather.2.cloned.1.call-start = ((), (), s32[]{:S(2)}) async-start(), calls=%async_computation.9 | async-start | bytes 3538944 | tf_op jit(solution)/shard_map/all_gather | solution.py:808
  144.5 59.1 %all-to-all-start.2 = ((bf16[16,56,768]{2,1,0:T(8,128)(2,1)}), bf16[16,56,768]{2,1,0:T(8,128)(2,1)}, u32[]{:S(2)}, u32[]{:S(2)}) async-start(bf16[16,56,768]{2,1,0:T(8,128)(2,1)} %bitcast.87), calls=%async_computation.2 | async-start | bytes 2752512 | tf_op jit(solution)/shard_map/all_to_all | solution.py:780
  203.6 48.2 %all-to-all-start.3 = ((bf16[16,2,56,768]{3,2,1,0:T(8,128)(2,1)}), bf16[16,2,56,768]{3,2,1,0:T(8,128)(2,1)S(1)}, u32[]{:S(2)}, u32[]{:S(2)}) async-start(bf16[16,2,56,768]{3,2,1,0:T(8,128)(2,1)} %get-tuple-element.141), calls=%async_computation.3 | async-start | bytes 5505024 | tf_op jit(solution)/shard_map/all_to_all | solution.py:780
  207.4 75.5 %reduce-scatter.5.cloned.1.call-start = ((), (), s32[]{:S(2)}) async-start(), calls=%async_computation.10 | async-start | bytes 1769472 | tf_op jit(solution)/shard_map/reduce_scatter | solution.py:931
  225.1 106.6 %reduce-scatter.7.cloned.1.call-start = ((), (), s32[]{:S(2)}) async-start(), calls=%async_computation.11 | async-start | bytes 1769472 | tf_op jit(solution)/shard_map/reduce_scatter | solution.py:931
  253.3 49.7 %all-to-all-start.4 = ((bf16[16,2,56,768]{3,2,1,0:T(8,128)(2,1)}), bf16[16,2,56,768]{3,2,1,0:T(8,128)(2,1)}, u32[]{:S(2)}, u32[]{:S(2)}) async-start(bf16[16,2,56,768]{3,2,1,0:T(8,128)(2,1)} %get-tuple-element.148), calls=%async_computation.5 | async-start | bytes 5505024 | tf_op jit(solution)/shard_map/all_to_all | solution.py:780
  257.8 120.9 %reduce-scatter.9.cloned.1.call-start = ((), (), s32[]{:S(2)}) async-start(), calls=%async_computation.12 | async-start | bytes 1769472 | tf_op jit(solution)/shard_map/reduce_scatter | solution.py:931
  264.4 132.5 %reduce-scatter.11.cloned.1.call-start = ((), (), s32[]{:S(2)}) async-start(), calls=%async_computation.13 | async-start | bytes 1769472 | tf_op jit(solution)/shard_map/reduce_scatter | solution.py:931
  323.5 15.2 %collective-permute-start.13 = (bf16[4,96,3200]{2,1,0:T(8,128)(2,1)}, bf16[4,96,3200]{2,1,0:T(8,128)(2,1)S(1)}, u32[]{:S(2)}, u32[]{:S(2)}) collective-permute-start(bf16[4,96,3200]{2,1,0:T(8,128)(2,1)} %get-tuple-element.165), channel_id=1, source_target_pairs={{0,4},{4,0},{8,12},{12,8},{16,20},{20,16},{24,28},{28,24},{1,5},{5... | collective-permute-start | bytes 7372808 | tf_op jit(solution)/shard_map/ppermute | solution.py:572
  327.4 116.3 %collective-permute-start.20 = (f32[1,960]{1,0:T(1,128)S(1)}, f32[1,960]{1,0:T(1,128)S(1)}, u32[]{:S(2)}, u32[]{:S(2)}) collective-permute-start(f32[1,960]{1,0:T(1,128)S(1)} %pad_maximum_fusion.4), channel_id=1, source_target_pairs={{0,2},{1,3},{2,0},{3,1},{4,6},{5,7},{6,4},{7,5},{8,10},{9,11},{10,... | collective-permute-start | bytes 11528 | tf_op jit(solution)/shard_map/ppermute | solution.py:577
  341.5 35.7 %collective-permute-start.16 = (bf16[1,2,24,3200]{3,2,1,0:T(8,128)(2,1)S(1)}, bf16[1,2,24,3200]{3,2,1,0:T(8,128)(2,1)S(1)}, u32[]{:S(2)}, u32[]{:S(2)}) collective-permute-start(bf16[1,2,24,3200]{3,2,1,0:T(8,128)(2,1)S(1)} %get-tuple-element.313), channel_id=1, source_target_pairs={{0,8},{4,12},{8,0},{12,4},{16,24},{20,28},{24,16},{28,20},{1,9},{5... | collective-permute-start | bytes 921608 | tf_op jit(solution)/shard_map/ppermute | solution.py:572
  343.1 32.9 %collective-permute-start.14 = (bf16[1,2,24,3200]{3,2,1,0:T(8,128)(2,1)S(1)}, bf16[1,2,24,3200]{3,2,1,0:T(8,128)(2,1)S(1)}, u32[]{:S(2)}, u32[]{:S(2)}) collective-permute-start(bf16[1,2,24,3200]{3,2,1,0:T(8,128)(2,1)S(1)} %get-tuple-element.312), channel_id=1, source_target_pairs={{0,16},{4,20},{8,24},{12,28},{16,0},{20,4},{24,8},{28,12},{1,17},{... | collective-permute-start | bytes 921608 | tf_op jit(solution)/shard_map/ppermute | solution.py:572
  377.4 15.4 %collective-permute-start.17 = (bf16[1,4,24,3200]{3,2,1,0:T(8,128)(2,1)S(1)}, bf16[1,4,24,3200]{3,2,1,0:T(8,128)(2,1)S(1)}, u32[]{:S(2)}, u32[]{:S(2)}) collective-permute-start(bf16[1,4,24,3200]{3,2,1,0:T(8,128)(2,1)S(1)} %pad_maximum_fusion.2), channel_id=1, source_target_pairs={{0,16},{4,20},{8,24},{12,28},{16,0},{20,4},{24,8},{28,12},{1,17},{... | collective-permute-start | bytes 1843208 | tf_op jit(solution)/shard_map/ppermute | solution.py:572
  378.0 15.1 %collective-permute-start.15 = (bf16[1,4,24,3200]{3,2,1,0:T(8,128)(2,1)S(1)}, bf16[1,4,24,3200]{3,2,1,0:T(8,128)(2,1)S(1)}, u32[]{:S(2)}, u32[]{:S(2)}) collective-permute-start(bf16[1,4,24,3200]{3,2,1,0:T(8,128)(2,1)S(1)} %fusion.9), channel_id=1, source_target_pairs={{0,8},{4,12},{8,0},{12,4},{16,24},{20,28},{24,16},{28,20},{1,9},{5... | collective-permute-start | bytes 1843208 | tf_op jit(solution)/shard_map/ppermute | solution.py:572
  394.6 15.2 %collective-permute-start.18 = (bf16[2,24,3200]{2,1,0:T(8,128)(2,1)S(1)}, bf16[2,24,3200]{2,1,0:T(8,128)(2,1)S(1)}, u32[]{:S(2)}, u32[]{:S(2)}) collective-permute-start(bf16[2,24,3200]{2,1,0:T(8,128)(2,1)S(1)} %fusion.3), channel_id=1, source_target_pairs={{0,2},{1,3},{2,0},{3,1},{4,6},{5,7},{6,4},{7,5},{8,10},{9,11},{10,... | collective-permute-start | bytes 921608 | tf_op jit(solution)/shard_map/ppermute | solution.py:572
  412.4 32.6 %collective-permute-start.19 = (bf16[1,24,3200]{2,1,0:T(8,128)(2,1)S(1)}, bf16[1,24,3200]{2,1,0:T(8,128)(2,1)S(1)}, u32[]{:S(2)}, u32[]{:S(2)}) collective-permute-start(bf16[1,24,3200]{2,1,0:T(8,128)(2,1)S(1)} %dynamic-slice_convert_fusion.2), channel_id=1, source_target_pairs={{0,1},{1,0},{2,3},{3,2},{4,5},{5,4},{6,7},{7,6},{8,9},{9,8},{10,11... | collective-permute-start | bytes 460808 | tf_op jit(solution)/shard_map/ppermute | solution.py:572
  (32 other events, 474.6 us)
Sparse Core Ops, SparseCore 0:
  126.2 64.6 all-gather.1
  225.2 35.6 reduce-scatter.4
  263.9 33.3 reduce-scatter.6
  299.9 35.6 reduce-scatter.8
  337.8 34.3 reduce-scatter.10

commit v2 on v1

--- a/solution.py
+++ b/solution.py
@@ -543,9 +543,9 @@
 def dense_update_kernel(kept_ref, received_ref, *refs):
     inputs, outputs = (refs[:9], refs[9:])
     gradient = kept_ref[...] + wide(received_ref[...])
-    extra = gradient[:, 4 * D :]
-    experts = inputs[3].shape[1]
-    gradients = (gradient[:, : 4 * D], extra[:, :experts], extra.T[experts : experts + 4])
+    extra = gradient[:, 4 * D :].T
+    experts = inputs[3].shape[0]
+    gradients = (gradient[:, : 4 * D], extra[:experts], extra[experts : experts + 4])
     rates = ((RATE_DENSE, DECAY_RATE), (RATE_DENSE, DECAY_RATE), (RATE_NORMS, 0.0))
     place = 0
     for kind in range(3):
@@ -592,7 +592,7 @@
     return block
 
 
-def gather_experts(block, beside, released, waiting):
+def gather_experts(block, beside, released):
     experts, tensors = (lax.axis_size(EXPERT), lax.axis_size(TENSOR))
     expert = lax.axis_index(EXPERT)
     columns = block.shape[-1]
@@ -609,9 +609,7 @@
         [swap(from_far[:, :middle], EXPERT, near), swap(from_near[:, middle:], EXPERT, far)],
         axis=1,
     )
-    corner, beside, released, waiting = lax.optimization_barrier(
-        (corner, beside, released, waiting)
-    )
+    corner, beside, released = lax.optimization_barrier((corner, beside, released))
     pieces = (block, from_near, from_far, corner)
     crossed = [swap(piece, EXPERT, 1) for piece in pieces]
     near_bit, far_bit = ((expert // near) % 2, (expert // far) % 2)
@@ -625,7 +623,7 @@
 
     whole = ordered(expert % 2, arranged(pieces), arranged(crossed))
     whole = jnp.moveaxis(whole, 0, 1)
-    return whole.reshape(-1, columns), beside, across(released), waiting
+    return whole.reshape(-1, columns), beside, across(released)
 
 
 def scatter_sums(held, sending):
@@ -805,11 +803,11 @@
     first_stage, peer_bias, sent_first = lax.optimization_barrier(
         (gather_tensor(packed), peer_bias, in_own[: D // 2])
     )
-    out_pair = lax.all_gather(out_own, TENSOR, axis_index_groups=pairs)
-    gathered, in_first, in_second, up_sent = gather_experts(
-        first_stage, across(sent_first), in_own[D // 2 :], up_sent
-    )
+    out_first = lax.all_gather(out_own[: units // 2], TENSOR, axis_index_groups=pairs)
     up_all = exchange(up_sent.reshape(members, MB, padded, D))
+    gathered, in_first, in_second = gather_experts(
+        first_stage, across(sent_first), in_own[D // 2 :]
+    )
     upper = tensor >= half
     peer_in = peer_bias[:, :units]
     bias_in = wide(
@@ -854,7 +852,7 @@
     in_peer = jnp.concatenate([in_first, in_second], axis=0)
     in_pair = jnp.where(upper, jnp.stack([in_peer, in_own]), jnp.stack([in_own, in_peer]))
     arrived = [exchange(earlier.reshape(members, padded, D))]
-    later, arrived[0] = lax.optimization_barrier((sent[1], arrived[0]))
+    later, arrived[0], out_first = lax.optimization_barrier((sent[1], arrived[0], out_first))
     arrived.append(exchange(later.reshape(members, padded, D)))
     count = max(
         n
@@ -893,12 +891,16 @@
                 + [shape((total_rows, D), bf16), shape((8, D), f32)],
             )(expert_scalar, arrived[step], up_all, gathered, in_pair, bias_in)
         )
+    sent_second, hidden_last = lax.optimization_barrier((out_own[units // 2 :], hidden[-1][2]))
+    hidden[-1] = (*hidden[-1][:2], hidden_last, *hidden[-1][3:])
+    out_second = lax.all_gather(sent_second, TENSOR, axis_index_groups=pairs)
+    out_pair = jnp.concatenate([out_first, out_second], axis=1)
     blocks = units // BLK
     row_grads = [h[2] for h in hidden]
     sum_out = [row_sums([h[0] for h in hidden], row_grads, at, True) for at in range(blocks)]
     results = []
     for step in range(MB):
-        before = [] if step == 0 else sum_out
+        before = sum_out if step == 0 else []
         results.append(
             vmem_call(
                 partial(result_kernel, len(before)),
@@ -1031,7 +1033,8 @@
     )(b_in_low, core_scalar, mixed, *flat_steps)
     kept, received, stages = scatter_sums(held, sending)
     dense = [shape(attn_weights.shape, f32)] * 3 + [shape(attn_weights.shape, bf16)]
-    routers = [shape(router_weights.shape, f32)] * 3 + [shape(router_weights.shape, bf16)]
+    turned_shape = router_weights.shape[::-1]
+    routers = [shape(turned_shape, f32)] * 3 + [shape(turned_shape, bf16)]
     norms = [shape(norm_params.shape, f32)] * 3
     states = (
         kept,
@@ -1039,9 +1042,9 @@
         attn_weights,
         attn_first,
         attn_second,
-        router_weights,
-        router_first,
-        router_second,
+        router_weights.T,
+        router_first.T,
+        router_second.T,
         norm_params,
         norm_first,
         norm_second,
@@ -1100,7 +1103,9 @@
     )
     return (
         *backward[-1][:2],
-        *updated,
+        *updated[:4],
+        *(value.T for value in updated[4:8]),
+        *updated[8:],
         *w_in_results,
         *w_out_results,
         bin_first_new,

time: 469 us -> 533 us (1.14)
  waiting for transfers between devices: 136 us -> 202 us
    ppermute x17, waiting for transfers between devices: 40.4 us -> 74.1 us  [swap(): return lax.ppermute(values, axis, [(i, i ^ distance) for i in range(size)])]
    all_to_all x5, waiting for transfers between devices: 38.7 us -> 65.8 us  [exchange(): lax.all_to_all(values, BOTH, 0, 0, axis_index_groups=groups, tiled=True)]
    all_gather x1 -> x2, waiting for transfers between devices: 27.9 us -> 49.6 us  [the longest x1 37.5 us: per_device(): lax.all_gather(out_own[:units // 2], TENSOR, axis_index_groups=pairs)]
    ppermute x4, waiting for transfers between devices: 29 us -> 11.3 us  [across(): lax.ppermute(values, TENSOR, [(i, (i + size // 2) % size) for i in range(...]
    unnamed x62 -> x55, local copies, waits for them, and re-layouts: 20.1 us -> 13.7 us
  transfers between devices with their start and end apart: 31 -> 32, of which waited for: 13 -> 16; matrix products, arithmetic and copies ran while one was open for 8% -> 8% of each run, Pallas kernels for 46% -> 36%
where the time goes in v2:
time: 533 us; the launch traced here: 525 us
  Pallas kernels  216 us (41%)
  waiting for transfers between devices  202 us (38%)
  starting transfers between devices  42 us (8%)
  other arithmetic  29.5 us (6%)
  local copies, waits for them, and re-layouts  20.8 us (4%)
  between operations  15 us (3%)
    ppermute x17, waiting for transfers between devices, swap(): return lax.ppermute(values, axis, [(i, i ^ distance) for i in range(size)])  74.1 us
    all_to_all x5, waiting for transfers between devices, exchange(): lax.all_to_all(values, BOTH, 0, 0, axis_index_groups=groups, tiled=True)  65.8 us
    pallas_call x2, Pallas kernels, renew(): vmem_call(partial(renew_kernel, len(tokens)), 30, grid=(1,), out_shape=ja...  62.7 us
    all_gather x1, waiting for transfers between devices, per_device(): lax.all_gather(out_own[:units // 2], TENSOR, axis_index_groups=pairs)  37.5 us
    pallas_call x4, Pallas kernels, soap_turn(): vmem_call(partial(turn_kernel, along_rows, rate, len(token)), 8, grid=(1,...  29 us
    pallas_call x2, Pallas kernels, per_device(): vmem_call(partial(result_kernel, len(before)), 12, grid=(tiles,), in_spec...  25.7 us
    pallas_call x4, Pallas kernels, row_sums(): vmem_call(row_sums_kernel, 5, grid=(2,), in_specs=[paired if left_paired...  25.1 us
    pallas_call x2, Pallas kernels, per_device(): vmem_call(partial(attention_backward_kernel, expert_total, len(tokens[ste...  23.8 us
  transfers between devices with their start and end apart: 32, of which 16 were waited for; matrix products, arithmetic and copies ran while one was open for 8% of the time, Pallas kernels for 36%

profile of v2, /device:TPU:0, one launch (start us, length us, event | category | flops | bytes accessed | tf_op | source)
XLA Modules:
  0.0 525.1 jit_solution(15723788196057593140)
XLA Ops:
  29.0 14.3 %collective-permute-done.1 = bf16[2,24,3200]{2,1,0:T(8,128)(2,1)S(1)} collective-permute-done((bf16[2,24,3200]{2,1,0:T(8,128)(2,1)S(1)}, bf16[2,24,3200]{2,1,0:T(8,128)(2,1)S(1)}, u32[]{:S(2)}, u32[]{:S(2)}) %collective-permute-start.1) | collective-permute-done | bytes 307232 | tf_op jit(solution)/shard_map/ppermute | solution.py:572
  65.2 32.5 %collective-permute-done.5 = bf16[1,2,24,3200]{3,2,1,0:T(8,128)(2,1)S(1)} collective-permute-done((bf16[1,2,24,3200]{3,2,1,0:T(8,128)(2,1)S(1)}, bf16[1,2,24,3200]{3,2,1,0:T(8,128)(2,1)S(1)}, u32[]{:S(2)}, u32[]{:S(2)}) %collective-permute-start.5) | collective-permute-done | bytes 307232 | tf_op jit(solution)/shard_map/ppermute | solution.py:572
  109.9 11.7 %shard_map.516 = (bf16[8,2,56,768]{3,2,1,0:T(8,128)(2,1)}, bf16[8,2,56,768]{3,2,1,0:T(8,128)(2,1)}, bf16[2,196,2304]{2,1,0:T(8,128)(2,1)}, bf16[2,196,768]{2,1,0...) custom-call(bf16[2,1,196,768]{3,2,1,0:T(8,128)(2,1)} %copy.107.x_ref.refs_2_.refs_1_, ...), custom_call_target="tpu_custom_call" | custom-call | flops 12099999744 | tf_op jit(solution)/shard_map/pallas_call | solution.py:830
  121.6 8.2 %collective-permute-done.12 = bf16[384,768]{1,0:T(8,128)(2,1)} collective-permute-done((bf16[384,768]{1,0:T(8,128)(2,1)S(1)}, bf16[384,768]{1,0:T(8,128)(2,1)}, u32[]{:S(2)}, u32[]{:S(2)}) %collective-permute-start.12) | collective-permute-done | bytes 589856 | tf_op jit(solution)/shard_map/ppermute | solution.py:577
  135.7 37.5 %all-gather.4.cloned.1.call-done = bf16[2,384,768]{2,1,0:T(8,128)(2,1)} async-done(((bf16[1,384,768]{2,1,0:T(8,128)(2,1)}), bf16[2,384,768]{2,1,0:T(8,128)(2,1)}) %all-gather.4.cloned.1.call-update) | async-done | bytes 1179664 | tf_op jit(solution)/shard_map/all_gather | solution.py:806
  181.5 14.5 %all-to-all-done.2.rows_ref = bf16[16,56,768]{2,1,0:T(8,128)(2,1)S(1)} async-done(((bf16[16,56,768]{2,1,0:T(8,128)(2,1)}), bf16[16,56,768]{2,1,0:T(8,128)(2,1)S(1)}, u32[]{:S(2)}, u32[]{:S(2)}) %all-to-all-start.2) | async-done | bytes 1376288 | tf_op jit(solution)/shard_map/all_to_all | solution.py:778
  197.1 11.8 %shard_map.519 = (bf16[2,896,768]{2,1,0:T(8,128)(2,1)}, bf16[2,896,768]{2,1,0:T(8,128)(2,1)}, bf16[896,768]{1,0:T(8,128)(2,1)}, f32[8,768]{1,0:T(8,128)}) custom-call(s32[1]{0:T(128)} %bitcast.27.expert_ref, bf16[16,56,768]{2,1,0:T(8,128)(2,1)} %copy-done.5, bf16[16,2,56,768]{3,2,1,0:T(8,128)(2,1)} %all-to-all-done.up_ref, bf16[768,3200]{1,0:T(8,128)(2,1)} %bitcast.77, ...), custom_call_target="tpu_custom_call" | custom-call | flops 13200000000 | tf_op jit(solution)/shard_map/pallas_call | solution.py:877
  208.9 11.8 %shard_map.518 = (bf16[2,896,768]{2,1,0:T(8,128)(2,1)}, bf16[2,896,768]{2,1,0:T(8,128)(2,1)}, bf16[896,768]{1,0:T(8,128)(2,1)}, f32[8,768]{1,0:T(8,128)}) custom-call(s32[1]{0:T(128)} %bitcast.27.expert_ref, bf16[16,56,768]{2,1,0:T(8,128)(2,1)} %all-to-all-done.1.rows_ref, bf16[16,2,56,768]{3,2,1,0:T(8,128)(2,1)} %all-to-all-done.up_ref, ...), custom_call_target="tpu_custom_call" | custom-call | flops 13200000000 | tf_op jit(solution)/shard_map/pallas_call | solution.py:877
  232.5 12.1 %all-gather.6.cloned.1.call-done = bf16[768,768]{1,0:T(8,128)(2,1)} async-done(((bf16[384,768]{1,0:T(8,128)(2,1)}), bf16[768,768]{1,0:T(8,128)(2,1)}) %all-gather.6.cloned.1.call-update) | async-done | bytes 1179664 | tf_op jit(solution)/shard_map/all_gather | solution.py:896
  247.4 12.9 %shard_map.522 = (bf16[16,2,56,768]{3,2,1,0:T(8,128)(2,1)}, bf16[2,896,768]{2,1,0:T(8,128)(2,1)}, f32[8,1536]{1,0:T(8,128)}) custom-call(bf16[2,384,768]{2,1,0:T(8,128)(2,1)} %shard_map.520.refs_0_, bf16[2,384,768]{2,1,0:T(8,128)(2,1)} %shard_map.521.refs_1_, bf16[2,896,768]{2,1,0:T(8,128)(2,1)} %get-tuple-element.134.refs_0_.refs_2_, ...), custom_call_target="tpu_custom_call" | custom-call | flops 13200000000 | tf_op jit(solution)/shard_map/pallas_call | solution.py:905
  265.4 12.8 %shard_map.523 = (bf16[16,2,56,768]{3,2,1,0:T(8,128)(2,1)}, bf16[2,896,768]{2,1,0:T(8,128)(2,1)}, f32[8,1536]{1,0:T(8,128)}) custom-call(bf16[2,896,768]{2,1,0:T(8,128)(2,1)} %get-tuple-element.135.refs_1_.refs_0_, bf16[2,896,768]{2,1,0:T(8,128)(2,1)} %get-tuple-element.143.refs_1_, bf16[896,768]{1,0:T(8,128)(2,1)} %get-tuple-element.138.refs_3_.refs_2_, ...), custom_call_target="tpu_custom_call" | custom-call | flops 13200000000 | tf_op jit(solution)/shard_map/pallas_call | solution.py:905
  278.2 31.2 %all-to-all-done.3 = bf16[16,2,56,768]{3,2,1,0:T(8,128)(2,1)S(1)} async-done(((bf16[16,2,56,768]{3,2,1,0:T(8,128)(2,1)}), bf16[16,2,56,768]{3,2,1,0:T(8,128)(2,1)S(1)}, u32[]{:S(2)}, u32[]{:S(2)}) %all-to-all-start.3) | async-done | bytes 2752544 | tf_op jit(solution)/shard_map/all_to_all | solution.py:778
  322.0 6.8 %shard_map.525.refs_1_ = bf16[2,768,384]{2,1,0:T(8,128)(2,1)} custom-call(bf16[896,768]{1,0:T(8,128)(2,1)} %bitcast.24.refs_0_, bf16[896,768]{1,0:T(8,128)(2,1)} %bitcast.95, bf16[2,896,768]{2,1,0:T(8,128)(2,1)} %get-tuple-element.142.refs_2_, bf16[2,896,768]{2,1,0:T(8,128)(2,1)} %get-tuple-element.144.refs_3_), custom_call_target="tpu_custom_call" | custom-call | flops 5500000256 | tf_op jit(solution)/shard_map/pallas_call | solution.py:716
  328.8 11.7 %shard_map.526 = (bf16[2,1,196,768]{3,2,1,0:T(8,128)(2,1)}, f32[2,1,196,768]{3,2,1,0:T(8,128)}, bf16[196,768]{1,0:T(8,128)(2,1)}, bf16[196,2304]{1,0:T(8,128)(2,...) custom-call(bf16[2,768,384]{2,1,0:T(8,128)(2,1)} %shard_map.524.refs_0_, ...), custom_call_target="tpu_custom_call" | custom-call | flops 16499999744 | tf_op jit(solution)/shard_map/pallas_call | solution.py:970
  340.6 6.8 %shard_map.527 = (f32[1,768,768]{2,1,0:T(8,128)}, f32[1,768,768]{2,1,0:T(8,128)}, f32[1,768,768]{2,1,0:T(8,128)}, bf16[1,768,768]{2,1,0:T(8,128)(2,1)}, f32[1,2,384,384]{3,2,1,0:T(8,128)}, /*index=5*/f32[384,384]{1,0:T(8,128)}) custom-call(bf16[196,128]{1,0:T(8,128)(2,1)} %get-tuple-element.150.refs_0_.refs_4_, bf16[384,768]{1,0:T(8,128)(2,1)} %bitcast.108, ...), custom_call_target="tpu_custom_call" | custom-call | flops 8800000000 | tf_op jit(solution)/shard_map/pallas_call | solution.py:691
  347.4 20.2 %all-to-all-done.4 = bf16[16,2,56,768]{3,2,1,0:T(8,128)(2,1)} async-done(((bf16[16,2,56,768]{3,2,1,0:T(8,128)(2,1)}), bf16[16,2,56,768]{3,2,1,0:T(8,128)(2,1)}, u32[]{:S(2)}, u32[]{:S(2)}) %all-to-all-start.4) | async-done | bytes 2752544 | tf_op jit(solution)/shard_map/all_to_all | solution.py:778
  367.6 12.0 %shard_map.528 = (bf16[2,1,196,768]{3,2,1,0:T(8,128)(2,1)}, f32[2,1,196,768]{3,2,1,0:T(8,128)}, bf16[196,768]{1,0:T(8,128)(2,1)}, bf16[196,2304]{1,0:T(8,128)(2,...) custom-call(f32[384,384]{1,0:T(8,128)} %get-tuple-element.151.refs_0, ...), custom_call_target="tpu_custom_call", output_to_operand_aliasing={{0}: (10, {}), {1}: (11, {})} | custom-call | flops 16499999744 | tf_op jit(solution)/shard_map/pallas_call | solution.py:970
  379.6 8.1 %shard_map.529 = (f32[4,96,3200]{2,1,0:T(8,128)}, bf16[4,96,3200]{2,1,0:T(8,128)(2,1)}, f32[8,128]{1,0:T(8,128)}) custom-call(bf16[1,768]{1,0:T(2,128)(2,1)} %copy-done.14, s32[1]{0:T(128)} %bitcast.35.core_ref, bf16[2,196,768]{2,1,0:T(8,128)(2,1)} %get-tuple-element.147.refs_7_.refs_6_.mixed_ref, bf16[196,768]{1,0:T(8,128)(2,1)} %get-tuple-element.157.refs_0_, ...), custom_call_target="tpu_custom_call" | custom-call | flops 8800000000 | tf_op jit(solution)/shard_map/pallas_call | solution.py:1026
  394.4 7.3 %shard_map.531 = (f32[1,768,768]{2,1,0:T(8,128)}, f32[1,768,768]{2,1,0:T(8,128)}, f32[1,768,768]{2,1,0:T(8,128)}, bf16[1,768,768]{2,1,0:T(8,128)(2,1)}, f32[1,2,384,384]{3,2,1,0:T(8,128)}, /*index=5*/f32[384,384]{1,0:T(8,128)}) custom-call(f32[8,128]{1,0:T(8,128)} %get-tuple-element.181.refs_0_,, ...), custom_call_target="tpu_custom_call", output_to_operand_aliasing={{0}: (7, {}), {1}: (8, {}), {2}: (9, {}), {3}: (10, {}), {4... | custom-call | flops 8800000000 | tf_op jit(solution)/shard_map/pallas_call | solution.py:691
  404.3 31.5 %shard_map.532.refs_0_ = f32[1,2,384,384]{3,2,1,0:T(8,128)} custom-call(f32[4,96,3200]{2,1,0:T(8,128)} %convert_add_fusion.refs_0_, f32[384,384]{1,0:T(8,128)} %get-tuple-element.151.refs_0_.refs_1_, f32[384,384]{1,0:T(8,128)} %get-tuple-element.187.refs_2_), custom_call_target="tpu_custom_call" | custom-call | flops 32999999488 | tf_op jit(solution)/shard_map/pallas_call | solution.py:166
  437.9 7.7 %collective-permute-done.14 = bf16[1,2,24,3200]{3,2,1,0:T(8,128)(2,1)S(1)} collective-permute-done((bf16[1,2,24,3200]{3,2,1,0:T(8,128)(2,1)S(1)}, bf16[1,2,24,3200]{3,2,1,0:T(8,128)(2,1)S(1)}, u32[]{:S(2)}, u32[]{:S(2)}) %collective-permute-start.14) | collective-permute-done | bytes 307232 | tf_op jit(solution)/shard_map/ppermute | solution.py:572
  449.1 7.7 %shard_map.533 = (f32[1,768,768]{2,1,0:T(8,128)}, f32[1,768,768]{2,1,0:T(8,128)}, f32[1,768,768]{2,1,0:T(8,128)}, bf16[1,768,768]{2,1,0:T(8,128)(2,1)}, f32[1,2,384,384]{3,2,1,0:T(8,128)}, /*index=5*/f32[384,384]{1,0:T(8,128)}) custom-call(f32[1,2,384,384]{3,2,1,0:T(8,128)} %shard_map.532.refs_0_, f32[1,4,24,3200]{3,2,1,0:T(8,128)} %pad_maximum_fusion.1.refs_1_, ...), custom_call_target="tpu_custom_call" | custom-call | flops 8800000000 | tf_op jit(solution)/shard_map/pallas_call | solution.py:691
  466.6 7.2 %shard_map.534 = (f32[1,768,768]{2,1,0:T(8,128)}, f32[1,768,768]{2,1,0:T(8,128)}, f32[1,768,768]{2,1,0:T(8,128)}, bf16[1,768,768]{2,1,0:T(8,128)(2,1)}, f32[1,2,384,384]{3,2,1,0:T(8,128)}, /*index=5*/f32[384,384]{1,0:T(8,128)}) custom-call(f32[384,384]{1,0:T(8,128)} %get-tuple-element.188.refs_0, ...), custom_call_target="tpu_custom_call", output_to_operand_aliasing={{0}: (8, {}), {1}: (9, {}), {2}: (10, {}), {3}: (11, {}), {... | custom-call | flops 8800000000 | tf_op jit(solution)/shard_map/pallas_call | solution.py:691
  482.3 31.2 %shard_map.535 = f32[1,2,384,384]{3,2,1,0:T(8,128)} custom-call(f32[1,24,3200]{2,1,0:T(8,128)} %constant_dynamic-slice_fusion.2.refs_0_, f32[384,384]{1,0:T(8,128)} %get-tuple-element.188.refs_0_.refs_1_, f32[384,384]{1,0:T(8,128)} %get-tuple-element.203.refs_2_), custom_call_target="tpu_custom_call" | custom-call | flops 32999999488 | tf_op jit(solution)/shard_map/pallas_call | solution.py:166
  (185 shorter events, 140.9 us)
Async XLA Ops:
  8.8 34.7 %collective-permute-start.2 = (bf16[1,960]{1,0:T(2,128)(2,1)S(1)}, bf16[1,960]{1,0:T(2,128)(2,1)S(1)}, u32[]{:S(2)}, u32[]{:S(2)}) collective-permute-start(bf16[1,960]{1,0:T(2,128)(2,1)S(1)} %pad_maximum_fusion.4), channel_id=1, source_target_pairs={{0,2},{1,3},{2,0},{3,1},{4,6},{5,7},{6,4},{7,5},{8,10},{9,11},{10,... | collective-permute-start | bytes 5768 | tf_op jit(solution)/shard_map/ppermute | solution.py:577
  27.5 15.9 %collective-permute-start.1 = (bf16[2,24,3200]{2,1,0:T(8,128)(2,1)S(1)}, bf16[2,24,3200]{2,1,0:T(8,128)(2,1)S(1)}, u32[]{:S(2)}, u32[]{:S(2)}) collective-permute-start(bf16[2,24,3200]{2,1,0:T(8,128)(2,1)S(1)} %maximum_select_fusion.10), channel_id=1, source_target_pairs={{0,2},{1,3},{2,0},{3,1},{4,6},{5,7},{6,4},{7,5},{8,10},{9,11},{10,... | collective-permute-start | bytes 921608 | tf_op jit(solution)/shard_map/ppermute | solution.py:572
  43.5 19.8 %collective-permute-start.4 = (bf16[1,4,24,3200]{3,2,1,0:T(8,128)(2,1)S(1)}, bf16[1,4,24,3200]{3,2,1,0:T(8,128)(2,1)S(1)}, u32[]{:S(2)}, u32[]{:S(2)}) collective-permute-start(bf16[1,4,24,3200]{3,2,1,0:T(8,128)(2,1)S(1)} %bitcast.87), channel_id=1, source_target_pairs={{0,16},{4,20},{8,24},{12,28},{16,0},{20,4},{24,8},{28,12},{1,17},{... | collective-permute-start | bytes 1843208 | tf_op jit(solution)/shard_map/ppermute | solution.py:572
  45.1 18.8 %collective-permute-start.3 = (bf16[1,4,24,3200]{3,2,1,0:T(8,128)(2,1)S(1)}, bf16[1,4,24,3200]{3,2,1,0:T(8,128)(2,1)S(1)}, u32[]{:S(2)}, u32[]{:S(2)}) collective-permute-start(bf16[1,4,24,3200]{3,2,1,0:T(8,128)(2,1)S(1)} %bitcast.88), channel_id=1, source_target_pairs={{0,8},{4,12},{8,0},{12,4},{16,24},{20,28},{24,16},{28,20},{1,9},{5... | collective-permute-start | bytes 1843208 | tf_op jit(solution)/shard_map/ppermute | solution.py:572
  50.1 79.7 %all-to-all-start = ((bf16[16,2,56,768]{3,2,1,0:T(8,128)(2,1)}), bf16[16,2,56,768]{3,2,1,0:T(8,128)(2,1)}, u32[]{:S(2)}, u32[]{:S(2)}) async-start(bf16[16,2,56,768]{3,2,1,0:T(8,128)(2,1)} %bitcast.85), calls=%async_computation | async-start | bytes 5505024 | tf_op jit(solution)/shard_map/all_to_all | solution.py:778
  56.6 47.6 %collective-permute-start.8 = (bf16[1,4,24,3200]{3,2,1,0:T(8,128)(2,1)S(1)}, bf16[1,4,24,3200]{3,2,1,0:T(8,128)(2,1)S(1)}, u32[]{:S(2)}, u32[]{:S(2)}) collective-permute-start(bf16[1,4,24,3200]{3,2,1,0:T(8,128)(2,1)S(1)} %bitcast.89), channel_id=1, source_target_pairs={{0,4},{4,0},{8,12},{12,8},{16,20},{20,16},{24,28},{28,24},{1,5},{5... | collective-permute-start | bytes 1843208 | tf_op jit(solution)/shard_map/ppermute | solution.py:572
  56.8 44.1 %collective-permute-start.7 = (bf16[384,768]{1,0:T(8,128)(2,1)}, bf16[384,768]{1,0:T(8,128)(2,1)S(1)}, u32[]{:S(2)}, u32[]{:S(2)}) collective-permute-start(bf16[384,768]{1,0:T(8,128)(2,1)} %get-tuple-element.122), channel_id=1, source_target_pairs={{0,2},{1,3},{2,0},{3,1},{4,6},{5,7},{6,4},{7,5},{8,10},{9,11},{10,... | collective-permute-start | bytes 1769480 | tf_op jit(solution)/shard_map/ppermute | solution.py:577
  63.3 34.4 %collective-permute-start.5 = (bf16[1,2,24,3200]{3,2,1,0:T(8,128)(2,1)S(1)}, bf16[1,2,24,3200]{3,2,1,0:T(8,128)(2,1)S(1)}, u32[]{:S(2)}, u32[]{:S(2)}) collective-permute-start(bf16[1,2,24,3200]{3,2,1,0:T(8,128)(2,1)S(1)} %slice.107), channel_id=1, source_target_pairs={{0,8},{4,12},{8,0},{12,4},{16,24},{20,28},{24,16},{28,20},{1,9},{5... | collective-permute-start | bytes 921608 | tf_op jit(solution)/shard_map/ppermute | solution.py:572
  63.9 33.9 %collective-permute-start.6 = (bf16[1,2,24,3200]{3,2,1,0:T(8,128)(2,1)S(1)}, bf16[1,2,24,3200]{3,2,1,0:T(8,128)(2,1)S(1)}, u32[]{:S(2)}, u32[]{:S(2)}) collective-permute-start(bf16[1,2,24,3200]{3,2,1,0:T(8,128)(2,1)S(1)} %slice.108), channel_id=1, source_target_pairs={{0,16},{4,20},{8,24},{12,28},{16,0},{20,4},{24,8},{28,12},{1,17},{... | collective-permute-start | bytes 921608 | tf_op jit(solution)/shard_map/ppermute | solution.py:572
  65.0 39.2 %collective-permute-start.9 = (bf16[1,4,24,3200]{3,2,1,0:T(8,128)(2,1)S(1)}, bf16[1,4,24,3200]{3,2,1,0:T(8,128)(2,1)S(1)}, u32[]{:S(2)}, u32[]{:S(2)}) collective-permute-start(bf16[1,4,24,3200]{3,2,1,0:T(8,128)(2,1)S(1)} %collective-permute-done.3), channel_id=1, source_target_pairs={{0,4},{4,0},{8,12},{12,8},{16,20},{20,16},{24,28},{28,24},{1,5},{5... | collective-permute-start | bytes 1843208 | tf_op jit(solution)/shard_map/ppermute | solution.py:572
  100.9 28.9 %collective-permute-start.12 = (bf16[384,768]{1,0:T(8,128)(2,1)S(1)}, bf16[384,768]{1,0:T(8,128)(2,1)}, u32[]{:S(2)}, u32[]{:S(2)}) collective-permute-start(bf16[384,768]{1,0:T(8,128)(2,1)S(1)} %copy-done.10), channel_id=1, source_target_pairs={{0,2},{1,3},{2,0},{3,1},{4,6},{5,7},{6,4},{7,5},{8,10},{9,11},{10,... | collective-permute-start | bytes 1769480 | tf_op jit(solution)/shard_map/ppermute | solution.py:577
  129.8 43.3 %all-to-all-start.1 = ((bf16[16,56,768]{2,1,0:T(8,128)(2,1)}), bf16[16,56,768]{2,1,0:T(8,128)(2,1)}, u32[]{:S(2)}, u32[]{:S(2)}) async-start(bf16[16,56,768]{2,1,0:T(8,128)(2,1)} %bitcast.97), calls=%async_computation.1 | async-start | bytes 2752512 | tf_op jit(solution)/shard_map/all_to_all | solution.py:778
  134.4 38.8 %all-gather.4.cloned.1.call-start = ((), (), s32[]{:S(2)}) async-start(), calls=%async_computation.9 | async-start | bytes 1769472 | tf_op jit(solution)/shard_map/all_gather | solution.py:806
  173.2 22.8 %all-to-all-start.2 = ((bf16[16,56,768]{2,1,0:T(8,128)(2,1)}), bf16[16,56,768]{2,1,0:T(8,128)(2,1)S(1)}, u32[]{:S(2)}, u32[]{:S(2)}) async-start(bf16[16,56,768]{2,1,0:T(8,128)(2,1)} %bitcast.96), calls=%async_computation.2 | async-start | bytes 2752512 | tf_op jit(solution)/shard_map/all_to_all | solution.py:778
  177.1 67.5 %all-gather.6.cloned.1.call-start = ((), (), s32[]{:S(2)}) async-start(), calls=%async_computation.14 | async-start | bytes 1769472 | tf_op jit(solution)/shard_map/all_gather | solution.py:896
  260.3 49.0 %all-to-all-start.3 = ((bf16[16,2,56,768]{3,2,1,0:T(8,128)(2,1)}), bf16[16,2,56,768]{3,2,1,0:T(8,128)(2,1)S(1)}, u32[]{:S(2)}, u32[]{:S(2)}) async-start(bf16[16,2,56,768]{3,2,1,0:T(8,128)(2,1)} %get-tuple-element.145), calls=%async_computation.3 | async-start | bytes 5505024 | tf_op jit(solution)/shard_map/all_to_all | solution.py:778
  264.1 76.5 %reduce-scatter.5.cloned.1.call-start = ((), (), s32[]{:S(2)}) async-start(), calls=%async_computation.10 | async-start | bytes 1769472 | tf_op jit(solution)/shard_map/reduce_scatter | solution.py:933
  264.8 129.6 %reduce-scatter.7.cloned.1.call-start = ((), (), s32[]{:S(2)}) async-start(), calls=%async_computation.11 | async-start | bytes 1769472 | tf_op jit(solution)/shard_map/reduce_scatter | solution.py:933
  310.9 56.7 %all-to-all-start.4 = ((bf16[16,2,56,768]{3,2,1,0:T(8,128)(2,1)}), bf16[16,2,56,768]{3,2,1,0:T(8,128)(2,1)}, u32[]{:S(2)}, u32[]{:S(2)}) async-start(bf16[16,2,56,768]{3,2,1,0:T(8,128)(2,1)} %get-tuple-element.152), calls=%async_computation.5 | async-start | bytes 5505024 | tf_op jit(solution)/shard_map/all_to_all | solution.py:778
  315.4 133.7 %reduce-scatter.9.cloned.1.call-start = ((), (), s32[]{:S(2)}) async-start(), calls=%async_computation.12 | async-start | bytes 1769472 | tf_op jit(solution)/shard_map/reduce_scatter | solution.py:933
  322.0 144.6 %reduce-scatter.11.cloned.1.call-start = ((), (), s32[]{:S(2)}) async-start(), calls=%async_computation.13 | async-start | bytes 1769472 | tf_op jit(solution)/shard_map/reduce_scatter | solution.py:933
  389.5 124.0 %collective-permute-start.20 = (f32[1,960]{1,0:T(1,128)S(1)}, f32[1,960]{1,0:T(1,128)S(1)}, u32[]{:S(2)}, u32[]{:S(2)}) collective-permute-start(f32[1,960]{1,0:T(1,128)S(1)} %pad_maximum_fusion.5), channel_id=1, source_target_pairs={{0,2},{1,3},{2,0},{3,1},{4,6},{5,7},{6,4},{7,5},{8,10},{9,11},{10,... | collective-permute-start | bytes 11528 | tf_op jit(solution)/shard_map/ppermute | solution.py:577
  445.8 15.4 %collective-permute-start.15 = (bf16[1,4,24,3200]{3,2,1,0:T(8,128)(2,1)S(1)}, bf16[1,4,24,3200]{3,2,1,0:T(8,128)(2,1)S(1)}, u32[]{:S(2)}, u32[]{:S(2)}) collective-permute-start(bf16[1,4,24,3200]{3,2,1,0:T(8,128)(2,1)S(1)} %fusion.9), channel_id=1, source_target_pairs={{0,8},{4,12},{8,0},{12,4},{16,24},{20,28},{24,16},{28,20},{1,9},{5... | collective-permute-start | bytes 1843208 | tf_op jit(solution)/shard_map/ppermute | solution.py:572
  482.2 32.6 %collective-permute-start.19 = (bf16[1,24,3200]{2,1,0:T(8,128)(2,1)S(1)}, bf16[1,24,3200]{2,1,0:T(8,128)(2,1)S(1)}, u32[]{:S(2)}, u32[]{:S(2)}) collective-permute-start(bf16[1,24,3200]{2,1,0:T(8,128)(2,1)S(1)} %dynamic-slice_convert_fusion.2), channel_id=1, source_target_pairs={{0,1},{1,0},{2,3},{3,2},{4,5},{5,4},{6,7},{7,6},{8,9},{9,8},{10,11... | collective-permute-start | bytes 460808 | tf_op jit(solution)/shard_map/ppermute | solution.py:572
  (33 other events, 587.3 us)
Sparse Core Ops, SparseCore 0:
  137.3 35.7 all-gather.3
  209.0 35.5 all-gather.5
  267.7 34.7 reduce-scatter.4
  305.3 35.4 reduce-scatter.6
  343.5 34.3 reduce-scatter.8
  389.7 35.0 reduce-scatter.10

commit v3 on v1

--- a/solution.py
+++ b/solution.py
@@ -134,9 +134,9 @@
 def renew_kernel(skipped, *refs):
     refs=refs[skipped:]
     m_ref=refs[-1]
-    zs=refs[:-2]
+    zs=refs[:-3]
     nb=len(zs)
-    qs=[refs[-2].at[0,i] for i in range(nb)]
+    qs=[r.at[0,i] for r in refs[-3:-1] for i in range(r.shape[1])]
     n=BLK; kb=n//128; h=SUB
     for b in range(nb):
         z=zs[b][...]
@@ -161,18 +161,19 @@
                 p=mt(m_ref[b,o+128:,sl],inv[b])
                 m_ref[b,o+128:,sl]=p
                 m_ref[b,o+128:,o+128:]=m_ref[b,o+128:,o+128:]-mt(p,p)
-def renew(tokens, stretched):
-    count=len(stretched)
+def renew(tokens, first, second):
+    shapes=[(1, len(group), BLK, BLK) for group in (first, second)]
+    count=len(first)+len(second)
     return vmem_call(
         partial(renew_kernel, len(tokens)),
-        30,
+        40,
         grid=(1,),
-        out_shape=jax.ShapeDtypeStruct((1, count, BLK, BLK), jnp.float32),
+        out_shape=[jax.ShapeDtypeStruct(s, jnp.float32) for s in shapes],
         in_specs=[pl.BlockSpec(memory_space=pl.ANY)] * len(tokens)
         + [full_block((BLK, BLK))] * count,
-        out_specs=full_block((1, count, BLK, BLK)),
+        out_specs=[full_block(s) for s in shapes],
         scratch_shapes=[pltpu.VMEM((count, BLK, BLK), jnp.float32)],
-    )(*tokens, *stretched)
+    )(*tokens, *first, *second)
 
 
 def low(values):
@@ -543,9 +544,9 @@
 def dense_update_kernel(kept_ref, received_ref, *refs):
     inputs, outputs = (refs[:9], refs[9:])
     gradient = kept_ref[...] + wide(received_ref[...])
-    extra = gradient[:, 4 * D :]
-    experts = inputs[3].shape[1]
-    gradients = (gradient[:, : 4 * D], extra[:, :experts], extra.T[experts : experts + 4])
+    extra = gradient[:, 4 * D :].T
+    experts = inputs[3].shape[0]
+    gradients = (gradient[:, : 4 * D], extra[:experts], extra[experts : experts + 4])
     rates = ((RATE_DENSE, DECAY_RATE), (RATE_DENSE, DECAY_RATE), (RATE_NORMS, 0.0))
     place = 0
     for kind in range(3):
@@ -1031,7 +1032,8 @@
     )(b_in_low, core_scalar, mixed, *flat_steps)
     kept, received, stages = scatter_sums(held, sending)
     dense = [shape(attn_weights.shape, f32)] * 3 + [shape(attn_weights.shape, bf16)]
-    routers = [shape(router_weights.shape, f32)] * 3 + [shape(router_weights.shape, bf16)]
+    turned_shape = router_weights.shape[::-1]
+    routers = [shape(turned_shape, f32)] * 3 + [shape(turned_shape, bf16)]
     norms = [shape(norm_params.shape, f32)] * 3
     states = (
         kept,
@@ -1039,9 +1041,9 @@
         attn_weights,
         attn_first,
         attn_second,
-        router_weights,
-        router_first,
-        router_second,
+        router_weights.T,
+        router_first.T,
+        router_second.T,
         norm_params,
         norm_first,
         norm_second,
@@ -1068,7 +1070,6 @@
                 out_turned[-1][:5],
             )
         )
-    w_out_basis_new = renew(stages[:1], [turned[5] for turned in out_turned])
     in_turned = []
     for at in range(blocks):
         in_turned.append(
@@ -1076,14 +1077,16 @@
                 False,
                 RATE_INPUT,
                 at,
-                [w_out_basis_new, stages[1]] if at == 0 else [in_turned[-1][5], stages[2]],
+                [out_turned[-1][5], stages[0]] if at == 0 else [in_turned[-1][5], stages[2]],
                 grads_in[at],
                 (w_in, w_in_first, w_in_second),
                 (w_in_stat, w_in_basis),
                 in_turned[-1][:5] if at > 0 else [],
             )
         )
-    w_in_basis_new = renew(stages[3:], [turned[5] for turned in in_turned])
+    w_out_basis_new, w_in_basis_new = renew(
+        stages[3:], [turned[5] for turned in out_turned], [turned[5] for turned in in_turned]
+    )
     bias_other, w_in_basis_new = lax.optimization_barrier((bias_other, w_in_basis_new))
     w_in_results = (*in_turned[-1][:5], w_in_basis_new)
     w_out_results = (*out_turned[-1][:5], w_out_basis_new)
@@ -1100,7 +1103,9 @@
     )
     return (
         *backward[-1][:2],
-        *updated,
+        *updated[:4],
+        *(value.T for value in updated[4:8]),
+        *updated[8:],
         *w_in_results,
         *w_out_results,
         bin_first_new,

time: 469 us -> 453 us (0.966)
  Pallas kernels: 215 us -> 192 us
  waiting for transfers between devices: 136 us -> 152 us
  local copies, waits for them, and re-layouts: 24.1 us -> 15.1 us
    pallas_call x2 -> x1, Pallas kernels: 62.3 us -> 39.7 us  [renew(): vmem_call(partial(renew_kernel, len(tokens)), 40, grid=(1,), out_shape=[j...]
    reduce_scatter x4, waiting for transfers between devices: 0.02 us -> 15.4 us  [shared(): return lax.psum_scatter(sums, TENSOR, axis_index_groups=pairs)]
    unnamed x62 -> x49, local copies, waits for them, and re-layouts: 20.1 us -> 11 us
  transfers between devices with their start and end apart: 31 -> 31, of which waited for: 13 -> 15; matrix products, arithmetic and copies ran while one was open for 8% -> 8% of each run, Pallas kernels for 46% -> 43%
where the time goes in v3:
time: 453 us; the launch traced here: 444 us
  Pallas kernels  192 us (42%)
  waiting for transfers between devices  152 us (34%)
  starting transfers between devices  45.3 us (10%)
  other arithmetic  25.3 us (6%)
  between operations  15.3 us (3%)
  local copies, waits for them, and re-layouts  15.1 us (3%)
    ppermute x17, waiting for transfers between devices, swap(): return lax.ppermute(values, axis, [(i, i ^ distance) for i in range(size)])  40.4 us
    pallas_call x1, Pallas kernels, renew(): vmem_call(partial(renew_kernel, len(tokens)), 40, grid=(1,), out_shape=[j...  39.7 us
    all_to_all x5, waiting for transfers between devices, exchange(): lax.all_to_all(values, BOTH, 0, 0, axis_index_groups=groups, tiled=True)  38.5 us
    ppermute x4, waiting for transfers between devices, across(): lax.ppermute(values, TENSOR, [(i, (i + size // 2) % size) for i in range(...  29.2 us
    pallas_call x4, Pallas kernels, soap_turn(): vmem_call(partial(turn_kernel, along_rows, rate, len(token)), 8, grid=(1,...  28.2 us
    all_gather x1, waiting for transfers between devices, per_device(): out_pair = lax.all_gather(out_own, TENSOR, axis_index_groups=pairs)  28.1 us
    pallas_call x2, Pallas kernels, per_device(): vmem_call(partial(result_kernel, len(before)), 12, grid=(tiles,), in_spec...  25.5 us
    pallas_call x4, Pallas kernels, row_sums(): vmem_call(row_sums_kernel, 5, grid=(2,), in_specs=[paired if left_paired...  25 us
  transfers between devices with their start and end apart: 31, of which 15 were waited for; matrix products, arithmetic and copies ran while one was open for 8% of the time, Pallas kernels for 43%

profile of v3, /device:TPU:0, one launch (start us, length us, event | category | flops | bytes accessed | tf_op | source)
XLA Modules:
  0.0 444.4 jit_solution(18024612023991876124)
XLA Ops:
  21.3 15.4 %collective-permute-done.1 = bf16[2,24,3200]{2,1,0:T(8,128)(2,1)S(1)} collective-permute-done((bf16[2,24,3200]{2,1,0:T(8,128)(2,1)S(1)}, bf16[2,24,3200]{2,1,0:T(8,128)(2,1)S(1)}, u32[]{:S(2)}, u32[]{:S(2)}) %collective-permute-start.1) | collective-permute-done | bytes 307232 | tf_op jit(solution)/shard_map/ppermute | solution.py:573
  43.0 9.6 %collective-permute-done.3 = bf16[1,4,24,3200]{3,2,1,0:T(8,128)(2,1)S(1)} collective-permute-done((bf16[1,4,24,3200]{3,2,1,0:T(8,128)(2,1)S(1)}, bf16[1,4,24,3200]{3,2,1,0:T(8,128)(2,1)S(1)}, u32[]{:S(2)}, u32[]{:S(2)}) %collective-permute-start.3) | collective-permute-done | bytes 614432 | tf_op jit(solution)/shard_map/ppermute | solution.py:573
  83.3 11.7 %shard_map.517 = (bf16[8,2,56,768]{3,2,1,0:T(8,128)(2,1)}, bf16[8,2,56,768]{3,2,1,0:T(8,128)(2,1)}, bf16[2,196,2304]{2,1,0:T(8,128)(2,1)}, bf16[2,196,768]{2,1,0...) custom-call(bf16[2,1,196,768]{3,2,1,0:T(8,128)(2,1)} %copy.108.x_ref.refs_2_.refs_1_, ...), custom_call_target="tpu_custom_call" | custom-call | flops 12099999744 | tf_op jit(solution)/shard_map/pallas_call | solution.py:833
  94.9 23.7 %collective-permute-done.12 = bf16[384,768]{1,0:T(8,128)(2,1)} collective-permute-done((bf16[384,768]{1,0:T(8,128)(2,1)S(1)}, bf16[384,768]{1,0:T(8,128)(2,1)}, u32[]{:S(2)}, u32[]{:S(2)}) %collective-permute-start.12) | collective-permute-done | bytes 589856 | tf_op jit(solution)/shard_map/ppermute | solution.py:578
  126.8 17.8 %all-to-all-done.1.rows_ref = bf16[16,56,768]{2,1,0:T(8,128)(2,1)} async-done(((bf16[16,56,768]{2,1,0:T(8,128)(2,1)}), bf16[16,56,768]{2,1,0:T(8,128)(2,1)}, u32[]{:S(2)}, u32[]{:S(2)}) %all-to-all-start.1) | async-done | bytes 1376288 | tf_op jit(solution)/shard_map/all_to_all | solution.py:781
  150.9 11.8 %shard_map.518 = (bf16[2,896,768]{2,1,0:T(8,128)(2,1)}, bf16[2,896,768]{2,1,0:T(8,128)(2,1)}, bf16[896,768]{1,0:T(8,128)(2,1)}, f32[8,768]{1,0:T(8,128)}) custom-call(s32[1]{0:T(128)} %bitcast.27.expert_ref, bf16[16,56,768]{2,1,0:T(8,128)(2,1)} %all-to-all-done.1.rows_ref, bf16[16,2,56,768]{3,2,1,0:T(8,128)(2,1)} %all-to-all-done.up_ref, ...), custom_call_target="tpu_custom_call" | custom-call | flops 13200000000 | tf_op jit(solution)/shard_map/pallas_call | solution.py:880
  162.7 28.1 %all-gather.2.cloned.1.call-done.refs_3_.refs_5_ = bf16[2,768,768]{2,1,0:T(8,128)(2,1)} async-done(((bf16[1,768,768]{2,1,0:T(8,128)(2,1)}), bf16[2,768,768]{2,1,0:T(8,128)(2,1)}) %all-gather.2.cloned.1.call-update) | async-done | bytes 2359312 | tf_op jit(solution)/shard_map/all_gather | solution.py:809
  190.8 12.7 %shard_map.519 = (bf16[16,2,56,768]{3,2,1,0:T(8,128)(2,1)}, bf16[2,896,768]{2,1,0:T(8,128)(2,1)}, f32[8,1536]{1,0:T(8,128)}) custom-call(bf16[2,896,768]{2,1,0:T(8,128)(2,1)} %get-tuple-element.135.refs_0_, bf16[2,896,768]{2,1,0:T(8,128)(2,1)} %get-tuple-element.136.refs_1_, bf16[896,768]{1,0:T(8,128)(2,1)} %get-tuple-element.137.refs_2_, ...), custom_call_target="tpu_custom_call" | custom-call | flops 13200000000 | tf_op jit(solution)/shard_map/pallas_call | solution.py:904
  207.4 11.8 %shard_map.520 = (bf16[2,896,768]{2,1,0:T(8,128)(2,1)}, bf16[2,896,768]{2,1,0:T(8,128)(2,1)}, bf16[896,768]{1,0:T(8,128)(2,1)}, f32[8,768]{1,0:T(8,128)}) custom-call(s32[1]{0:T(128)} %bitcast.27.expert_ref, bf16[16,56,768]{2,1,0:T(8,128)(2,1)} %all-to-all-done.2.rows_ref, bf16[16,2,56,768]{3,2,1,0:T(8,128)(2,1)} %all-to-all-done.up_ref, ...), custom_call_target="tpu_custom_call" | custom-call | flops 13200000000 | tf_op jit(solution)/shard_map/pallas_call | solution.py:880
  219.2 5.9 %shard_map.521.refs_0_ = bf16[2,384,768]{2,1,0:T(8,128)(2,1)} custom-call(bf16[2,896,768]{2,1,0:T(8,128)(2,1)} %get-tuple-element.135.refs_0_, bf16[2,896,768]{2,1,0:T(8,128)(2,1)} %get-tuple-element.139.refs_1_.refs_2_, bf16[896,768]{1,0:T(8,128)(2,1)} %get-tuple-element.137.refs_2_, bf16[896,768]{1,0:T(8,128)(2,1)} %get-tuple-element.140.refs_3_.refs_4_), custom_call_target="tpu_custom_call" | custom-call | flops 5500000256 | tf_op jit(solution)/shard_map/pallas_call | solution.py:719
  231.5 12.8 %shard_map.523 = (bf16[16,2,56,768]{3,2,1,0:T(8,128)(2,1)}, bf16[2,896,768]{2,1,0:T(8,128)(2,1)}, f32[8,1536]{1,0:T(8,128)}) custom-call(bf16[2,384,768]{2,1,0:T(8,128)(2,1)} %shard_map.521.refs_0_, bf16[2,384,768]{2,1,0:T(8,128)(2,1)} %shard_map.522.refs_1_, bf16[2,896,768]{2,1,0:T(8,128)(2,1)} %get-tuple-element.139.refs_1_.refs_2_, ...), custom_call_target="tpu_custom_call" | custom-call | flops 13200000000 | tf_op jit(solution)/shard_map/pallas_call | solution.py:904
  244.3 7.5 %all-to-all-done.3 = bf16[16,2,56,768]{3,2,1,0:T(8,128)(2,1)S(1)} async-done(((bf16[16,2,56,768]{3,2,1,0:T(8,128)(2,1)}), bf16[16,2,56,768]{3,2,1,0:T(8,128)(2,1)S(1)}, u32[]{:S(2)}, u32[]{:S(2)}) %all-to-all-start.3) | async-done | bytes 2752544 | tf_op jit(solution)/shard_map/all_to_all | solution.py:781
  257.8 6.5 %shard_map.524.refs_0_ = bf16[2,768,384]{2,1,0:T(8,128)(2,1)} custom-call(bf16[896,768]{1,0:T(8,128)(2,1)} %bitcast.24.refs_0_, bf16[896,768]{1,0:T(8,128)(2,1)} %bitcast.26.refs_1_, bf16[2,896,768]{2,1,0:T(8,128)(2,1)} %get-tuple-element.138.refs_2_, bf16[2,896,768]{2,1,0:T(8,128)(2,1)} %get-tuple-element.142.refs_3_), custom_call_target="tpu_custom_call" | custom-call | flops 5500000256 | tf_op jit(solution)/shard_map/pallas_call | solution.py:719
  264.4 6.7 %shard_map.525.refs_1_ = bf16[2,768,384]{2,1,0:T(8,128)(2,1)} custom-call(bf16[896,768]{1,0:T(8,128)(2,1)} %bitcast.24.refs_0_, bf16[896,768]{1,0:T(8,128)(2,1)} %bitcast.26.refs_1_, bf16[2,896,768]{2,1,0:T(8,128)(2,1)} %get-tuple-element.138.refs_2_, bf16[2,896,768]{2,1,0:T(8,128)(2,1)} %get-tuple-element.142.refs_3_), custom_call_target="tpu_custom_call" | custom-call | flops 5500000256 | tf_op jit(solution)/shard_map/pallas_call | solution.py:719
  271.1 11.7 %shard_map.526 = (bf16[2,1,196,768]{3,2,1,0:T(8,128)(2,1)}, f32[2,1,196,768]{3,2,1,0:T(8,128)}, bf16[196,768]{1,0:T(8,128)(2,1)}, bf16[196,2304]{1,0:T(8,128)(2,...) custom-call(bf16[2,768,384]{2,1,0:T(8,128)(2,1)} %shard_map.524.refs_0_, ...), custom_call_target="tpu_custom_call" | custom-call | flops 16499999744 | tf_op jit(solution)/shard_map/pallas_call | solution.py:969
  282.8 6.9 %shard_map.527 = (f32[1,768,768]{2,1,0:T(8,128)}, f32[1,768,768]{2,1,0:T(8,128)}, f32[1,768,768]{2,1,0:T(8,128)}, bf16[1,768,768]{2,1,0:T(8,128)(2,1)}, f32[1,2,384,384]{3,2,1,0:T(8,128)}, /*index=5*/f32[384,384]{1,0:T(8,128)}) custom-call(bf16[196,128]{1,0:T(8,128)(2,1)} %get-tuple-element.148.refs_0_.refs_4_, bf16[384,768]{1,0:T(8,128)(2,1)} %bitcast.104, ...), custom_call_target="tpu_custom_call" | custom-call | flops 8800000000 | tf_op jit(solution)/shard_map/pallas_call | solution.py:694
  289.6 13.3 %all-to-all-done.4 = bf16[16,2,56,768]{3,2,1,0:T(8,128)(2,1)} async-done(((bf16[16,2,56,768]{3,2,1,0:T(8,128)(2,1)}), bf16[16,2,56,768]{3,2,1,0:T(8,128)(2,1)}, u32[]{:S(2)}, u32[]{:S(2)}) %all-to-all-start.4) | async-done | bytes 2752544 | tf_op jit(solution)/shard_map/all_to_all | solution.py:781
  302.9 12.2 %shard_map.528 = (bf16[2,1,196,768]{3,2,1,0:T(8,128)(2,1)}, f32[2,1,196,768]{3,2,1,0:T(8,128)}, bf16[196,768]{1,0:T(8,128)(2,1)}, bf16[196,2304]{1,0:T(8,128)(2,...) custom-call(f32[384,384]{1,0:T(8,128)} %get-tuple-element.149.refs_0, ...), custom_call_target="tpu_custom_call", output_to_operand_aliasing={{0}: (10, {}), {1}: (11, {})} | custom-call | flops 16499999744 | tf_op jit(solution)/shard_map/pallas_call | solution.py:969
  315.2 8.1 %shard_map.529 = (f32[4,96,3200]{2,1,0:T(8,128)}, bf16[4,96,3200]{2,1,0:T(8,128)(2,1)}, f32[8,128]{1,0:T(8,128)}) custom-call(bf16[1,768]{1,0:T(2,128)(2,1)} %copy-done.9, s32[1]{0:T(128)} %bitcast.33.core_ref, bf16[2,196,768]{2,1,0:T(8,128)(2,1)} %get-tuple-element.145.refs_7_.refs_6_.mixed_ref, bf16[196,768]{1,0:T(8,128)(2,1)} %get-tuple-element.155.refs_0_, ...), custom_call_target="tpu_custom_call" | custom-call | flops 8800000000 | tf_op jit(solution)/shard_map/pallas_call | solution.py:1025
  329.5 6.9 %shard_map.531 = (f32[1,768,768]{2,1,0:T(8,128)}, f32[1,768,768]{2,1,0:T(8,128)}, f32[1,768,768]{2,1,0:T(8,128)}, bf16[1,768,768]{2,1,0:T(8,128)(2,1)}, f32[1,2,384,384]{3,2,1,0:T(8,128)}, /*index=5*/f32[384,384]{1,0:T(8,128)}) custom-call(f32[8,128]{1,0:T(8,128)} %get-tuple-element.179.refs_0_,, ...), custom_call_target="tpu_custom_call", output_to_operand_aliasing={{0}: (7, {}), {1}: (8, {}), {2}: (9, {}), {3}: (10, {}), {4... | custom-call | flops 8800000000 | tf_op jit(solution)/shard_map/pallas_call | solution.py:694
  350.2 7.2 %shard_map.532 = (f32[1,768,768]{2,1,0:T(8,128)}, f32[1,768,768]{2,1,0:T(8,128)}, f32[1,768,768]{2,1,0:T(8,128)}, bf16[1,768,768]{2,1,0:T(8,128)(2,1)}, f32[1,2,384,384]{3,2,1,0:T(8,128)}, /*index=5*/f32[384,384]{1,0:T(8,128)}) custom-call(f32[384,384]{1,0:T(8,128)} %get-tuple-element.185.refs_0_.refs_2_, f32[4,96,3200]{2,1,0:T(8,128)} %copy-done, ...), custom_call_target="tpu_custom_call" | custom-call | flops 8800000000 | tf_op jit(solution)/shard_map/pallas_call | solution.py:694
  367.8 15.4 %reduce-scatter.11.cloned.1.call-done = bf16[1,768,384]{2,1,0:T(8,128)(2,1)} async-done(((bf16[2,768,384]{2,1,0:T(8,128)(2,1)}), bf16[1,768,384]{2,1,0:T(8,128)(2,1)}) %reduce-scatter.11.cloned.1.call-update) | async-done | bytes 589840 | tf_op jit(solution)/shard_map/reduce_scatter | solution.py:932
  383.2 7.2 %shard_map.533 = (f32[1,768,768]{2,1,0:T(8,128)}, f32[1,768,768]{2,1,0:T(8,128)}, f32[1,768,768]{2,1,0:T(8,128)}, bf16[1,768,768]{2,1,0:T(8,128)(2,1)}, f32[1,2,384,384]{3,2,1,0:T(8,128)}, /*index=5*/f32[384,384]{1,0:T(8,128)}) custom-call(f32[384,384]{1,0:T(8,128)} %get-tuple-element.186.refs_0, ...), custom_call_target="tpu_custom_call", output_to_operand_aliasing={{0}: (8, {}), {1}: (9, {}), {2}: (10, {}), {3}: (11, {}), {... | custom-call | flops 8800000000 | tf_op jit(solution)/shard_map/pallas_call | solution.py:694
  393.2 39.7 %shard_map.534 = (f32[1,2,384,384]{3,2,1,0:T(8,128)}, f32[1,2,384,384]{3,2,1,0:T(8,128)}) custom-call(f32[1,24,3200]{2,1,0:T(8,128)} %constant_dynamic-slice_fusion.2.refs_0_, f32[384,384]{1,0:T(8,128)} %get-tuple-element.149.refs_0_.refs_1_, f32[384,384]{1,0:T(8,128)} %get-tuple-element.185.refs_0_.refs_2_, f32[384,384]{1,0:T(8,128)} %get-tuple-element.186.refs_0_.refs_3_, ...), custom_call_target="tpu_custom_call" | custom-call | flops 44000002048 | tf_op jit(solution)/shard_map/pallas_call | solution.py:167
  (173 shorter events, 118.6 us)
Async XLA Ops:
  9.9 10.8 %collective-permute-start = (bf16[1,24,3200]{2,1,0:T(8,128)(2,1)S(1)}, bf16[1,24,3200]{2,1,0:T(8,128)(2,1)S(1)}, u32[]{:S(2)}, u32[]{:S(2)}) collective-permute-start(bf16[1,24,3200]{2,1,0:T(8,128)(2,1)S(1)} %bitcast.89), channel_id=1, source_target_pairs={{0,1},{1,0},{2,3},{3,2},{4,5},{5,4},{6,7},{7,6},{8,9},{9,8},{10,11... | collective-permute-start | bytes 460808 | tf_op jit(solution)/shard_map/ppermute | solution.py:573
  14.3 22.5 %collective-permute-start.2 = (bf16[1,960]{1,0:T(2,128)(2,1)S(1)}, bf16[1,960]{1,0:T(2,128)(2,1)S(1)}, u32[]{:S(2)}, u32[]{:S(2)}) collective-permute-start(bf16[1,960]{1,0:T(2,128)(2,1)S(1)} %pad_maximum_fusion.3), channel_id=1, source_target_pairs={{0,2},{1,3},{2,0},{3,1},{4,6},{5,7},{6,4},{7,5},{8,10},{9,11},{10,... | collective-permute-start | bytes 5768 | tf_op jit(solution)/shard_map/ppermute | solution.py:578
  20.8 15.9 %collective-permute-start.1 = (bf16[2,24,3200]{2,1,0:T(8,128)(2,1)S(1)}, bf16[2,24,3200]{2,1,0:T(8,128)(2,1)S(1)}, u32[]{:S(2)}, u32[]{:S(2)}) collective-permute-start(bf16[2,24,3200]{2,1,0:T(8,128)(2,1)S(1)} %maximum_select_fusion.10), channel_id=1, source_target_pairs={{0,2},{1,3},{2,0},{3,1},{4,6},{5,7},{6,4},{7,5},{8,10},{9,11},{10,... | collective-permute-start | bytes 921608 | tf_op jit(solution)/shard_map/ppermute | solution.py:573
  36.8 15.8 %collective-permute-start.3 = (bf16[1,4,24,3200]{3,2,1,0:T(8,128)(2,1)S(1)}, bf16[1,4,24,3200]{3,2,1,0:T(8,128)(2,1)S(1)}, u32[]{:S(2)}, u32[]{:S(2)}) collective-permute-start(bf16[1,4,24,3200]{3,2,1,0:T(8,128)(2,1)S(1)} %bitcast.84), channel_id=1, source_target_pairs={{0,8},{4,12},{8,0},{12,4},{16,24},{20,28},{24,16},{28,20},{1,9},{5... | collective-permute-start | bytes 1843208 | tf_op jit(solution)/shard_map/ppermute | solution.py:573
  38.4 15.9 %collective-permute-start.4 = (bf16[1,4,24,3200]{3,2,1,0:T(8,128)(2,1)S(1)}, bf16[1,4,24,3200]{3,2,1,0:T(8,128)(2,1)S(1)}, u32[]{:S(2)}, u32[]{:S(2)}) collective-permute-start(bf16[1,4,24,3200]{3,2,1,0:T(8,128)(2,1)S(1)} %bitcast.85), channel_id=1, source_target_pairs={{0,16},{4,20},{8,24},{12,28},{16,0},{20,4},{24,8},{28,12},{1,17},{... | collective-permute-start | bytes 1843208 | tf_op jit(solution)/shard_map/ppermute | solution.py:573
  43.0 24.9 %collective-permute-start.7 = (bf16[384,768]{1,0:T(8,128)(2,1)S(1)}, bf16[384,768]{1,0:T(8,128)(2,1)}, u32[]{:S(2)}, u32[]{:S(2)}) collective-permute-start(bf16[384,768]{1,0:T(8,128)(2,1)S(1)} %copy-done.8), channel_id=1, source_target_pairs={{0,2},{1,3},{2,0},{3,1},{4,6},{5,7},{6,4},{7,5},{8,10},{9,11},{10,... | collective-permute-start | bytes 1769480 | tf_op jit(solution)/shard_map/ppermute | solution.py:578
  67.9 50.7 %all-to-all-start = ((bf16[16,2,56,768]{3,2,1,0:T(8,128)(2,1)}), bf16[16,2,56,768]{3,2,1,0:T(8,128)(2,1)}, u32[]{:S(2)}, u32[]{:S(2)}) async-start(bf16[16,2,56,768]{3,2,1,0:T(8,128)(2,1)} %bitcast.82), calls=%async_computation | async-start | bytes 5505024 | tf_op jit(solution)/shard_map/all_to_all | solution.py:781
  77.0 41.6 %collective-permute-start.12 = (bf16[384,768]{1,0:T(8,128)(2,1)S(1)}, bf16[384,768]{1,0:T(8,128)(2,1)}, u32[]{:S(2)}, u32[]{:S(2)}) collective-permute-start(bf16[384,768]{1,0:T(8,128)(2,1)S(1)} %copy-done.7), channel_id=1, source_target_pairs={{0,2},{1,3},{2,0},{3,1},{4,6},{5,7},{6,4},{7,5},{8,10},{9,11},{10,... | collective-permute-start | bytes 1769480 | tf_op jit(solution)/shard_map/ppermute | solution.py:578
  118.6 25.9 %all-to-all-start.1 = ((bf16[16,56,768]{2,1,0:T(8,128)(2,1)}), bf16[16,56,768]{2,1,0:T(8,128)(2,1)}, u32[]{:S(2)}, u32[]{:S(2)}) async-start(bf16[16,56,768]{2,1,0:T(8,128)(2,1)} %bitcast.95), calls=%async_computation.1 | async-start | bytes 2752512 | tf_op jit(solution)/shard_map/all_to_all | solution.py:781
  123.2 67.6 %all-gather.2.cloned.1.call-start = ((), (), s32[]{:S(2)}) async-start(), calls=%async_computation.9 | async-start | bytes 3538944 | tf_op jit(solution)/shard_map/all_gather | solution.py:809
  144.5 59.0 %all-to-all-start.2 = ((bf16[16,56,768]{2,1,0:T(8,128)(2,1)}), bf16[16,56,768]{2,1,0:T(8,128)(2,1)}, u32[]{:S(2)}, u32[]{:S(2)}) async-start(bf16[16,56,768]{2,1,0:T(8,128)(2,1)} %bitcast.94), calls=%async_computation.2 | async-start | bytes 2752512 | tf_op jit(solution)/shard_map/all_to_all | solution.py:781
  203.6 48.2 %all-to-all-start.3 = ((bf16[16,2,56,768]{3,2,1,0:T(8,128)(2,1)}), bf16[16,2,56,768]{3,2,1,0:T(8,128)(2,1)S(1)}, u32[]{:S(2)}, u32[]{:S(2)}) async-start(bf16[16,2,56,768]{3,2,1,0:T(8,128)(2,1)} %get-tuple-element.143), calls=%async_computation.3 | async-start | bytes 5505024 | tf_op jit(solution)/shard_map/all_to_all | solution.py:781
  207.3 75.4 %reduce-scatter.5.cloned.1.call-start = ((), (), s32[]{:S(2)}) async-start(), calls=%async_computation.10 | async-start | bytes 1769472 | tf_op jit(solution)/shard_map/reduce_scatter | solution.py:932
  225.1 104.4 %reduce-scatter.7.cloned.1.call-start = ((), (), s32[]{:S(2)}) async-start(), calls=%async_computation.11 | async-start | bytes 1769472 | tf_op jit(solution)/shard_map/reduce_scatter | solution.py:932
  253.3 49.7 %all-to-all-start.4 = ((bf16[16,2,56,768]{3,2,1,0:T(8,128)(2,1)}), bf16[16,2,56,768]{3,2,1,0:T(8,128)(2,1)}, u32[]{:S(2)}, u32[]{:S(2)}) async-start(bf16[16,2,56,768]{3,2,1,0:T(8,128)(2,1)} %get-tuple-element.150), calls=%async_computation.5 | async-start | bytes 5505024 | tf_op jit(solution)/shard_map/all_to_all | solution.py:781
  257.7 92.5 %reduce-scatter.9.cloned.1.call-start = ((), (), s32[]{:S(2)}) async-start(), calls=%async_computation.12 | async-start | bytes 1769472 | tf_op jit(solution)/shard_map/reduce_scatter | solution.py:932
  264.3 118.8 %reduce-scatter.11.cloned.1.call-start = ((), (), s32[]{:S(2)}) async-start(), calls=%async_computation.13 | async-start | bytes 1769472 | tf_op jit(solution)/shard_map/reduce_scatter | solution.py:932
  323.2 13.2 %collective-permute-start.13 = (bf16[4,96,3200]{2,1,0:T(8,128)(2,1)}, bf16[4,96,3200]{2,1,0:T(8,128)(2,1)S(1)}, u32[]{:S(2)}, u32[]{:S(2)}) collective-permute-start(bf16[4,96,3200]{2,1,0:T(8,128)(2,1)} %get-tuple-element.167), channel_id=1, source_target_pairs={{0,4},{4,0},{8,12},{12,8},{16,20},{20,16},{24,28},{28,24},{1,5},{5... | collective-permute-start | bytes 7372808 | tf_op jit(solution)/shard_map/ppermute | solution.py:573
  325.1 107.7 %collective-permute-start.20 = (f32[1,960]{1,0:T(1,128)S(1)}, f32[1,960]{1,0:T(1,128)S(1)}, u32[]{:S(2)}, u32[]{:S(2)}) collective-permute-start(f32[1,960]{1,0:T(1,128)S(1)} %pad_maximum_fusion.4), channel_id=1, source_target_pairs={{0,2},{1,3},{2,0},{3,1},{4,6},{5,7},{6,4},{7,5},{8,10},{9,11},{10,... | collective-permute-start | bytes 11528 | tf_op jit(solution)/shard_map/ppermute | solution.py:578
  337.1 9.4 %collective-permute-start.16 = (bf16[1,2,24,3200]{3,2,1,0:T(8,128)(2,1)S(1)}, bf16[1,2,24,3200]{3,2,1,0:T(8,128)(2,1)S(1)}, u32[]{:S(2)}, u32[]{:S(2)}) collective-permute-start(bf16[1,2,24,3200]{3,2,1,0:T(8,128)(2,1)S(1)} %get-tuple-element.315), channel_id=1, source_target_pairs={{0,8},{4,12},{8,0},{12,4},{16,24},{20,28},{24,16},{28,20},{1,9},{5... | collective-permute-start | bytes 921608 | tf_op jit(solution)/shard_map/ppermute | solution.py:573
  346.6 15.2 %collective-permute-start.17 = (bf16[1,4,24,3200]{3,2,1,0:T(8,128)(2,1)S(1)}, bf16[1,4,24,3200]{3,2,1,0:T(8,128)(2,1)S(1)}, u32[]{:S(2)}, u32[]{:S(2)}) collective-permute-start(bf16[1,4,24,3200]{3,2,1,0:T(8,128)(2,1)S(1)} %pad_maximum_fusion.2), channel_id=1, source_target_pairs={{0,16},{4,20},{8,24},{12,28},{16,0},{20,4},{24,8},{28,12},{1,17},{... | collective-permute-start | bytes 1843208 | tf_op jit(solution)/shard_map/ppermute | solution.py:573
  348.7 15.3 %collective-permute-start.15 = (bf16[1,4,24,3200]{3,2,1,0:T(8,128)(2,1)S(1)}, bf16[1,4,24,3200]{3,2,1,0:T(8,128)(2,1)S(1)}, u32[]{:S(2)}, u32[]{:S(2)}) collective-permute-start(bf16[1,4,24,3200]{3,2,1,0:T(8,128)(2,1)S(1)} %pad_maximum_fusion.1), channel_id=1, source_target_pairs={{0,8},{4,12},{8,0},{12,4},{16,24},{20,28},{24,16},{28,20},{1,9},{5... | collective-permute-start | bytes 1843208 | tf_op jit(solution)/shard_map/ppermute | solution.py:573
  365.6 24.8 %collective-permute-start.18 = (bf16[2,24,3200]{2,1,0:T(8,128)(2,1)S(1)}, bf16[2,24,3200]{2,1,0:T(8,128)(2,1)S(1)}, u32[]{:S(2)}, u32[]{:S(2)}) collective-permute-start(bf16[2,24,3200]{2,1,0:T(8,128)(2,1)S(1)} %fusion.4), channel_id=1, source_target_pairs={{0,2},{1,3},{2,0},{3,1},{4,6},{5,7},{6,4},{7,5},{8,10},{9,11},{10,... | collective-permute-start | bytes 921608 | tf_op jit(solution)/shard_map/ppermute | solution.py:573
  393.0 41.1 %collective-permute-start.19 = (bf16[1,24,3200]{2,1,0:T(8,128)(2,1)S(1)}, bf16[1,24,3200]{2,1,0:T(8,128)(2,1)S(1)}, u32[]{:S(2)}, u32[]{:S(2)}) collective-permute-start(bf16[1,24,3200]{2,1,0:T(8,128)(2,1)S(1)} %dynamic-slice_convert_fusion.2), channel_id=1, source_target_pairs={{0,1},{1,0},{2,3},{3,2},{4,5},{5,4},{6,7},{7,6},{8,9},{9,8},{10,11... | collective-permute-start | bytes 460808 | tf_op jit(solution)/shard_map/ppermute | solution.py:573
  (29 other events, 511.1 us)
Sparse Core Ops, SparseCore 0:
  126.2 64.6 all-gather.1
  225.2 35.6 reduce-scatter.4
  263.9 33.2 reduce-scatter.6
  299.8 35.7 reduce-scatter.8
  337.8 45.3 reduce-scatter.10

commit v4 on v3

--- a/solution.py
+++ b/solution.py
@@ -804,11 +804,11 @@
         out_shape=shape((expert_total, half, MB, padded, D), bf16),
     )(target, cotangent)
     first_stage, peer_bias, sent_first = lax.optimization_barrier(
-        (gather_tensor(packed), peer_bias, in_own[: D // 2])
+        (gather_tensor(packed), peer_bias, in_own[: 5 * D // 8])
     )
     out_pair = lax.all_gather(out_own, TENSOR, axis_index_groups=pairs)
     gathered, in_first, in_second, up_sent = gather_experts(
-        first_stage, across(sent_first), in_own[D // 2 :], up_sent
+        first_stage, across(sent_first), in_own[5 * D // 8 :], up_sent
     )
     up_all = exchange(up_sent.reshape(members, MB, padded, D))
     upper = tensor >= half

time: 453 us -> 456 us (level)
    unnamed x49 -> x47, local copies, waits for them, and re-layouts: 11 us -> 11 us
  transfers between devices with their start and end apart: 31 -> 31, of which waited for: 15 -> 16; matrix products, arithmetic and copies ran while one was open for 8% -> 8% of each run, Pallas kernels for 43% -> 42%
where the time goes in v4:
time: 456 us; the launch traced here: 447 us
  Pallas kernels  192 us (42%)
  waiting for transfers between devices  155 us (34%)
  starting transfers between devices  45.3 us (10%)
  other arithmetic  25.4 us (6%)
  between operations  15.3 us (3%)
  local copies, waits for them, and re-layouts  14.9 us (3%)
    ppermute x17, waiting for transfers between devices, swap(): return lax.ppermute(values, axis, [(i, i ^ distance) for i in range(size)])  40.3 us
    all_to_all x5, waiting for transfers between devices, exchange(): lax.all_to_all(values, BOTH, 0, 0, axis_index_groups=groups, tiled=True)  40.2 us
    pallas_call x1, Pallas kernels, renew(): vmem_call(partial(renew_kernel, len(tokens)), 40, grid=(1,), out_shape=[j...  39.7 us
    ppermute x4, waiting for transfers between devices, across(): lax.ppermute(values, TENSOR, [(i, (i + size // 2) % size) for i in range(...  32.2 us
    pallas_call x4, Pallas kernels, soap_turn(): vmem_call(partial(turn_kernel, along_rows, rate, len(token)), 8, grid=(1,...  28.2 us
    all_gather x1, waiting for transfers between devices, per_device(): out_pair = lax.all_gather(out_own, TENSOR, axis_index_groups=pairs)  26.5 us
    pallas_call x2, Pallas kernels, per_device(): vmem_call(partial(result_kernel, len(before)), 12, grid=(tiles,), in_spec...  25.5 us
    pallas_call x4, Pallas kernels, row_sums(): vmem_call(row_sums_kernel, 5, grid=(2,), in_specs=[paired if left_paired...  25 us
  transfers between devices with their start and end apart: 31, of which 16 were waited for; matrix products, arithmetic and copies ran while one was open for 8% of the time, Pallas kernels for 42%

profile of v4, /device:TPU:0, one launch (start us, length us, event | category | flops | bytes accessed | tf_op | source)
XLA Modules:
  0.0 447.4 jit_solution(689241499559104291)
XLA Ops:
  21.1 15.4 %collective-permute-done.1 = bf16[2,24,3200]{2,1,0:T(8,128)(2,1)S(1)} collective-permute-done((bf16[2,24,3200]{2,1,0:T(8,128)(2,1)S(1)}, bf16[2,24,3200]{2,1,0:T(8,128)(2,1)S(1)}, u32[]{:S(2)}, u32[]{:S(2)}) %collective-permute-start.1) | collective-permute-done | bytes 307232 | tf_op jit(solution)/shard_map/ppermute | solution.py:573
  42.8 9.6 %collective-permute-done.3 = bf16[1,4,24,3200]{3,2,1,0:T(8,128)(2,1)S(1)} collective-permute-done((bf16[1,4,24,3200]{3,2,1,0:T(8,128)(2,1)S(1)}, bf16[1,4,24,3200]{3,2,1,0:T(8,128)(2,1)S(1)}, u32[]{:S(2)}, u32[]{:S(2)}) %collective-permute-start.3) | collective-permute-done | bytes 614432 | tf_op jit(solution)/shard_map/ppermute | solution.py:573
  62.3 11.8 %collective-permute-done.7 = bf16[480,768]{1,0:T(8,128)(2,1)} collective-permute-done((bf16[480,768]{1,0:T(8,128)(2,1)S(1)}, bf16[480,768]{1,0:T(8,128)(2,1)}, u32[]{:S(2)}, u32[]{:S(2)}) %collective-permute-start.7) | collective-permute-done | bytes 737312 | tf_op jit(solution)/shard_map/ppermute | solution.py:578
  89.5 11.7 %shard_map.517 = (bf16[8,2,56,768]{3,2,1,0:T(8,128)(2,1)}, bf16[8,2,56,768]{3,2,1,0:T(8,128)(2,1)}, bf16[2,196,2304]{2,1,0:T(8,128)(2,1)}, bf16[2,196,768]{2,1,0...) custom-call(bf16[2,1,196,768]{3,2,1,0:T(8,128)(2,1)} %copy.108.x_ref.refs_2_.refs_1_, ...), custom_call_target="tpu_custom_call" | custom-call | flops 12099999744 | tf_op jit(solution)/shard_map/pallas_call | solution.py:833
  101.1 20.5 %collective-permute-done.12 = bf16[288,768]{1,0:T(8,128)(2,1)} collective-permute-done((bf16[288,768]{1,0:T(8,128)(2,1)S(1)}, bf16[288,768]{1,0:T(8,128)(2,1)}, u32[]{:S(2)}, u32[]{:S(2)}) %collective-permute-start.12) | collective-permute-done | bytes 442400 | tf_op jit(solution)/shard_map/ppermute | solution.py:578
  130.7 18.4 %all-to-all-done.1.rows_ref = bf16[16,56,768]{2,1,0:T(8,128)(2,1)} async-done(((bf16[16,56,768]{2,1,0:T(8,128)(2,1)}), bf16[16,56,768]{2,1,0:T(8,128)(2,1)}, u32[]{:S(2)}, u32[]{:S(2)}) %all-to-all-start.1) | async-done | bytes 1376288 | tf_op jit(solution)/shard_map/all_to_all | solution.py:781
  155.5 11.8 %shard_map.518 = (bf16[2,896,768]{2,1,0:T(8,128)(2,1)}, bf16[2,896,768]{2,1,0:T(8,128)(2,1)}, bf16[896,768]{1,0:T(8,128)(2,1)}, f32[8,768]{1,0:T(8,128)}) custom-call(s32[1]{0:T(128)} %bitcast.27.expert_ref, bf16[16,56,768]{2,1,0:T(8,128)(2,1)} %all-to-all-done.1.rows_ref, bf16[16,2,56,768]{3,2,1,0:T(8,128)(2,1)} %all-to-all-done.up_ref, ...), custom_call_target="tpu_custom_call" | custom-call | flops 13200000000 | tf_op jit(solution)/shard_map/pallas_call | solution.py:880
  167.3 26.5 %all-gather.2.cloned.1.call-done.refs_3_.refs_5_ = bf16[2,768,768]{2,1,0:T(8,128)(2,1)} async-done(((bf16[1,768,768]{2,1,0:T(8,128)(2,1)}), bf16[2,768,768]{2,1,0:T(8,128)(2,1)}) %all-gather.2.cloned.1.call-update) | async-done | bytes 2359312 | tf_op jit(solution)/shard_map/all_gather | solution.py:809
  193.8 12.7 %shard_map.519 = (bf16[16,2,56,768]{3,2,1,0:T(8,128)(2,1)}, bf16[2,896,768]{2,1,0:T(8,128)(2,1)}, f32[8,1536]{1,0:T(8,128)}) custom-call(bf16[2,896,768]{2,1,0:T(8,128)(2,1)} %get-tuple-element.135.refs_0_, bf16[2,896,768]{2,1,0:T(8,128)(2,1)} %get-tuple-element.136.refs_1_, bf16[896,768]{1,0:T(8,128)(2,1)} %get-tuple-element.137.refs_2_, ...), custom_call_target="tpu_custom_call" | custom-call | flops 13200000000 | tf_op jit(solution)/shard_map/pallas_call | solution.py:904
  210.4 11.8 %shard_map.520 = (bf16[2,896,768]{2,1,0:T(8,128)(2,1)}, bf16[2,896,768]{2,1,0:T(8,128)(2,1)}, bf16[896,768]{1,0:T(8,128)(2,1)}, f32[8,768]{1,0:T(8,128)}) custom-call(s32[1]{0:T(128)} %bitcast.27.expert_ref, bf16[16,56,768]{2,1,0:T(8,128)(2,1)} %all-to-all-done.2.rows_ref, bf16[16,2,56,768]{3,2,1,0:T(8,128)(2,1)} %all-to-all-done.up_ref, ...), custom_call_target="tpu_custom_call" | custom-call | flops 13200000000 | tf_op jit(solution)/shard_map/pallas_call | solution.py:880
  234.4 12.8 %shard_map.523 = (bf16[16,2,56,768]{3,2,1,0:T(8,128)(2,1)}, bf16[2,896,768]{2,1,0:T(8,128)(2,1)}, f32[8,1536]{1,0:T(8,128)}) custom-call(bf16[2,384,768]{2,1,0:T(8,128)(2,1)} %shard_map.521.refs_0_, bf16[2,384,768]{2,1,0:T(8,128)(2,1)} %shard_map.522.refs_1_, bf16[2,896,768]{2,1,0:T(8,128)(2,1)} %get-tuple-element.139.refs_1_.refs_2_, ...), custom_call_target="tpu_custom_call" | custom-call | flops 13200000000 | tf_op jit(solution)/shard_map/pallas_call | solution.py:904
  247.2 7.5 %all-to-all-done.3 = bf16[16,2,56,768]{3,2,1,0:T(8,128)(2,1)S(1)} async-done(((bf16[16,2,56,768]{3,2,1,0:T(8,128)(2,1)}), bf16[16,2,56,768]{3,2,1,0:T(8,128)(2,1)S(1)}, u32[]{:S(2)}, u32[]{:S(2)}) %all-to-all-start.3) | async-done | bytes 2752544 | tf_op jit(solution)/shard_map/all_to_all | solution.py:781
  260.8 6.5 %shard_map.524.refs_0_ = bf16[2,768,384]{2,1,0:T(8,128)(2,1)} custom-call(bf16[896,768]{1,0:T(8,128)(2,1)} %bitcast.24.refs_0_, bf16[896,768]{1,0:T(8,128)(2,1)} %bitcast.26.refs_1_, bf16[2,896,768]{2,1,0:T(8,128)(2,1)} %get-tuple-element.138.refs_2_, bf16[2,896,768]{2,1,0:T(8,128)(2,1)} %get-tuple-element.142.refs_3_), custom_call_target="tpu_custom_call" | custom-call | flops 5500000256 | tf_op jit(solution)/shard_map/pallas_call | solution.py:719
  267.4 6.7 %shard_map.525.refs_1_ = bf16[2,768,384]{2,1,0:T(8,128)(2,1)} custom-call(bf16[896,768]{1,0:T(8,128)(2,1)} %bitcast.24.refs_0_, bf16[896,768]{1,0:T(8,128)(2,1)} %bitcast.26.refs_1_, bf16[2,896,768]{2,1,0:T(8,128)(2,1)} %get-tuple-element.138.refs_2_, bf16[2,896,768]{2,1,0:T(8,128)(2,1)} %get-tuple-element.142.refs_3_), custom_call_target="tpu_custom_call" | custom-call | flops 5500000256 | tf_op jit(solution)/shard_map/pallas_call | solution.py:719
  274.1 11.7 %shard_map.526 = (bf16[2,1,196,768]{3,2,1,0:T(8,128)(2,1)}, f32[2,1,196,768]{3,2,1,0:T(8,128)}, bf16[196,768]{1,0:T(8,128)(2,1)}, bf16[196,2304]{1,0:T(8,128)(2,...) custom-call(bf16[2,768,384]{2,1,0:T(8,128)(2,1)} %shard_map.524.refs_0_, ...), custom_call_target="tpu_custom_call" | custom-call | flops 16499999744 | tf_op jit(solution)/shard_map/pallas_call | solution.py:969
  285.7 6.9 %shard_map.527 = (f32[1,768,768]{2,1,0:T(8,128)}, f32[1,768,768]{2,1,0:T(8,128)}, f32[1,768,768]{2,1,0:T(8,128)}, bf16[1,768,768]{2,1,0:T(8,128)(2,1)}, f32[1,2,384,384]{3,2,1,0:T(8,128)}, /*index=5*/f32[384,384]{1,0:T(8,128)}) custom-call(bf16[196,128]{1,0:T(8,128)(2,1)} %get-tuple-element.148.refs_0_.refs_4_, bf16[384,768]{1,0:T(8,128)(2,1)} %bitcast.104, ...), custom_call_target="tpu_custom_call" | custom-call | flops 8800000000 | tf_op jit(solution)/shard_map/pallas_call | solution.py:694
  292.6 13.3 %all-to-all-done.4 = bf16[16,2,56,768]{3,2,1,0:T(8,128)(2,1)} async-done(((bf16[16,2,56,768]{3,2,1,0:T(8,128)(2,1)}), bf16[16,2,56,768]{3,2,1,0:T(8,128)(2,1)}, u32[]{:S(2)}, u32[]{:S(2)}) %all-to-all-start.4) | async-done | bytes 2752544 | tf_op jit(solution)/shard_map/all_to_all | solution.py:781
  305.9 12.3 %shard_map.528 = (bf16[2,1,196,768]{3,2,1,0:T(8,128)(2,1)}, f32[2,1,196,768]{3,2,1,0:T(8,128)}, bf16[196,768]{1,0:T(8,128)(2,1)}, bf16[196,2304]{1,0:T(8,128)(2,...) custom-call(f32[384,384]{1,0:T(8,128)} %get-tuple-element.149.refs_0, ...), custom_call_target="tpu_custom_call", output_to_operand_aliasing={{0}: (10, {}), {1}: (11, {})} | custom-call | flops 16499999744 | tf_op jit(solution)/shard_map/pallas_call | solution.py:969
  318.2 8.1 %shard_map.529 = (f32[4,96,3200]{2,1,0:T(8,128)}, bf16[4,96,3200]{2,1,0:T(8,128)(2,1)}, f32[8,128]{1,0:T(8,128)}) custom-call(bf16[1,768]{1,0:T(2,128)(2,1)} %copy-done.8, s32[1]{0:T(128)} %bitcast.33.core_ref, bf16[2,196,768]{2,1,0:T(8,128)(2,1)} %get-tuple-element.145.refs_7_.refs_6_.mixed_ref, bf16[196,768]{1,0:T(8,128)(2,1)} %get-tuple-element.155.refs_0_, ...), custom_call_target="tpu_custom_call" | custom-call | flops 8800000000 | tf_op jit(solution)/shard_map/pallas_call | solution.py:1025
  332.5 6.9 %shard_map.531 = (f32[1,768,768]{2,1,0:T(8,128)}, f32[1,768,768]{2,1,0:T(8,128)}, f32[1,768,768]{2,1,0:T(8,128)}, bf16[1,768,768]{2,1,0:T(8,128)(2,1)}, f32[1,2,384,384]{3,2,1,0:T(8,128)}, /*index=5*/f32[384,384]{1,0:T(8,128)}) custom-call(f32[8,128]{1,0:T(8,128)} %get-tuple-element.179.refs_0_,, ...), custom_call_target="tpu_custom_call", output_to_operand_aliasing={{0}: (7, {}), {1}: (8, {}), {2}: (9, {}), {3}: (10, {}), {4... | custom-call | flops 8800000000 | tf_op jit(solution)/shard_map/pallas_call | solution.py:694
  353.2 7.2 %shard_map.532 = (f32[1,768,768]{2,1,0:T(8,128)}, f32[1,768,768]{2,1,0:T(8,128)}, f32[1,768,768]{2,1,0:T(8,128)}, bf16[1,768,768]{2,1,0:T(8,128)(2,1)}, f32[1,2,384,384]{3,2,1,0:T(8,128)}, /*index=5*/f32[384,384]{1,0:T(8,128)}) custom-call(f32[384,384]{1,0:T(8,128)} %get-tuple-element.185.refs_0_.refs_2_, f32[4,96,3200]{2,1,0:T(8,128)} %copy-done, ...), custom_call_target="tpu_custom_call" | custom-call | flops 8800000000 | tf_op jit(solution)/shard_map/pallas_call | solution.py:694
  370.7 15.4 %reduce-scatter.11.cloned.1.call-done = bf16[1,768,384]{2,1,0:T(8,128)(2,1)} async-done(((bf16[2,768,384]{2,1,0:T(8,128)(2,1)}), bf16[1,768,384]{2,1,0:T(8,128)(2,1)}) %reduce-scatter.11.cloned.1.call-update) | async-done | bytes 589840 | tf_op jit(solution)/shard_map/reduce_scatter | solution.py:932
  386.2 7.2 %shard_map.533 = (f32[1,768,768]{2,1,0:T(8,128)}, f32[1,768,768]{2,1,0:T(8,128)}, f32[1,768,768]{2,1,0:T(8,128)}, bf16[1,768,768]{2,1,0:T(8,128)(2,1)}, f32[1,2,384,384]{3,2,1,0:T(8,128)}, /*index=5*/f32[384,384]{1,0:T(8,128)}) custom-call(f32[384,384]{1,0:T(8,128)} %get-tuple-element.186.refs_0, ...), custom_call_target="tpu_custom_call", output_to_operand_aliasing={{0}: (8, {}), {1}: (9, {}), {2}: (10, {}), {3}: (11, {}), {... | custom-call | flops 8800000000 | tf_op jit(solution)/shard_map/pallas_call | solution.py:694
  396.2 39.7 %shard_map.534 = (f32[1,2,384,384]{3,2,1,0:T(8,128)}, f32[1,2,384,384]{3,2,1,0:T(8,128)}) custom-call(f32[1,24,3200]{2,1,0:T(8,128)} %constant_dynamic-slice_fusion.2.refs_0_, f32[384,384]{1,0:T(8,128)} %get-tuple-element.149.refs_0_.refs_1_, f32[384,384]{1,0:T(8,128)} %get-tuple-element.185.refs_0_.refs_2_, f32[384,384]{1,0:T(8,128)} %get-tuple-element.186.refs_0_.refs_3_, ...), custom_call_target="tpu_custom_call" | custom-call | flops 44000002048 | tf_op jit(solution)/shard_map/pallas_call | solution.py:167
  (172 shorter events, 119.9 us)
Async XLA Ops:
  9.9 10.6 %collective-permute-start = (bf16[1,24,3200]{2,1,0:T(8,128)(2,1)S(1)}, bf16[1,24,3200]{2,1,0:T(8,128)(2,1)S(1)}, u32[]{:S(2)}, u32[]{:S(2)}) collective-permute-start(bf16[1,24,3200]{2,1,0:T(8,128)(2,1)S(1)} %bitcast.89), channel_id=1, source_target_pairs={{0,1},{1,0},{2,3},{3,2},{4,5},{5,4},{6,7},{7,6},{8,9},{9,8},{10,11... | collective-permute-start | bytes 460808 | tf_op jit(solution)/shard_map/ppermute | solution.py:573
  14.3 22.3 %collective-permute-start.2 = (bf16[1,960]{1,0:T(2,128)(2,1)S(1)}, bf16[1,960]{1,0:T(2,128)(2,1)S(1)}, u32[]{:S(2)}, u32[]{:S(2)}) collective-permute-start(bf16[1,960]{1,0:T(2,128)(2,1)S(1)} %pad_maximum_fusion.3), channel_id=1, source_target_pairs={{0,2},{1,3},{2,0},{3,1},{4,6},{5,7},{6,4},{7,5},{8,10},{9,11},{10,... | collective-permute-start | bytes 5768 | tf_op jit(solution)/shard_map/ppermute | solution.py:578
  20.6 15.9 %collective-permute-start.1 = (bf16[2,24,3200]{2,1,0:T(8,128)(2,1)S(1)}, bf16[2,24,3200]{2,1,0:T(8,128)(2,1)S(1)}, u32[]{:S(2)}, u32[]{:S(2)}) collective-permute-start(bf16[2,24,3200]{2,1,0:T(8,128)(2,1)S(1)} %maximum_select_fusion.10), channel_id=1, source_target_pairs={{0,2},{1,3},{2,0},{3,1},{4,6},{5,7},{6,4},{7,5},{8,10},{9,11},{10,... | collective-permute-start | bytes 921608 | tf_op jit(solution)/shard_map/ppermute | solution.py:573
  36.6 15.8 %collective-permute-start.3 = (bf16[1,4,24,3200]{3,2,1,0:T(8,128)(2,1)S(1)}, bf16[1,4,24,3200]{3,2,1,0:T(8,128)(2,1)S(1)}, u32[]{:S(2)}, u32[]{:S(2)}) collective-permute-start(bf16[1,4,24,3200]{3,2,1,0:T(8,128)(2,1)S(1)} %bitcast.84), channel_id=1, source_target_pairs={{0,8},{4,12},{8,0},{12,4},{16,24},{20,28},{24,16},{28,20},{1,9},{5... | collective-permute-start | bytes 1843208 | tf_op jit(solution)/shard_map/ppermute | solution.py:573
  38.2 15.9 %collective-permute-start.4 = (bf16[1,4,24,3200]{3,2,1,0:T(8,128)(2,1)S(1)}, bf16[1,4,24,3200]{3,2,1,0:T(8,128)(2,1)S(1)}, u32[]{:S(2)}, u32[]{:S(2)}) collective-permute-start(bf16[1,4,24,3200]{3,2,1,0:T(8,128)(2,1)S(1)} %bitcast.85), channel_id=1, source_target_pairs={{0,16},{4,20},{8,24},{12,28},{16,0},{20,4},{24,8},{28,12},{1,17},{... | collective-permute-start | bytes 1843208 | tf_op jit(solution)/shard_map/ppermute | solution.py:573
  42.8 31.3 %collective-permute-start.7 = (bf16[480,768]{1,0:T(8,128)(2,1)S(1)}, bf16[480,768]{1,0:T(8,128)(2,1)}, u32[]{:S(2)}, u32[]{:S(2)}) collective-permute-start(bf16[480,768]{1,0:T(8,128)(2,1)S(1)} %copy-done.6), channel_id=1, source_target_pairs={{0,2},{1,3},{2,0},{3,1},{4,6},{5,7},{6,4},{7,5},{8,10},{9,11},{10,... | collective-permute-start | bytes 2211848 | tf_op jit(solution)/shard_map/ppermute | solution.py:578
  74.1 48.5 %all-to-all-start = ((bf16[16,2,56,768]{3,2,1,0:T(8,128)(2,1)}), bf16[16,2,56,768]{3,2,1,0:T(8,128)(2,1)}, u32[]{:S(2)}, u32[]{:S(2)}) async-start(bf16[16,2,56,768]{3,2,1,0:T(8,128)(2,1)} %bitcast.82), calls=%async_computation | async-start | bytes 5505024 | tf_op jit(solution)/shard_map/all_to_all | solution.py:781
  83.1 38.5 %collective-permute-start.12 = (bf16[288,768]{1,0:T(8,128)(2,1)S(1)}, bf16[288,768]{1,0:T(8,128)(2,1)}, u32[]{:S(2)}, u32[]{:S(2)}) collective-permute-start(bf16[288,768]{1,0:T(8,128)(2,1)S(1)} %slice_bitcast_fusion.1), channel_id=1, source_target_pairs={{0,2},{1,3},{2,0},{3,1},{4,6},{5,7},{6,4},{7,5},{8,10},{9,11},{10,... | collective-permute-start | bytes 1327112 | tf_op jit(solution)/shard_map/ppermute | solution.py:578
  122.6 26.5 %all-to-all-start.1 = ((bf16[16,56,768]{2,1,0:T(8,128)(2,1)}), bf16[16,56,768]{2,1,0:T(8,128)(2,1)}, u32[]{:S(2)}, u32[]{:S(2)}) async-start(bf16[16,56,768]{2,1,0:T(8,128)(2,1)} %bitcast.95), calls=%async_computation.1 | async-start | bytes 2752512 | tf_op jit(solution)/shard_map/all_to_all | solution.py:781
  127.1 66.7 %all-gather.2.cloned.1.call-start = ((), (), s32[]{:S(2)}) async-start(), calls=%async_computation.9 | async-start | bytes 3538944 | tf_op jit(solution)/shard_map/all_gather | solution.py:809
  149.1 57.4 %all-to-all-start.2 = ((bf16[16,56,768]{2,1,0:T(8,128)(2,1)}), bf16[16,56,768]{2,1,0:T(8,128)(2,1)}, u32[]{:S(2)}, u32[]{:S(2)}) async-start(bf16[16,56,768]{2,1,0:T(8,128)(2,1)} %bitcast.94), calls=%async_computation.2 | async-start | bytes 2752512 | tf_op jit(solution)/shard_map/all_to_all | solution.py:781
  206.5 48.2 %all-to-all-start.3 = ((bf16[16,2,56,768]{3,2,1,0:T(8,128)(2,1)}), bf16[16,2,56,768]{3,2,1,0:T(8,128)(2,1)S(1)}, u32[]{:S(2)}, u32[]{:S(2)}) async-start(bf16[16,2,56,768]{3,2,1,0:T(8,128)(2,1)} %get-tuple-element.143), calls=%async_computation.3 | async-start | bytes 5505024 | tf_op jit(solution)/shard_map/all_to_all | solution.py:781
  210.3 75.4 %reduce-scatter.5.cloned.1.call-start = ((), (), s32[]{:S(2)}) async-start(), calls=%async_computation.10 | async-start | bytes 1769472 | tf_op jit(solution)/shard_map/reduce_scatter | solution.py:932
  228.1 104.4 %reduce-scatter.7.cloned.1.call-start = ((), (), s32[]{:S(2)}) async-start(), calls=%async_computation.11 | async-start | bytes 1769472 | tf_op jit(solution)/shard_map/reduce_scatter | solution.py:932
  256.2 49.7 %all-to-all-start.4 = ((bf16[16,2,56,768]{3,2,1,0:T(8,128)(2,1)}), bf16[16,2,56,768]{3,2,1,0:T(8,128)(2,1)}, u32[]{:S(2)}, u32[]{:S(2)}) async-start(bf16[16,2,56,768]{3,2,1,0:T(8,128)(2,1)} %get-tuple-element.150), calls=%async_computation.5 | async-start | bytes 5505024 | tf_op jit(solution)/shard_map/all_to_all | solution.py:781
  260.7 92.5 %reduce-scatter.9.cloned.1.call-start = ((), (), s32[]{:S(2)}) async-start(), calls=%async_computation.12 | async-start | bytes 1769472 | tf_op jit(solution)/shard_map/reduce_scatter | solution.py:932
  267.3 118.9 %reduce-scatter.11.cloned.1.call-start = ((), (), s32[]{:S(2)}) async-start(), calls=%async_computation.13 | async-start | bytes 1769472 | tf_op jit(solution)/shard_map/reduce_scatter | solution.py:932
  326.2 13.2 %collective-permute-start.13 = (bf16[4,96,3200]{2,1,0:T(8,128)(2,1)}, bf16[4,96,3200]{2,1,0:T(8,128)(2,1)S(1)}, u32[]{:S(2)}, u32[]{:S(2)}) collective-permute-start(bf16[4,96,3200]{2,1,0:T(8,128)(2,1)} %get-tuple-element.167), channel_id=1, source_target_pairs={{0,4},{4,0},{8,12},{12,8},{16,20},{20,16},{24,28},{28,24},{1,5},{5... | collective-permute-start | bytes 7372808 | tf_op jit(solution)/shard_map/ppermute | solution.py:573
  328.1 107.7 %collective-permute-start.20 = (f32[1,960]{1,0:T(1,128)S(1)}, f32[1,960]{1,0:T(1,128)S(1)}, u32[]{:S(2)}, u32[]{:S(2)}) collective-permute-start(f32[1,960]{1,0:T(1,128)S(1)} %pad_maximum_fusion.4), channel_id=1, source_target_pairs={{0,2},{1,3},{2,0},{3,1},{4,6},{5,7},{6,4},{7,5},{8,10},{9,11},{10,... | collective-permute-start | bytes 11528 | tf_op jit(solution)/shard_map/ppermute | solution.py:578
  340.0 9.4 %collective-permute-start.16 = (bf16[1,2,24,3200]{3,2,1,0:T(8,128)(2,1)S(1)}, bf16[1,2,24,3200]{3,2,1,0:T(8,128)(2,1)S(1)}, u32[]{:S(2)}, u32[]{:S(2)}) collective-permute-start(bf16[1,2,24,3200]{3,2,1,0:T(8,128)(2,1)S(1)} %get-tuple-element.313), channel_id=1, source_target_pairs={{0,8},{4,12},{8,0},{12,4},{16,24},{20,28},{24,16},{28,20},{1,9},{5... | collective-permute-start | bytes 921608 | tf_op jit(solution)/shard_map/ppermute | solution.py:573
  349.6 15.2 %collective-permute-start.17 = (bf16[1,4,24,3200]{3,2,1,0:T(8,128)(2,1)S(1)}, bf16[1,4,24,3200]{3,2,1,0:T(8,128)(2,1)S(1)}, u32[]{:S(2)}, u32[]{:S(2)}) collective-permute-start(bf16[1,4,24,3200]{3,2,1,0:T(8,128)(2,1)S(1)} %pad_maximum_fusion.2), channel_id=1, source_target_pairs={{0,16},{4,20},{8,24},{12,28},{16,0},{20,4},{24,8},{28,12},{1,17},{... | collective-permute-start | bytes 1843208 | tf_op jit(solution)/shard_map/ppermute | solution.py:573
  351.7 15.3 %collective-permute-start.15 = (bf16[1,4,24,3200]{3,2,1,0:T(8,128)(2,1)S(1)}, bf16[1,4,24,3200]{3,2,1,0:T(8,128)(2,1)S(1)}, u32[]{:S(2)}, u32[]{:S(2)}) collective-permute-start(bf16[1,4,24,3200]{3,2,1,0:T(8,128)(2,1)S(1)} %pad_maximum_fusion.1), channel_id=1, source_target_pairs={{0,8},{4,12},{8,0},{12,4},{16,24},{20,28},{24,16},{28,20},{1,9},{5... | collective-permute-start | bytes 1843208 | tf_op jit(solution)/shard_map/ppermute | solution.py:573
  368.5 24.9 %collective-permute-start.18 = (bf16[2,24,3200]{2,1,0:T(8,128)(2,1)S(1)}, bf16[2,24,3200]{2,1,0:T(8,128)(2,1)S(1)}, u32[]{:S(2)}, u32[]{:S(2)}) collective-permute-start(bf16[2,24,3200]{2,1,0:T(8,128)(2,1)S(1)} %fusion.4), channel_id=1, source_target_pairs={{0,2},{1,3},{2,0},{3,1},{4,6},{5,7},{6,4},{7,5},{8,10},{9,11},{10,... | collective-permute-start | bytes 921608 | tf_op jit(solution)/shard_map/ppermute | solution.py:573
  396.0 41.1 %collective-permute-start.19 = (bf16[1,24,3200]{2,1,0:T(8,128)(2,1)S(1)}, bf16[1,24,3200]{2,1,0:T(8,128)(2,1)S(1)}, u32[]{:S(2)}, u32[]{:S(2)}) collective-permute-start(bf16[1,24,3200]{2,1,0:T(8,128)(2,1)S(1)} %dynamic-slice_convert_fusion.2), channel_id=1, source_target_pairs={{0,1},{1,0},{2,3},{3,2},{4,5},{5,4},{6,7},{7,6},{8,9},{9,8},{10,11... | collective-permute-start | bytes 460808 | tf_op jit(solution)/shard_map/ppermute | solution.py:573
  (28 other events, 513.6 us)
Sparse Core Ops, SparseCore 0:
  130.1 63.6 all-gather.1
  228.2 35.6 reduce-scatter.4
  266.8 33.2 reduce-scatter.6
  302.8 35.6 reduce-scatter.8
  340.8 45.3 reduce-scatter.10
